TPU v7x, 128 devices: a whole 4x4x4 slice. The times are simulated.
128 devices in a mesh: row: 8 (over z, y_lo), col: 16 (over y_hi, x, core).
Axes of the slice: x: 4, y: 4 (y_hi: 2, y_lo: 2; y = y_hi * 2 + y_lo), z: 4, core: 2. Of those that a mesh axis runs over, the one named last changes fastest.
Arguments:
- hidden: bfloat16 [2048, 26624], P('col', 'row'), may hold values from -6 to 6
- weight: bfloat16 [26624, 8192], P('row', 'col'), may hold values from -0.0546875 to 0.0546875
- grad_out: bfloat16 [2048, 8192], P('row', 'col'), may hold values from -6 to 6
Outputs:
- output: bfloat16 [2048, 8192], P('row', 'col')
- grad_hidden: bfloat16 [2048, 26624], P('col', 'row')
- grad_weight: bfloat16 [26624, 8192], P('row', 'col')
All inputs are finite; a program needn't handle non-finite values.
Results may differ from a plain program's by a relative error of at most 0.019.
Values may be sent and summed in bfloat16 or wider, within the bound.
No kernel may reach another device: no remote copies, remote signals or barrier semaphores. Data moves between devices by JAX's collectives and lax.ppermute only.
A program may use at most 128 MiB of HBM per device.

v0:
```python
import jax
import jax.numpy as jnp
from jax import lax
from jax.sharding import PartitionSpec as P


def per_device(hidden, weight, grad_out):
    cotangents = lax.all_gather(grad_out, "row", axis=0, tiled=True)
    gathered = lax.all_gather(hidden, "col", axis=0, tiled=True)
    partial_out = jnp.dot(gathered, weight, preferred_element_type=jnp.float32)
    grad_weight = lax.dot_general(
        gathered, cotangents, (((0,), (0,)), ((), ())), preferred_element_type=jnp.float32
    )
    output = lax.psum_scatter(
        partial_out.astype(jnp.bfloat16), "row", scatter_dimension=0, tiled=True
    )
    part = lax.dot_general(
        cotangents, weight, (((1,), (1,)), ((), ())), preferred_element_type=jnp.float32
    )
    part = lax.optimization_barrier(part.astype(jnp.bfloat16))
    grad_hidden = lax.psum_scatter(
        part.astype(jnp.float32).astype(jnp.bfloat16), "col", scatter_dimension=0, tiled=True
    )
    return (output, grad_hidden, grad_weight.astype(jnp.bfloat16))


def solution(mesh):
    placed = (P("col", "row"), P("row", "col"), P("row", "col"))
    return jax.shard_map(
        per_device,
        mesh=mesh,
        in_specs=placed,
        out_specs=(P("row", "col"), P("col", "row"), P("row", "col")),
        check_vma=False,
    )
```

profile of v0, /device:TPU:1, one launch (start us, length us, event | category | flops | bytes accessed | tf_op | source)
XLA Modules:
  0.0 352.4 jit_solution(8082366088749023770)
XLA Ops:
  7.2 0.0 copy-start
  7.2 0.0 all-gather.5.cloned.1.call-start
  7.2 0.7 all-gather.5.cloned.1.call-update
  7.9 0.0 all-gather.3.cloned.1.call-start
  8.0 0.7 all-gather.3.cloned.1.call-update
  8.7 0.0 reduce-scatter.5.cloned.1.call-start
  8.7 56.3 %all-gather.5.cloned.1.call-done = bf16[2048,512]{1,0:T(8,128)(2,1)} async-done(((bf16[256,512]{1,0:T(8,128)(2,1)}), bf16[2048,512]{1,0:T(8,128)(2,1)}) %all-gather.5.cloned.1.call-update) | async-done | bytes 2097168 | tf_op jit(solution)/shard_map/all_gather | solution.py:8
  65.0 0.0 copy-done
  65.0 12.5 %convolution_convert_fusion = bf16[2048,3328]{1,0:T(8,128)(2,1)} fusion(bf16[2048,512]{1,0:T(8,128)(2,1)} %all-gather.5.cloned.1.call-done, bf16[3328,512]{1,0:T(8,128)(2,1)S(1)} %copy-done), kind=kOutput, calls=%fused_computation | convolution fusion | flops 6986137600 | bytes 19136512 | tf_op jit(solution)/shard_map/dot_general | solution.py:17
  77.5 0.0 reduce-scatter.5.cloned.1.call-update
  77.5 0.0 reduce-scatter.3.cloned.1.call-start
  77.6 85.4 %all-gather.3.cloned.1.call-done = bf16[2048,3328]{1,0:T(8,128)(2,1)} async-done(((bf16[128,3328]{1,0:T(8,128)(2,1)}), bf16[2048,3328]{1,0:T(8,128)(2,1)}) %all-gather.3.cloned.1.call-update) | async-done | bytes 13631504 | tf_op jit(solution)/shard_map/all_gather | solution.py:9
  162.9 11.3 %convolution_convert_fusion.2 = bf16[2048,512]{1,0:T(8,128)(2,1)} fusion(bf16[2048,3328]{1,0:T(8,128)(2,1)} %all-gather.3.cloned.1.call-done, bf16[3328,512]{1,0:T(8,128)(2,1)S(1)} %copy-done), kind=kOutput, calls=%fused_computation.2 | convolution fusion | flops 6980370432 | bytes 19136512 | tf_op jit(solution)/shard_map/dot_general | solution.py:10
  174.2 0.0 reduce-scatter.3.cloned.1.call-update
  174.2 15.8 %convolution_convert_fusion.1 = bf16[3328,512]{1,0:T(8,128)(2,1)} fusion(bf16[2048,3328]{1,0:T(8,128)(2,1)} %all-gather.3.cloned.1.call-done, bf16[2048,512]{1,0:T(8,128)(2,1)} %all-gather.5.cloned.1.call-done), kind=kOutput, calls=%fused_computation.1 | convolution fusion | flops 6981025792 | bytes 19136512 | tf_op jit(solution)/shard_map/dot_general | solution.py:11
  190.0 101.5 %reduce-scatter.5.cloned.1.call-done = bf16[128,3328]{1,0:T(8,128)(2,1)} async-done(((bf16[2048,3328]{1,0:T(8,128)(2,1)}), bf16[128,3328]{1,0:T(8,128)(2,1)}) %reduce-scatter.5.cloned.1.call-update) | async-done | bytes 851984 | tf_op jit(solution)/shard_map/reduce_scatter | solution.py:21
  291.6 54.3 %reduce-scatter.3.cloned.1.call-done = bf16[256,512]{1,0:T(8,128)(2,1)} async-done(((bf16[2048,512]{1,0:T(8,128)(2,1)}), bf16[256,512]{1,0:T(8,128)(2,1)}) %reduce-scatter.3.cloned.1.call-update) | async-done | bytes 262160 | tf_op jit(solution)/shard_map/reduce_scatter | solution.py:14
Async XLA Ops:
  7.2 57.9 %copy-start = (bf16[3328,512]{1,0:T(8,128)(2,1)S(1)}, bf16[3328,512]{1,0:T(8,128)(2,1)}, u32[]{:S(2)}) copy-start(bf16[3328,512]{1,0:T(8,128)(2,1)} %param.4) | copy-start | bytes 10223620
  7.2 57.8 %all-gather.5.cloned.1.call-start = ((), (), s32[]{:S(2)}) async-start(), calls=%async_computation.4 | async-start | bytes 2359296 | tf_op jit(solution)/shard_map/all_gather | solution.py:8
  7.9 155.0 %all-gather.3.cloned.1.call-start = ((), (), s32[]{:S(2)}) async-start(), calls=%async_computation.2 | async-start | bytes 14483456 | tf_op jit(solution)/shard_map/all_gather | solution.py:9
  8.7 282.9 %reduce-scatter.5.cloned.1.call-start = ((), (), s32[]{:S(2)}) async-start(), calls=%async_computation.5 | async-start | bytes 14483456 | tf_op jit(solution)/shard_map/reduce_scatter | solution.py:21
  77.5 268.3 %reduce-scatter.3.cloned.1.call-start = ((), (), s32[]{:S(2)}) async-start(), calls=%async_computation.3 | async-start | bytes 2359296 | tf_op jit(solution)/shard_map/reduce_scatter | solution.py:14
Sparse Core Ops, SparseCore 0:
  9.7 55.3 all-gather.4
  67.4 95.4 all-gather.2
  167.9 123.5 reduce-scatter.4
  294.4 51.3 reduce-scatter.2
where the time goes:
time: 352 us
  waiting for transfers between devices  299 us (85%)
  matrix products  39.6 us (11%)
  between operations  13.8 us (4%)
    reduce_scatter x1, waiting for transfers between devices, per_device(): lax.psum_scatter(part.astype(jnp.float32).astype(jnp.bfloat16), 'col', sc...  102 us
    all_gather x1, waiting for transfers between devices, per_device(): gathered = lax.all_gather(hidden, 'col', axis=0, tiled=True)  85.4 us
    all_gather x1, waiting for transfers between devices, per_device(): cotangents = lax.all_gather(grad_out, 'row', axis=0, tiled=True)  56.3 us
    reduce_scatter x1, waiting for transfers between devices, per_device(): lax.psum_scatter(partial_out.astype(jnp.bfloat16), 'row', scatter_dimensi...  54.3 us
    dot_general x1, matrix products, per_device(): lax.dot_general(gathered, cotangents, (((0,), (0,)), ((), ())), preferred...  15.8 us
    dot_general x1, matrix products, per_device(): lax.dot_general(cotangents, weight, (((1,), (1,)), ((), ())), preferred_e...  12.5 us
    dot_general x1, matrix products, per_device(): partial_out = jnp.dot(gathered, weight, preferred_element_type=jnp.float32)  11.3 us
  transfers between devices with their start and end apart: 4, of which 4 were waited for; matrix products, arithmetic and copies ran while one was open for 11% of the time, Pallas kernels for 0%

commit v1 on v0

v1 whole, which is shorter than its diff:
```python
import jax
import jax.numpy as jnp
from jax import lax
from jax.sharding import PartitionSpec as P

BF, F32 = jnp.bfloat16, jnp.float32
AXES = ("row", "col")
VIA_Y = 48


def place(row, col):
    z, y_lo = divmod(row, 2)
    y_hi, rest = divmod(col, 8)
    x, core = divmod(rest, 2)
    return x, y_hi, y_lo, z, core


def permutation(move):
    pairs = []
    for row in range(8):
        for col in range(16):
            x, y_hi, y_lo, z, core = move(*place(row, col))
            pairs.append((row * 16 + col, (z % 4 * 2 + y_lo) * 16 + y_hi * 8 + x % 4 * 2 + core))
    return pairs


X1 = permutation(lambda x, yh, yl, z, c: (x + 1 - 2 * c, yh, yl, z, c))
X2 = permutation(lambda x, yh, yl, z, c: (x - 1 + 2 * c, yh, yl, z, c))
Z1 = permutation(lambda x, yh, yl, z, c: (x, yh, yl, z + 1 - 2 * c, c))
Z2 = permutation(lambda x, yh, yl, z, c: (x, yh, yl, z - 1 + 2 * c, c))
YH = permutation(lambda x, yh, yl, z, c: (x, 1 - yh, yl, z, c))
YL = permutation(lambda x, yh, yl, z, c: (x, yh, 1 - yl, z, c))
CORE = permutation(lambda x, yh, yl, z, c: (x, yh, yl, z, 1 - c))


def send(value, perm):
    return lax.ppermute(value, AXES, perm)


def add(*terms):
    total = terms[0].astype(F32)
    for term in terms[1:]:
        total = total + term.astype(F32)
    return total.astype(BF)


def dot(a, b, dims):
    return lax.dot_general(a, b, (dims, ((), ())), preferred_element_type=F32)


def per_device(hidden, weight, grad_out):
    row, col = lax.axis_index("row"), lax.axis_index("col")
    core = col % 2
    x, y_hi = col // 2 % 4, col // 8
    z, y_lo = row // 2, row % 2
    s = 1 - 2 * core
    a = VIA_Y

    mine = lax.dynamic_slice_in_dim(grad_out, core * 128, 128, 0)
    theirs = lax.dynamic_slice_in_dim(grad_out, (1 - core) * 128, 128, 0)
    g = jnp.concatenate([mine, send(theirs, CORE)], axis=1)
    w = jnp.concatenate([weight, send(weight, CORE)], axis=1)
    g = jnp.concatenate([g, send(g, YL)], axis=0)
    g3, g1 = send(g, Z1), send(g, Z2)
    g2 = send(g3, Z1)
    g = jnp.concatenate([g, g1, g2, g3], axis=0).reshape(8, 128, 1024)
    order = []
    for j in range(8):
        r = (y_hi + j // 4) % 2 * 4 + (x + s * (j % 4)) % 4
        order.append(((r // 2 - z) * s) % 4 * 2 + (r + y_lo) % 2)
    g = jnp.concatenate(
        [lax.dynamic_index_in_dim(g, i, 0, keepdims=False) for i in order], axis=0
    )

    h0 = hidden
    h3, h1, k0 = send(h0, X1), send(h0, X2), send(h0, YH)
    h2 = send(h3, X1)
    k3b, k1b = send(k0[a:], X1), send(k0[a:], X2)
    k3a, k1a = send(h3[:a], YH), send(h1[:a], YH)
    k2b = send(k3b, X1)
    k2a = send(h2[:a], YH)
    h_near = jnp.concatenate([h0, h1, h2, h3], axis=0)
    h_far = jnp.concatenate([k0, k1a, k1b, k2a, k2b, k3a, k3b], axis=0)

    far = dot(g[512:], w, ((1,), (1,))).astype(BF).reshape(4, 128, 3328)
    near = dot(g[:512], w, ((1,), (1,))).astype(BF).reshape(4, 128, 3328)
    r3 = send(far[2, a:], X1)
    r2 = send(far[3, a:], X2)
    n2 = send(far[2, :a], YH)
    n1, n3 = send(far[1, :a], YH), send(far[3, :a], YH)
    r1 = send(add(far[1, a:], r3), X1)
    d3 = send(jnp.concatenate([add(near[2, :a], n2), near[2, a:]], axis=0), X1)
    d2 = send(jnp.concatenate([add(near[3, :a], n3), near[3, a:]], axis=0), X2)
    n0 = send(jnp.concatenate([far[0, :a], add(far[0, a:], r1, r2)], axis=0), YH)
    d1 = send(
        jnp.concatenate([add(near[1, :a], n1, d3[:a]), add(near[1, a:], d3[a:])], axis=0), X1
    )
    grad_hidden = add(near[0], n0, d1, d2)

    out = jnp.concatenate(
        [dot(h_near, w, ((1,), (0,))).astype(BF), dot(h_far, w, ((1,), (0,))).astype(BF)], axis=0
    ).reshape(8, 128, 1024)

    def rows_for(dz):
        picked = []
        for dy in range(2):
            r = (z + s * dz) % 4 * 2 + (y_lo + dy) % 2
            j = (r // 4 + y_hi) % 2 * 4 + ((r % 4 - x) * s) % 4
            picked.append(lax.dynamic_index_in_dim(out, j, 0, keepdims=False))
        return jnp.concatenate(picked, axis=0)

    o3, o2 = send(rows_for(2), Z1), send(rows_for(3), Z2)
    o1 = send(add(rows_for(1), o3), Z1)
    o = add(rows_for(0), o1, o2)
    o = add(o[:128], send(o[128:], YL))
    own, other = o[:, :512], send(o[:, 512:], CORE)
    output = jnp.where(
        core == 0, jnp.concatenate([own, other], axis=0), jnp.concatenate([other, own], axis=0)
    )

    h = jnp.concatenate([h_near, h_far], axis=0)
    v = send(dot(h, g[:, 512:], ((0,), (0,))).astype(BF), CORE)
    grad_weight = (dot(h, g[:, :512], ((0,), (0,))) + v.astype(F32)).astype(BF)
    return output, grad_hidden, grad_weight


def solution(mesh):
    placed = (P("col", "row"), P("row", "col"), P("row", "col"))
    return jax.shard_map(
        per_device,
        mesh=mesh,
        in_specs=placed,
        out_specs=(P("row", "col"), P("col", "row"), P("row", "col")),
        check_vma=False,
    )
```

time: 352 us -> 197 us (0.56)
  waiting for transfers between devices: 299 us -> 70.9 us
  starting transfers between devices: 0.16 us -> 62.2 us
  local copies, waits for them, and re-layouts: 0.01 us -> 20 us
  between operations: 13.8 us -> 1.22 us
  other arithmetic: 0 us -> 5.78 us
    reduce_scatter x2 -> x0, waiting for transfers between devices: 156 us -> none  [the longest x1 102 us: per_device(): lax.psum_scatter(part.astype(jnp.float32).astype(jnp.bfloat16), 'col', sc...]
    all_gather x2 -> x0, waiting for transfers between devices: 142 us -> none  [the longest x1 85.4 us: per_device(): gathered = lax.all_gather(hidden, 'col', axis=0, tiled=True)]
    ppermute x0 -> x32, waiting for transfers between devices: none -> 70.9 us  [send(): return lax.ppermute(value, AXES, perm)]
    ppermute x0 -> x32, starting transfers between devices: none -> 62.2 us  [send(): return lax.ppermute(value, AXES, perm)]
    unnamed x2 -> x41, local copies, waits for them, and re-layouts: 0.01 us -> 14.8 us
    dot_general x3 -> x6, matrix products: 39.6 us -> 36.7 us  [dot(): return lax.dot_general(a, b, (dims, ((), ())), preferred_element_type=F32)]
  transfers between devices with their start and end apart: 4 -> 32, of which waited for: 4 -> 9; matrix products, arithmetic and copies ran while one was open for 11% -> 29% of each run, Pallas kernels for 0% -> 0%
where the time goes in v1:
time: 197 us
  waiting for transfers between devices  70.9 us (36%)
  starting transfers between devices  62.2 us (32%)
  matrix products  36.7 us (19%)
  local copies, waits for them, and re-layouts  20 us (10%)
  other arithmetic  5.78 us (3%)
    ppermute x32, waiting for transfers between devices, send(): return lax.ppermute(value, AXES, perm)  70.9 us
    ppermute x32, starting transfers between devices, send(): return lax.ppermute(value, AXES, perm)  62.2 us
    dot_general x6, matrix products, dot(): return lax.dot_general(a, b, (dims, ((), ())), preferred_element_type=F32)  36.7 us
    unnamed x41, local copies, waits for them, and re-layouts  14.8 us
  transfers between devices with their start and end apart: 32, of which 9 were waited for; matrix products, arithmetic and copies ran while one was open for 29% of the time, Pallas kernels for 0%

profile of v1, /device:TPU:1, one launch (start us, length us, event | category | flops | bytes accessed | tf_op | source)
XLA Modules:
  0.0 196.7 jit_solution(14690344092792957445)
XLA Ops:
  0.7 1.0 constant_dynamic-slice_fusion.1
  1.6 1.5 collective-permute-start.16
  3.1 2.6 %collective-permute-start.1 = (bf16[128,3328]{1,0:T(8,128)(2,1)}, bf16[128,3328]{1,0:T(8,128)(2,1)}, u32[]{:S(2)}, u32[]{:S(2)}) collective-permute-start(bf16[128,3328]{1,0:T(8,128)(2,1)} %param.3), channel_id=1, source_target_pairs={{0,2},{1,7},{2,4},{3,1},{4,6},{5,3},{6,0},{7,5},{8,10},{9,15},{10,... | collective-permute-start | bytes 2555912 | tf_op jit(solution)/shard_map/ppermute | solution.py:37
  5.7 2.9 %collective-permute-start.4 = (bf16[128,3328]{1,0:T(8,128)(2,1)}, bf16[128,3328]{1,0:T(8,128)(2,1)}, u32[]{:S(2)}, u32[]{:S(2)}) collective-permute-start(bf16[128,3328]{1,0:T(8,128)(2,1)} %param.3), channel_id=1, source_target_pairs={{0,8},{1,9},{2,10},{3,11},{4,12},{5,13},{6,14},{7,15},{8,0},{9,1},... | collective-permute-start | bytes 2555912 | tf_op jit(solution)/shard_map/ppermute | solution.py:37
  8.6 0.9 pad_maximum_fusion.8
  9.5 0.4 collective-permute-start.17
  9.9 4.0 %constant_dynamic-update-slice_fusion.1 = bf16[3328,1024]{1,0:T(8,128)(2,1)} fusion(bf16[3328,512]{1,0:T(8,128)(2,1)} %param.4), kind=kLoop, calls=%fused_computation.89 | loop fusion | bytes 6815744
  13.9 19.2 %collective-permute-done.17 = bf16[128,1024]{1,0:T(8,128)(2,1)} collective-permute-done((bf16[128,1024]{1,0:T(8,128)(2,1)}, bf16[128,1024]{1,0:T(8,128)(2,1)}, u32[]{:S(2)}, u32[]{:S(2)}) %collective-permute-start.17) | collective-permute-done | bytes 262176 | tf_op jit(solution)/shard_map/ppermute | solution.py:37
  33.1 1.0 pad_maximum_fusion.7
  34.2 3.8 %collective-permute-start.19 = (bf16[256,1024]{1,0:T(8,128)(2,1)S(1)}, bf16[256,1024]{1,0:T(8,128)(2,1)S(1)}, u32[]{:S(2)}, u32[]{:S(2)}) collective-permute-start(bf16[256,1024]{1,0:T(8,128)(2,1)S(1)} %pad_maximum_fusion.7), channel_id=1, source_target_pairs={{0,32},{1,97},{2,34},{3,99},{4,36},{5,101},{6,38},{7,103},{8,40},{... | collective-permute-start | bytes 1572872 | tf_op jit(solution)/shard_map/ppermute | solution.py:37
  38.0 1.2 constant_dynamic-update-slice_fusion.24
  39.3 1.7 constant_dynamic-update-slice_fusion.12
  41.0 2.1 %collective-permute-start.3 = (bf16[3328,512]{1,0:T(8,128)(2,1)S(1)}, bf16[3328,512]{1,0:T(8,128)(2,1)S(1)}, u32[]{:S(2)}, u32[]{:S(2)}) collective-permute-start(bf16[3328,512]{1,0:T(8,128)(2,1)S(1)} %copy-done), channel_id=1, source_target_pairs={{0,1},{1,0},{2,3},{3,2},{4,5},{5,4},{6,7},{7,6},{8,9},{9,8},{10,11... | collective-permute-start | bytes 10223624 | tf_op jit(solution)/shard_map/ppermute | solution.py:37
  43.0 1.1 slice.115
  44.1 0.3 collective-permute-start.6
  44.4 1.0 slice.114
  45.4 2.5 %collective-permute-start.8 = (bf16[80,3328]{1,0:T(8,128)(2,1)S(1)}, bf16[80,3328]{1,0:T(8,128)(2,1)S(1)}, u32[]{:S(2)}, u32[]{:S(2)}) collective-permute-start(bf16[80,3328]{1,0:T(8,128)(2,1)S(1)} %slice.115), channel_id=1, source_target_pairs={{0,2},{1,7},{2,4},{3,1},{4,6},{5,3},{6,0},{7,5},{8,10},{9,15},{10,... | collective-permute-start | bytes 1597448 | tf_op jit(solution)/shard_map/ppermute | solution.py:37
  48.0 1.0 slice.117
  49.0 2.0 %collective-permute-start.20 = (bf16[256,1024]{1,0:T(8,128)(2,1)S(1)}, bf16[256,1024]{1,0:T(8,128)(2,1)S(1)}, u32[]{:S(2)}, u32[]{:S(2)}) collective-permute-start(bf16[256,1024]{1,0:T(8,128)(2,1)S(1)} %collective-permute-done.19), channel_id=1, source_target_pairs={{0,32},{1,97},{2,34},{3,99},{4,36},{5,101},{6,38},{7,103},{8,40},{... | collective-permute-start | bytes 1572872 | tf_op jit(solution)/shard_map/ppermute | solution.py:37
  51.0 1.2 constant_dynamic-update-slice_fusion.23
  52.2 1.6 collective-permute-start.5
  53.9 3.5 %collective-permute-done.20 = bf16[256,1024]{1,0:T(8,128)(2,1)S(1)} collective-permute-done((bf16[256,1024]{1,0:T(8,128)(2,1)S(1)}, bf16[256,1024]{1,0:T(8,128)(2,1)S(1)}, u32[]{:S(2)}, u32[]{:S(2)}) %collective-permute-start.20) | collective-permute-done | bytes 524320 | tf_op jit(solution)/shard_map/ppermute | solution.py:37
  57.4 3.5 %collective-permute-start.2 = (bf16[128,3328]{1,0:T(8,128)(2,1)}, bf16[128,3328]{1,0:T(8,128)(2,1)S(1)}, u32[]{:S(2)}, u32[]{:S(2)}) collective-permute-start(bf16[128,3328]{1,0:T(8,128)(2,1)} %collective-permute-done.1), channel_id=1, source_target_pairs={{0,2},{1,7},{2,4},{3,1},{4,6},{5,3},{6,0},{7,5},{8,10},{9,15},{10,... | collective-permute-start | bytes 2555912 | tf_op jit(solution)/shard_map/ppermute | solution.py:37
  61.3 1.6 collective-permute-start.10
  63.0 7.8 %collective-permute-done.2 = bf16[128,3328]{1,0:T(8,128)(2,1)S(1)} collective-permute-done((bf16[128,3328]{1,0:T(8,128)(2,1)}, bf16[128,3328]{1,0:T(8,128)(2,1)S(1)}, u32[]{:S(2)}, u32[]{:S(2)}) %collective-permute-start.2) | collective-permute-done | bytes 852000 | tf_op jit(solution)/shard_map/ppermute | solution.py:37
  70.8 3.1 %collective-permute-start.9 = (bf16[80,3328]{1,0:T(8,128)(2,1)S(1)}, bf16[80,3328]{1,0:T(8,128)(2,1)S(1)}, u32[]{:S(2)}, u32[]{:S(2)}) collective-permute-start(bf16[80,3328]{1,0:T(8,128)(2,1)S(1)} %collective-permute-done.8), channel_id=1, source_target_pairs={{0,2},{1,7},{2,4},{3,1},{4,6},{5,3},{6,0},{7,5},{8,10},{9,15},{10,... | collective-permute-start | bytes 1597448 | tf_op jit(solution)/shard_map/ppermute | solution.py:37
  73.9 1.2 constant_dynamic-update-slice_fusion.21
  75.1 1.3 constant_dynamic-update-slice_fusion.20
  76.5 1.6 collective-permute-start.7
  78.2 7.4 %collective-permute-done.7 = bf16[48,3328]{1,0:T(8,128)(2,1)S(1)} collective-permute-done((bf16[48,3328]{1,0:T(8,128)(2,1)S(1)}, bf16[48,3328]{1,0:T(8,128)(2,1)S(1)}, u32[]{:S(2)}, u32[]{:S(2)}) %collective-permute-start.7) | collective-permute-done | bytes 319520 | tf_op jit(solution)/shard_map/ppermute | solution.py:37
  85.9 3.5 %copy-done.5 = bf16[1024,3328]{1,0:T(8,128)(2,1)} copy-done((bf16[1024,3328]{1,0:T(8,128)(2,1)}, bf16[1024,3328]{1,0:T(8,128)(2,1)S(1)}, u32[]{:S(2)}) %copy-start.5) | copy-done | bytes 6815768
  89.4 9.6 %convolution_convert_fusion = bf16[3328,512]{1,0:T(8,128)(2,1)} fusion(bf16[1024,3328]{1,0:T(8,128)(2,1)} %copy-done.5, bf16[1024,1024]{1,0:T(8,128)(2,1)S(1)} %get-tuple-element.3), kind=kOutput, calls=%fused_computation.1 | convolution fusion | flops 3491364864 | bytes 11272192 | tf_op jit(solution)/shard_map/dot_general | solution.py:48
  99.0 2.3 %collective-permute-start.31 = (bf16[3328,512]{1,0:T(8,128)(2,1)}, bf16[3328,512]{1,0:T(8,128)(2,1)}, u32[]{:S(2)}, u32[]{:S(2)}) collective-permute-start(bf16[3328,512]{1,0:T(8,128)(2,1)} %convolution_convert_fusion), channel_id=1, source_target_pairs={{0,1},{1,0},{2,3},{3,2},{4,5},{5,4},{6,7},{7,6},{8,9},{9,8},{10,11... | collective-permute-start | bytes 10223624 | tf_op jit(solution)/shard_map/ppermute | solution.py:37
  101.4 0.5 constant_dynamic-update-slice_fusion
  101.9 4.7 %convolution_convert_fusion.1 = bf16[512,3328]{1,0:T(8,128)(2,1)S(1)} fusion(bf16[3328,1024]{1,0:T(8,128)(2,1)S(1)} %constant_dynamic-update-slice_fusion, bf16[128,1024]{1,0:T(8,128)(2,1)S(1)} %get-tuple-element.4, bf16[128,1024]{1,0:T(8,128)(2,1)S(1)} %get-tuple-element.6, bf16[128,1024]{1,0:T(8,128)(2,1)S(1)} %get-tuple-element.8, ...), kind=kOutput, calls=%fused_computation.2 | convolution fusion | flops 3495559168 | bytes 11272192 | tf_op jit(solution)/shard_map/dot_general | solution.py:48
  106.8 1.5 collective-permute-start.21
  108.4 1.6 collective-permute-start.26
  110.0 4.7 %convolution_convert_fusion.2 = bf16[512,3328]{1,0:T(8,128)(2,1)S(1)} fusion(bf16[3328,1024]{1,0:T(8,128)(2,1)S(1)} %constant_dynamic-update-slice_fusion, bf16[128,1024]{1,0:T(8,128)(2,1)S(1)} %get-tuple-element.12, bf16[128,1024]{1,0:T(8,128)(2,1)S(1)} %get-tuple-element.14, bf16[128,1024]{1,0:T(8,128)(2,1)S(1)} %get-tuple-element.16, ...), kind=kOutput, calls=%fused_computation.3 | convolution fusion | flops 3495559168 | bytes 11272192 | tf_op jit(solution)/shard_map/dot_general | solution.py:48
  114.8 5.8 %convolution_convert_fusion.3 = bf16[512,1024]{1,0:T(8,128)(2,1)S(1)} fusion(bf16[512,3328]{1,0:T(8,128)(2,1)} %copy-done.4, bf16[3328,1024]{1,0:T(8,128)(2,1)S(1)} %constant_dynamic-update-slice_fusion), kind=kOutput, calls=%fused_computation.15 | convolution fusion | flops 3490185216 | bytes 11272192 | tf_op jit(solution)/shard_map/dot_general | solution.py:48
  120.5 5.2 %fusion.8 = bf16[512,1024]{1,0:T(8,128)(2,1)S(1)} fusion(bf16[3328,1024]{1,0:T(8,128)(2,1)S(1)} %constant_dynamic-update-slice_fusion, bf16[128,3328]{1,0:T(8,128)(2,1)} %collective-permute-done.1, bf16[128,3328]{1,0:T(8,128)(2,1)S(1)} %collective-permute-done.2, bf16[128,3328]{1,0:T(8,128)(2,1)} %collective-permute-done, bf16[128,3328]{1,0:T(8,128)(2,1)S(1)} %copy-done.2), kind=kOutput, calls=%fused_computation.14 | convolution fusion | flops 3503816704 | bytes 11272192 | tf_op jit(solution)/shard_map/dot_general | solution.py:48
  125.9 0.2 dynamic-slice_bitcast_fusion.15
  126.2 3.4 %collective-permute-start.11 = (bf16[256,1024]{1,0:T(8,128)(2,1)S(1)}, bf16[256,1024]{1,0:T(8,128)(2,1)S(1)}, u32[]{:S(2)}, u32[]{:S(2)}) collective-permute-start(bf16[256,1024]{1,0:T(8,128)(2,1)S(1)} %pad_maximum_fusion.5), channel_id=1, source_target_pairs={{0,32},{1,97},{2,34},{3,99},{4,36},{5,101},{6,38},{7,103},{8,40},{... | collective-permute-start | bytes 1572872 | tf_op jit(solution)/shard_map/ppermute | solution.py:37
  129.6 0.3 collective-permute-start.13
  130.0 8.4 %collective-permute-done.11 = bf16[256,1024]{1,0:T(8,128)(2,1)S(1)} collective-permute-done((bf16[256,1024]{1,0:T(8,128)(2,1)S(1)}, bf16[256,1024]{1,0:T(8,128)(2,1)S(1)}, u32[]{:S(2)}, u32[]{:S(2)}) %collective-permute-start.11) | collective-permute-done | bytes 524320 | tf_op jit(solution)/shard_map/ppermute | solution.py:37
  138.4 0.2 add_convert_fusion.3
  138.6 3.5 %collective-permute-start.12 = (bf16[256,1024]{1,0:T(8,128)(2,1)S(1)}, bf16[256,1024]{1,0:T(8,128)(2,1)S(1)}, u32[]{:S(2)}, u32[]{:S(2)}) collective-permute-start(bf16[256,1024]{1,0:T(8,128)(2,1)S(1)} %add_convert_fusion.3), channel_id=1, source_target_pairs={{0,32},{1,97},{2,34},{3,99},{4,36},{5,101},{6,38},{7,103},{8,40},{... | collective-permute-start | bytes 1572872 | tf_op jit(solution)/shard_map/ppermute | solution.py:37
  142.2 2.9 %collective-permute-start.22 = (bf16[80,3328]{1,0:T(8,128)(2,1)S(1)}, bf16[80,3328]{1,0:T(8,128)(2,1)S(1)}, u32[]{:S(2)}, u32[]{:S(2)}) collective-permute-start(bf16[80,3328]{1,0:T(8,128)(2,1)S(1)} %fusion.12), channel_id=1, source_target_pairs={{0,2},{1,7},{2,4},{3,1},{4,6},{5,3},{6,0},{7,5},{8,10},{9,15},{10,... | collective-permute-start | bytes 1597448 | tf_op jit(solution)/shard_map/ppermute | solution.py:37
  145.1 1.5 collective-permute-start.25
  146.6 1.6 collective-permute-done.12
  148.2 1.4 collective-permute-start.29
  149.6 0.3 add_convert_fusion.2
  149.9 2.8 %collective-permute-start.27 = (bf16[128,3328]{1,0:T(8,128)(2,1)S(1)}, bf16[128,3328]{1,0:T(8,128)(2,1)S(1)}, u32[]{:S(2)}, u32[]{:S(2)}) collective-permute-start(bf16[128,3328]{1,0:T(8,128)(2,1)S(1)} %pad_maximum_fusion.2), channel_id=1, source_target_pairs={{0,2},{1,7},{2,4},{3,1},{4,6},{5,3},{6,0},{7,5},{8,10},{9,15},{10,... | collective-permute-start | bytes 2555912 | tf_op jit(solution)/shard_map/ppermute | solution.py:37
  152.8 1.1 collective-permute-start.14
  153.8 0.2 fusion.14
  154.1 8.3 %collective-permute-done.27 = bf16[128,3328]{1,0:T(8,128)(2,1)S(1)} collective-permute-done((bf16[128,3328]{1,0:T(8,128)(2,1)S(1)}, bf16[128,3328]{1,0:T(8,128)(2,1)S(1)}, u32[]{:S(2)}, u32[]{:S(2)}) %collective-permute-start.27) | collective-permute-done | bytes 852000 | tf_op jit(solution)/shard_map/ppermute | solution.py:37
  162.4 1.6 collective-permute-start.24
  164.1 0.2 fusion.34
  164.4 3.2 %collective-permute-start.28 = (bf16[128,3328]{1,0:T(8,128)(2,1)S(1)}, bf16[128,3328]{1,0:T(8,128)(2,1)S(1)}, u32[]{:S(2)}, u32[]{:S(2)}) collective-permute-start(bf16[128,3328]{1,0:T(8,128)(2,1)S(1)} %pad_maximum_fusion.3), channel_id=1, source_target_pairs={{0,2},{1,7},{2,4},{3,1},{4,6},{5,3},{6,0},{7,5},{8,10},{9,15},{10,... | collective-permute-start | bytes 2555912 | tf_op jit(solution)/shard_map/ppermute | solution.py:37
  167.6 5.4 %collective-permute-start.15 = (bf16[128,512]{1,0:T(8,128)(2,1)S(1)}, bf16[128,512]{1,0:T(8,128)(2,1)S(1)}, u32[]{:S(2)}, u32[]{:S(2)}) collective-permute-start(bf16[128,512]{1,0:T(8,128)(2,1)S(1)} %get-tuple-element.56), channel_id=1, source_target_pairs={{0,1},{1,0},{2,3},{3,2},{4,5},{5,4},{6,7},{7,6},{8,9},{9,8},{10,11... | collective-permute-start | bytes 393224 | tf_op jit(solution)/shard_map/ppermute | solution.py:37
  173.2 0.8 collective-permute-done.15
  174.0 0.8 maximum_select_fusion
  174.8 6.7 %add_convert_fusion = bf16[3328,512]{1,0:T(8,128)(2,1)} fusion(bf16[3328,512]{1,0:T(8,128)(2,1)} %collective-permute-done.31, bf16[1024,3328]{1,0:T(8,128)(2,1)S(1)} %bitcast.117, bf16[1024,1024]{1,0:T(8,128)(2,1)S(1)} %get-tuple-element.3), kind=kOutput, calls=%fused_computation | convolution fusion | flops 3494772736 | bytes 14680064 | tf_op jit(solution)/shard_map/dot_general | solution.py:48
  181.5 13.8 %collective-permute-done.30 = bf16[128,3328]{1,0:T(8,128)(2,1)S(1)} collective-permute-done((bf16[128,3328]{1,0:T(8,128)(2,1)S(1)}, bf16[128,3328]{1,0:T(8,128)(2,1)S(1)}, u32[]{:S(2)}, u32[]{:S(2)}) %collective-permute-start.30) | collective-permute-done | bytes 852000 | tf_op jit(solution)/shard_map/ppermute | solution.py:37
  195.3 1.4 add_convert_fusion.1
  (83 shorter events, 2.3 us)
Async XLA Ops:
  1.6 7.0 %collective-permute-start.16 = (bf16[128,512]{1,0:T(8,128)(2,1)S(1)}, bf16[128,512]{1,0:T(8,128)(2,1)S(1)}, u32[]{:S(2)}, u32[]{:S(2)}) collective-permute-start(bf16[128,512]{1,0:T(8,128)(2,1)S(1)} %get-tuple-element.54), channel_id=1, source_target_pairs={{0,1},{1,0},{2,3},{3,2},{4,5},{5,4},{6,7},{7,6},{8,9},{9,8},{10,11... | collective-permute-start | bytes 393224 | tf_op jit(solution)/shard_map/ppermute | solution.py:37
  3.1 42.3 %collective-permute-start.1 = (bf16[128,3328]{1,0:T(8,128)(2,1)}, bf16[128,3328]{1,0:T(8,128)(2,1)}, u32[]{:S(2)}, u32[]{:S(2)}) collective-permute-start(bf16[128,3328]{1,0:T(8,128)(2,1)} %param.3), channel_id=1, source_target_pairs={{0,2},{1,7},{2,4},{3,1},{4,6},{5,3},{6,0},{7,5},{8,10},{9,15},{10,... | collective-permute-start | bytes 2555912 | tf_op jit(solution)/shard_map/ppermute | solution.py:37
  5.7 38.4 %collective-permute-start = (bf16[128,3328]{1,0:T(8,128)(2,1)}, bf16[128,3328]{1,0:T(8,128)(2,1)}, u32[]{:S(2)}, u32[]{:S(2)}) collective-permute-start(bf16[128,3328]{1,0:T(8,128)(2,1)} %param.3), channel_id=1, source_target_pairs={{0,6},{1,3},{2,0},{3,5},{4,2},{5,7},{6,4},{7,1},{8,14},{9,11},{10,... | collective-permute-start | bytes 2555912 | tf_op jit(solution)/shard_map/ppermute | solution.py:37
  5.7 35.2 %collective-permute-start.4 = (bf16[128,3328]{1,0:T(8,128)(2,1)}, bf16[128,3328]{1,0:T(8,128)(2,1)}, u32[]{:S(2)}, u32[]{:S(2)}) collective-permute-start(bf16[128,3328]{1,0:T(8,128)(2,1)} %param.3), channel_id=1, source_target_pairs={{0,8},{1,9},{2,10},{3,11},{4,12},{5,13},{6,14},{7,15},{8,0},{9,1},... | collective-permute-start | bytes 2555912 | tf_op jit(solution)/shard_map/ppermute | solution.py:37
  8.6 1.3 copy-start.3
  9.5 23.6 %collective-permute-start.17 = (bf16[128,1024]{1,0:T(8,128)(2,1)}, bf16[128,1024]{1,0:T(8,128)(2,1)}, u32[]{:S(2)}, u32[]{:S(2)}) collective-permute-start(bf16[128,1024]{1,0:T(8,128)(2,1)} %get-tuple-element.51), channel_id=1, source_target_pairs={{0,16},{1,17},{2,18},{3,19},{4,20},{5,21},{6,22},{7,23},{8,24},{9,... | collective-permute-start | bytes 786440 | tf_op jit(solution)/shard_map/ppermute | solution.py:37
  13.9 27.1 %copy-start = (bf16[3328,512]{1,0:T(8,128)(2,1)S(1)}, bf16[3328,512]{1,0:T(8,128)(2,1)}, u32[]{:S(2)}) copy-start(bf16[3328,512]{1,0:T(8,128)(2,1)} %param.4) | copy-start | bytes 10223620
  34.2 14.8 %collective-permute-start.19 = (bf16[256,1024]{1,0:T(8,128)(2,1)S(1)}, bf16[256,1024]{1,0:T(8,128)(2,1)S(1)}, u32[]{:S(2)}, u32[]{:S(2)}) collective-permute-start(bf16[256,1024]{1,0:T(8,128)(2,1)S(1)} %pad_maximum_fusion.7), channel_id=1, source_target_pairs={{0,32},{1,97},{2,34},{3,99},{4,36},{5,101},{6,38},{7,103},{8,40},{... | collective-permute-start | bytes 1572872 | tf_op jit(solution)/shard_map/ppermute | solution.py:37
  39.2 13.0 %collective-permute-start.18 = (bf16[256,1024]{1,0:T(8,128)(2,1)S(1)}, bf16[256,1024]{1,0:T(8,128)(2,1)S(1)}, u32[]{:S(2)}, u32[]{:S(2)}) collective-permute-start(bf16[256,1024]{1,0:T(8,128)(2,1)S(1)} %pad_maximum_fusion.7), channel_id=1, source_target_pairs={{0,96},{1,33},{2,98},{3,35},{4,100},{5,37},{6,102},{7,39},{8,104},... | collective-permute-start | bytes 1572872 | tf_op jit(solution)/shard_map/ppermute | solution.py:37
  40.9 12.9 %copy-start.1 = (bf16[1024,1024]{1,0:T(8,128)(2,1)S(1)}, bf16[1024,1024]{1,0:T(8,128)(2,1)}, u32[]{:S(2)}) copy-start(bf16[1024,1024]{1,0:T(8,128)(2,1)} %constant_dynamic-update-slice_fusion.12) | copy-start | bytes 6291460
  41.0 60.4 %collective-permute-start.3 = (bf16[3328,512]{1,0:T(8,128)(2,1)S(1)}, bf16[3328,512]{1,0:T(8,128)(2,1)S(1)}, u32[]{:S(2)}, u32[]{:S(2)}) collective-permute-start(bf16[3328,512]{1,0:T(8,128)(2,1)S(1)} %copy-done), channel_id=1, source_target_pairs={{0,1},{1,0},{2,3},{3,2},{4,5},{5,4},{6,7},{7,6},{8,9},{9,8},{10,11... | collective-permute-start | bytes 10223624 | tf_op jit(solution)/shard_map/ppermute | solution.py:37
  44.1 34.0 %collective-permute-start.6 = (bf16[80,3328]{1,0:T(8,128)(2,1)S(1)}, bf16[80,3328]{1,0:T(8,128)(2,1)S(1)}, u32[]{:S(2)}, u32[]{:S(2)}) collective-permute-start(bf16[80,3328]{1,0:T(8,128)(2,1)S(1)} %slice.115), channel_id=1, source_target_pairs={{0,6},{1,3},{2,0},{3,5},{4,2},{5,7},{6,4},{7,1},{8,14},{9,11},{10,... | collective-permute-start | bytes 1597448 | tf_op jit(solution)/shard_map/ppermute | solution.py:37
  45.4 15.9 %collective-permute-start.8 = (bf16[80,3328]{1,0:T(8,128)(2,1)S(1)}, bf16[80,3328]{1,0:T(8,128)(2,1)S(1)}, u32[]{:S(2)}, u32[]{:S(2)}) collective-permute-start(bf16[80,3328]{1,0:T(8,128)(2,1)S(1)} %slice.115), channel_id=1, source_target_pairs={{0,2},{1,7},{2,4},{3,1},{4,6},{5,3},{6,0},{7,5},{8,10},{9,15},{10,... | collective-permute-start | bytes 1597448 | tf_op jit(solution)/shard_map/ppermute | solution.py:37
  49.0 8.4 %collective-permute-start.20 = (bf16[256,1024]{1,0:T(8,128)(2,1)S(1)}, bf16[256,1024]{1,0:T(8,128)(2,1)S(1)}, u32[]{:S(2)}, u32[]{:S(2)}) collective-permute-start(bf16[256,1024]{1,0:T(8,128)(2,1)S(1)} %collective-permute-done.19), channel_id=1, source_target_pairs={{0,32},{1,97},{2,34},{3,99},{4,36},{5,101},{6,38},{7,103},{8,40},{... | collective-permute-start | bytes 1572872 | tf_op jit(solution)/shard_map/ppermute | solution.py:37
  52.2 24.3 %collective-permute-start.5 = (bf16[48,3328]{1,0:T(8,128)(2,1)S(1)}, bf16[48,3328]{1,0:T(8,128)(2,1)S(1)}, u32[]{:S(2)}, u32[]{:S(2)}) collective-permute-start(bf16[48,3328]{1,0:T(8,128)(2,1)S(1)} %slice.114), channel_id=1, source_target_pairs={{0,8},{1,9},{2,10},{3,11},{4,12},{5,13},{6,14},{7,15},{8,0},{9,1},... | collective-permute-start | bytes 958472 | tf_op jit(solution)/shard_map/ppermute | solution.py:37
  57.4 13.4 %collective-permute-start.2 = (bf16[128,3328]{1,0:T(8,128)(2,1)}, bf16[128,3328]{1,0:T(8,128)(2,1)S(1)}, u32[]{:S(2)}, u32[]{:S(2)}) collective-permute-start(bf16[128,3328]{1,0:T(8,128)(2,1)} %collective-permute-done.1), channel_id=1, source_target_pairs={{0,2},{1,7},{2,4},{3,1},{4,6},{5,3},{6,0},{7,5},{8,10},{9,15},{10,... | collective-permute-start | bytes 2555912 | tf_op jit(solution)/shard_map/ppermute | solution.py:37
  61.3 24.5 %collective-permute-start.10 = (bf16[48,3328]{1,0:T(8,128)(2,1)S(1)}, bf16[48,3328]{1,0:T(8,128)(2,1)S(1)}, u32[]{:S(2)}, u32[]{:S(2)}) collective-permute-start(bf16[48,3328]{1,0:T(8,128)(2,1)S(1)} %slice.117), channel_id=1, source_target_pairs={{0,8},{1,9},{2,10},{3,11},{4,12},{5,13},{6,14},{7,15},{8,0},{9,1},... | collective-permute-start | bytes 958472 | tf_op jit(solution)/shard_map/ppermute | solution.py:37
  70.8 14.9 %collective-permute-start.9 = (bf16[80,3328]{1,0:T(8,128)(2,1)S(1)}, bf16[80,3328]{1,0:T(8,128)(2,1)S(1)}, u32[]{:S(2)}, u32[]{:S(2)}) collective-permute-start(bf16[80,3328]{1,0:T(8,128)(2,1)S(1)} %collective-permute-done.8), channel_id=1, source_target_pairs={{0,2},{1,7},{2,4},{3,1},{4,6},{5,3},{6,0},{7,5},{8,10},{9,15},{10,... | collective-permute-start | bytes 1597448 | tf_op jit(solution)/shard_map/ppermute | solution.py:37
  76.5 9.2 %collective-permute-start.7 = (bf16[48,3328]{1,0:T(8,128)(2,1)S(1)}, bf16[48,3328]{1,0:T(8,128)(2,1)S(1)}, u32[]{:S(2)}, u32[]{:S(2)}) collective-permute-start(bf16[48,3328]{1,0:T(8,128)(2,1)S(1)} %slice.116), channel_id=1, source_target_pairs={{0,8},{1,9},{2,10},{3,11},{4,12},{5,13},{6,14},{7,15},{8,0},{9,1},... | collective-permute-start | bytes 958472 | tf_op jit(solution)/shard_map/ppermute | solution.py:37
  85.8 15.5 %slice-start = ((s8[6815744]{0:T(1024)(128)(4,1)}), s8[4194304]{0:T(1024)(128)(4,1)S(1)}, s32[]{:S(2)}) async-start(s8[6815744]{0:T(1024)(128)(4,1)} %bitcast.114), calls=%async_computation | async-start | bytes 8388608
  85.9 3.5 %copy-start.5 = (bf16[1024,3328]{1,0:T(8,128)(2,1)}, bf16[1024,3328]{1,0:T(8,128)(2,1)S(1)}, u32[]{:S(2)}) copy-start(bf16[1024,3328]{1,0:T(8,128)(2,1)S(1)} %get-tuple-element.39) | copy-start | bytes 20447236
  89.4 9.6 %copy-start.4 = (bf16[512,3328]{1,0:T(8,128)(2,1)}, bf16[512,3328]{1,0:T(8,128)(2,1)S(1)}, u32[]{:S(2)}) copy-start(bf16[512,3328]{1,0:T(8,128)(2,1)S(1)} %get-tuple-element.40) | copy-start | bytes 10223620
  89.4 12.0 %slice-start.1 = ((s8[6815744]{0:T(1024)(128)(4,1)}), s8[2621440]{0:T(1024)(128)(4,1)S(1)}, s32[]{:S(2)}) async-start(s8[6815744]{0:T(1024)(128)(4,1)} %bitcast.114), calls=%async_computation.1 | async-start | bytes 5242880
  99.0 75.8 %collective-permute-start.31 = (bf16[3328,512]{1,0:T(8,128)(2,1)}, bf16[3328,512]{1,0:T(8,128)(2,1)}, u32[]{:S(2)}, u32[]{:S(2)}) collective-permute-start(bf16[3328,512]{1,0:T(8,128)(2,1)} %convolution_convert_fusion), channel_id=1, source_target_pairs={{0,1},{1,0},{2,3},{3,2},{4,5},{5,4},{6,7},{7,6},{8,9},{9,8},{10,11... | collective-permute-start | bytes 10223624 | tf_op jit(solution)/shard_map/ppermute | solution.py:37
  106.8 35.2 %collective-permute-start.21 = (bf16[80,3328]{1,0:T(8,128)(2,1)S(1)}, bf16[80,3328]{1,0:T(8,128)(2,1)S(1)}, u32[]{:S(2)}, u32[]{:S(2)}) collective-permute-start(bf16[80,3328]{1,0:T(8,128)(2,1)S(1)} %get-tuple-element.23), channel_id=1, source_target_pairs={{0,2},{1,7},{2,4},{3,1},{4,6},{5,3},{6,0},{7,5},{8,10},{9,15},{10,... | collective-permute-start | bytes 1597448 | tf_op jit(solution)/shard_map/ppermute | solution.py:37
  108.3 41.6 %collective-permute-start.23 = (bf16[80,3328]{1,0:T(8,128)(2,1)S(1)}, bf16[80,3328]{1,0:T(8,128)(2,1)S(1)}, u32[]{:S(2)}, u32[]{:S(2)}) collective-permute-start(bf16[80,3328]{1,0:T(8,128)(2,1)S(1)} %get-tuple-element.24), channel_id=1, source_target_pairs={{0,6},{1,3},{2,0},{3,5},{4,2},{5,7},{6,4},{7,1},{8,14},{9,11},{10,... | collective-permute-start | bytes 1597448 | tf_op jit(solution)/shard_map/ppermute | solution.py:37
  108.4 21.2 %collective-permute-start.26 = (bf16[48,3328]{1,0:T(8,128)(2,1)S(1)}, bf16[48,3328]{1,0:T(8,128)(2,1)S(1)}, u32[]{:S(2)}, u32[]{:S(2)}) collective-permute-start(bf16[48,3328]{1,0:T(8,128)(2,1)S(1)} %get-tuple-element.21), channel_id=1, source_target_pairs={{0,8},{1,9},{2,10},{3,11},{4,12},{5,13},{6,14},{7,15},{8,0},{9,1},... | collective-permute-start | bytes 958472 | tf_op jit(solution)/shard_map/ppermute | solution.py:37
  114.7 5.8 %copy-start.2 = (bf16[128,3328]{1,0:T(8,128)(2,1)S(1)}, bf16[128,3328]{1,0:T(8,128)(2,1)}, u32[]{:S(2)}) copy-start(bf16[128,3328]{1,0:T(8,128)(2,1)} %param.3) | copy-start | bytes 2555908
  126.2 12.2 %collective-permute-start.11 = (bf16[256,1024]{1,0:T(8,128)(2,1)S(1)}, bf16[256,1024]{1,0:T(8,128)(2,1)S(1)}, u32[]{:S(2)}, u32[]{:S(2)}) collective-permute-start(bf16[256,1024]{1,0:T(8,128)(2,1)S(1)} %pad_maximum_fusion.5), channel_id=1, source_target_pairs={{0,32},{1,97},{2,34},{3,99},{4,36},{5,101},{6,38},{7,103},{8,40},{... | collective-permute-start | bytes 1572872 | tf_op jit(solution)/shard_map/ppermute | solution.py:37
  129.6 15.5 %collective-permute-start.13 = (bf16[256,1024]{1,0:T(8,128)(2,1)S(1)}, bf16[256,1024]{1,0:T(8,128)(2,1)S(1)}, u32[]{:S(2)}, u32[]{:S(2)}) collective-permute-start(bf16[256,1024]{1,0:T(8,128)(2,1)S(1)} %pad_maximum_fusion.6), channel_id=1, source_target_pairs={{0,96},{1,33},{2,98},{3,35},{4,100},{5,37},{6,102},{7,39},{8,104},... | collective-permute-start | bytes 1572872 | tf_op jit(solution)/shard_map/ppermute | solution.py:37
  138.6 9.6 %collective-permute-start.12 = (bf16[256,1024]{1,0:T(8,128)(2,1)S(1)}, bf16[256,1024]{1,0:T(8,128)(2,1)S(1)}, u32[]{:S(2)}, u32[]{:S(2)}) collective-permute-start(bf16[256,1024]{1,0:T(8,128)(2,1)S(1)} %add_convert_fusion.3), channel_id=1, source_target_pairs={{0,32},{1,97},{2,34},{3,99},{4,36},{5,101},{6,38},{7,103},{8,40},{... | collective-permute-start | bytes 1572872 | tf_op jit(solution)/shard_map/ppermute | solution.py:37
  142.2 10.6 %collective-permute-start.22 = (bf16[80,3328]{1,0:T(8,128)(2,1)S(1)}, bf16[80,3328]{1,0:T(8,128)(2,1)S(1)}, u32[]{:S(2)}, u32[]{:S(2)}) collective-permute-start(bf16[80,3328]{1,0:T(8,128)(2,1)S(1)} %fusion.12), channel_id=1, source_target_pairs={{0,2},{1,7},{2,4},{3,1},{4,6},{5,3},{6,0},{7,5},{8,10},{9,15},{10,... | collective-permute-start | bytes 1597448 | tf_op jit(solution)/shard_map/ppermute | solution.py:37
  145.1 19.0 %collective-permute-start.25 = (bf16[48,3328]{1,0:T(8,128)(2,1)S(1)}, bf16[48,3328]{1,0:T(8,128)(2,1)S(1)}, u32[]{:S(2)}, u32[]{:S(2)}) collective-permute-start(bf16[48,3328]{1,0:T(8,128)(2,1)S(1)} %get-tuple-element.22), channel_id=1, source_target_pairs={{0,8},{1,9},{2,10},{3,11},{4,12},{5,13},{6,14},{7,15},{8,0},{9,1},... | collective-permute-start | bytes 958472 | tf_op jit(solution)/shard_map/ppermute | solution.py:37
  148.2 15.9 %collective-permute-start.29 = (bf16[48,3328]{1,0:T(8,128)(2,1)S(1)}, bf16[48,3328]{1,0:T(8,128)(2,1)S(1)}, u32[]{:S(2)}, u32[]{:S(2)}) collective-permute-start(bf16[48,3328]{1,0:T(8,128)(2,1)S(1)} %get-tuple-element.20), channel_id=1, source_target_pairs={{0,8},{1,9},{2,10},{3,11},{4,12},{5,13},{6,14},{7,15},{8,0},{9,1},... | collective-permute-start | bytes 958472 | tf_op jit(solution)/shard_map/ppermute | solution.py:37
  149.6 25.2 %slice-start.2 = ((s8[6815744]{0:T(1024)(128)(4,1)}), s8[4194304]{0:T(1024)(128)(4,1)S(1)}, s32[]{:S(2)}) async-start(s8[6815744]{0:T(1024)(128)(4,1)} %bitcast.116), calls=%async_computation.2 | async-start | bytes 8388608
  149.9 12.5 %collective-permute-start.27 = (bf16[128,3328]{1,0:T(8,128)(2,1)S(1)}, bf16[128,3328]{1,0:T(8,128)(2,1)S(1)}, u32[]{:S(2)}, u32[]{:S(2)}) collective-permute-start(bf16[128,3328]{1,0:T(8,128)(2,1)S(1)} %pad_maximum_fusion.2), channel_id=1, source_target_pairs={{0,2},{1,7},{2,4},{3,1},{4,6},{5,3},{6,0},{7,5},{8,10},{9,15},{10,... | collective-permute-start | bytes 2555912 | tf_op jit(solution)/shard_map/ppermute | solution.py:37
  152.8 14.8 %collective-permute-start.14 = (bf16[128,1024]{1,0:T(8,128)(2,1)S(1)}, bf16[128,1024]{1,0:T(8,128)(2,1)S(1)}, u32[]{:S(2)}, u32[]{:S(2)}) collective-permute-start(bf16[128,1024]{1,0:T(8,128)(2,1)S(1)} %slice.119), channel_id=1, source_target_pairs={{0,16},{1,17},{2,18},{3,19},{4,20},{5,21},{6,22},{7,23},{8,24},{9,... | collective-permute-start | bytes 786440 | tf_op jit(solution)/shard_map/ppermute | solution.py:37
  154.1 20.7 %slice-start.3 = ((s8[6815744]{0:T(1024)(128)(4,1)}), s8[2621440]{0:T(1024)(128)(4,1)S(1)}, s32[]{:S(2)}) async-start(s8[6815744]{0:T(1024)(128)(4,1)} %bitcast.116), calls=%async_computation.3 | async-start | bytes 5242880
  162.4 19.1 %collective-permute-start.24 = (bf16[128,3328]{1,0:T(8,128)(2,1)S(1)}, bf16[128,3328]{1,0:T(8,128)(2,1)S(1)}, u32[]{:S(2)}, u32[]{:S(2)}) collective-permute-start(bf16[128,3328]{1,0:T(8,128)(2,1)S(1)} %pad_maximum_fusion.1), channel_id=1, source_target_pairs={{0,8},{1,9},{2,10},{3,11},{4,12},{5,13},{6,14},{7,15},{8,0},{9,1},... | collective-permute-start | bytes 2555912 | tf_op jit(solution)/shard_map/ppermute | solution.py:37
  164.4 17.2 %collective-permute-start.28 = (bf16[128,3328]{1,0:T(8,128)(2,1)S(1)}, bf16[128,3328]{1,0:T(8,128)(2,1)S(1)}, u32[]{:S(2)}, u32[]{:S(2)}) collective-permute-start(bf16[128,3328]{1,0:T(8,128)(2,1)S(1)} %pad_maximum_fusion.3), channel_id=1, source_target_pairs={{0,2},{1,7},{2,4},{3,1},{4,6},{5,3},{6,0},{7,5},{8,10},{9,15},{10,... | collective-permute-start | bytes 2555912 | tf_op jit(solution)/shard_map/ppermute | solution.py:37
  167.6 6.4 %collective-permute-start.15 = (bf16[128,512]{1,0:T(8,128)(2,1)S(1)}, bf16[128,512]{1,0:T(8,128)(2,1)S(1)}, u32[]{:S(2)}, u32[]{:S(2)}) collective-permute-start(bf16[128,512]{1,0:T(8,128)(2,1)S(1)} %get-tuple-element.56), channel_id=1, source_target_pairs={{0,1},{1,0},{2,3},{3,2},{4,5},{5,4},{6,7},{7,6},{8,9},{9,8},{10,11... | collective-permute-start | bytes 393224 | tf_op jit(solution)/shard_map/ppermute | solution.py:37
  173.1 22.2 %collective-permute-start.30 = (bf16[128,3328]{1,0:T(8,128)(2,1)S(1)}, bf16[128,3328]{1,0:T(8,128)(2,1)S(1)}, u32[]{:S(2)}, u32[]{:S(2)}) collective-permute-start(bf16[128,3328]{1,0:T(8,128)(2,1)S(1)} %pad_maximum_fusion.4), channel_id=1, source_target_pairs={{0,6},{1,3},{2,0},{3,5},{4,2},{5,7},{6,4},{7,1},{8,14},{9,11},{10,... | collective-permute-start | bytes 2555912 | tf_op jit(solution)/shard_map/ppermute | solution.py:37

commit v2 on v1

v2 whole, which is shorter than its diff:
```python
import jax
import jax.numpy as jnp
from jax import lax
from jax.experimental import pallas as pl
from jax.experimental.pallas import tpu as pltpu
from jax.sharding import PartitionSpec as P

BF, F32 = jnp.bfloat16, jnp.float32
AXES = ("row", "col")
GATHER_VIA_Y = 48
REDUCE_VIA_Y = 32


def place(row, col):
    z, y_lo = divmod(row, 2)
    y_hi, rest = divmod(col, 8)
    x, core = divmod(rest, 2)
    return x, y_hi, y_lo, z, core


def permutation(move):
    pairs = []
    for row in range(8):
        for col in range(16):
            x, y_hi, y_lo, z, core = move(*place(row, col))
            pairs.append((row * 16 + col, (z % 4 * 2 + y_lo) * 16 + y_hi * 8 + x % 4 * 2 + core))
    return pairs


X1 = permutation(lambda x, yh, yl, z, c: (x + 1 - 2 * c, yh, yl, z, c))
X2 = permutation(lambda x, yh, yl, z, c: (x - 1 + 2 * c, yh, yl, z, c))
Z1 = permutation(lambda x, yh, yl, z, c: (x, yh, yl, z + 1 - 2 * c, c))
Z2 = permutation(lambda x, yh, yl, z, c: (x, yh, yl, z - 1 + 2 * c, c))
YH = permutation(lambda x, yh, yl, z, c: (x, 1 - yh, yl, z, c))
YL = permutation(lambda x, yh, yl, z, c: (x, yh, 1 - yl, z, c))
CORE = permutation(lambda x, yh, yl, z, c: (x, yh, yl, z, 1 - c))


def send(value, perm):
    return lax.ppermute(value, AXES, perm)


def add(*terms):
    total = terms[0].astype(F32)
    for term in terms[1:]:
        total = total + term.astype(F32)
    return total.astype(BF)


def tie(*values):
    return lax.optimization_barrier(values)


def dot(a, b, dims):
    return lax.dot_general(a, b, (dims, ((), ())), preferred_element_type=F32)


def pick(blocks, order):
    def kernel(order_ref, blocks_ref, picked_ref):
        for j in range(len(order)):
            picked_ref[j] = blocks_ref[order_ref[j]]

    return pl.pallas_call(
        kernel,
        out_shape=jax.ShapeDtypeStruct((len(order), *blocks.shape[1:]), blocks.dtype),
        in_specs=[
            pl.BlockSpec(memory_space=pltpu.SMEM),
            pl.BlockSpec(memory_space=pltpu.VMEM),
        ],
        out_specs=pl.BlockSpec(memory_space=pltpu.VMEM),
        compiler_params=pltpu.CompilerParams(vmem_limit_bytes=12 << 20),
        cost_estimate=pl.CostEstimate(flops=0, bytes_accessed=2 * blocks.size, transcendentals=0),
    )(jnp.stack(order).astype(jnp.int32), blocks)


def per_device(hidden, weight, grad_out):
    row, col = lax.axis_index("row"), lax.axis_index("col")
    core = col % 2
    x, y_hi = col // 2 % 4, col // 8
    z, y_lo = row // 2, row % 2
    s = 1 - 2 * core
    a, b = GATHER_VIA_Y, REDUCE_VIA_Y

    h0 = hidden
    side = send(grad_out, YL)
    h3 = send(h0, X1)
    w_other = send(weight, CORE)
    g = jnp.concatenate([grad_out, side], axis=0)
    h0, h3, g, w_other = tie(h0, h3, g, w_other)
    g3, g1 = send(g, Z1), send(g, Z2)
    h1, h2, k0b = send(h0, X2), send(h3, X1), send(h0[a:], YH)
    g2 = send(g3, Z1)
    w = jnp.concatenate([weight, w_other], axis=1)
    h1, h2, k0b, g1, g2, w = tie(h1, h2, k0b, g1, g2, w)
    k3b, k1b = send(k0b, X1), send(k0b, X2)
    ka = send(jnp.concatenate([h0[:a], h1[:a], h2[:a], h3[:a]], axis=0), YH)
    g = jnp.concatenate([g, g1, g2, g3], axis=0).reshape(16, 128, 512)

    def order_of(which):
        t = 1 - 2 * which
        order = []
        for j in range(8):
            r = (y_hi + j // 4) % 2 * 4 + (x + t * (j % 4)) % 4
            order.append(((r // 2 - z) * s) % 4 * 4 + (r + y_lo) % 2 * 2 + which)
        return order

    picked = pick(g, order_of(core) + order_of(1 - core)).reshape(2048, 512)
    g = jnp.concatenate([picked[:1024], send(picked[1024:], CORE)], axis=1)

    far = dot(g[512:], w, ((1,), (1,))).astype(BF).reshape(4, 128, 3328)
    far, k3b, k1b, g, h0, k0b = tie(far, k3b, k1b, g, h0, k0b)
    k2b = send(k3b, X1)
    r3, r2 = send(far[2, b:], X1), send(far[3, b:], X2)
    n = send(far[:, :b].reshape(4 * b, 3328), YH).reshape(4, b, 3328)
    near = dot(g[:512], w, ((1,), (1,))).astype(BF).reshape(4, 128, 3328)
    h_near = jnp.concatenate([h0, h1, h2, h3], axis=0)
    r1 = add(far[1, b:], r3)
    r1, k0b = tie(r1, k0b)
    r1 = send(r1, X1)
    ka = ka.reshape(4, a, 3328)
    h_far = jnp.concatenate([ka[0], k0b, ka[1], k1b, ka[2], k2b, ka[3], k3b], axis=0)

    out = jnp.concatenate(
        [dot(h_near, w, ((1,), (0,))).astype(BF), dot(h_far, w, ((1,), (0,))).astype(BF)], axis=0
    )

    d3 = jnp.concatenate([add(near[2, :b], n[2]), near[2, b:]], axis=0)
    d2 = jnp.concatenate([add(near[3, :b], n[3]), near[3, b:]], axis=0)
    h = jnp.concatenate([h_near, h_far], axis=0)
    h, out, d3, d2 = tie(h, out, d3, d2)
    d3, d2 = send(d3, X1), send(d2, X2)
    n0 = send(add(far[0, b:], r1, r2), YH)

    d1 = jnp.concatenate([add(near[1, :b], n[1], d3[:b]), add(near[1, b:], d3[b:])], axis=0)
    d1 = send(d1, X1)
    order = [(r // 4 + y_hi) % 2 * 4 + ((r % 4 - x) * s) % 4 for r in range(8)]
    out = pick(out.reshape(8, 128, 1024), order)
    out = lax.all_to_all(out, "row", 0, 0, tiled=True)
    o = jnp.sum(out.astype(F32), axis=0).astype(BF)
    own, other = o[:, :512], send(o[:, 512:], CORE)
    output = jnp.where(
        core == 0, jnp.concatenate([own, other], axis=0), jnp.concatenate([other, own], axis=0)
    )

    v = send(dot(h, g[:, 512:], ((0,), (0,))).astype(BF), CORE)
    grad_weight = (dot(h, g[:, :512], ((0,), (0,))) + v.astype(F32)).astype(BF)
    grad_weight, d1 = tie(grad_weight, d1)
    grad_hidden = add(near[0], jnp.concatenate([n[0], n0], axis=0), d1, d2)
    return output, grad_hidden, grad_weight


def solution(mesh):
    placed = (P("col", "row"), P("row", "col"), P("row", "col"))
    return jax.shard_map(
        per_device,
        mesh=mesh,
        in_specs=placed,
        out_specs=(P("row", "col"), P("col", "row"), P("row", "col")),
        check_vma=False,
    )
```

time: 197 us -> 154 us (0.78)
  waiting for transfers between devices: 70.9 us -> 20.5 us
  other arithmetic: 5.78 us -> 22.7 us
  starting transfers between devices: 62.2 us -> 46.2 us
  Pallas kernels: 0 us -> 2.71 us
  matrix products: 36.7 us -> 39.2 us
    ppermute x32 -> x24, waiting for transfers between devices: 70.9 us -> 20.5 us  [send(): return lax.ppermute(value, AXES, perm)]
    ppermute x32 -> x24, starting transfers between devices: 62.2 us -> 42.5 us  [send(): return lax.ppermute(value, AXES, perm)]
    concatenate x8 -> x7, other arithmetic: 2.19 us -> 11.9 us  [the longest x1 5.69 us: per_device(): w = jnp.concatenate([weight, w_other], axis=1)]
    convert_element_type x9 -> x6, other arithmetic: 2.65 us -> 9.49 us  [add(): return total.astype(BF)]
    all_to_all x0 -> x1, starting transfers between devices: none -> 3.68 us  [per_device(): out = lax.all_to_all(out, 'row', 0, 0, tiled=True)]
    pallas_call x0 -> x2, Pallas kernels: none -> 2.71 us  [pick(): pl.pallas_call(kernel, out_shape=jax.ShapeDtypeStruct((len(order), *block...]
    dot_general x6, matrix products: 36.7 us -> 39.2 us  [dot(): return lax.dot_general(a, b, (dims, ((), ())), preferred_element_type=F32)]
    unnamed x41, local copies, waits for them, and re-layouts: 14.8 us -> 12.5 us
  transfers between devices with their start and end apart: 32 -> 25, of which waited for: 9 -> 6; matrix products, arithmetic and copies ran while one was open for 29% -> 50% of each run, Pallas kernels for 0% -> 1%
where the time goes in v2:
time: 154 us; the launch traced here: 153 us
  starting transfers between devices  46.2 us (30%)
  matrix products  39.2 us (25%)
  other arithmetic  22.7 us (15%)
  local copies, waits for them, and re-layouts  21.1 us (14%)
  waiting for transfers between devices  20.5 us (13%)
  Pallas kernels  2.71 us (2%)
    ppermute x24, starting transfers between devices, send(): return lax.ppermute(value, AXES, perm)  42.5 us
    dot_general x6, matrix products, dot(): return lax.dot_general(a, b, (dims, ((), ())), preferred_element_type=F32)  39.2 us
    ppermute x24, waiting for transfers between devices, send(): return lax.ppermute(value, AXES, perm)  20.5 us
    unnamed x41, local copies, waits for them, and re-layouts  12.5 us
    convert_element_type x6, other arithmetic, add(): return total.astype(BF)  9.49 us
    concatenate x1, other arithmetic, per_device(): w = jnp.concatenate([weight, w_other], axis=1)  5.69 us
    all_to_all x1, starting transfers between devices, per_device(): out = lax.all_to_all(out, 'row', 0, 0, tiled=True)  3.68 us
  transfers between devices with their start and end apart: 25, of which 6 were waited for; matrix products, arithmetic and copies ran while one was open for 50% of the time, Pallas kernels for 1%

profile of v2, /device:TPU:1, one launch (start us, length us, event | category | flops | bytes accessed | tf_op | source)
XLA Modules:
  0.0 153.4 jit_solution(17796227759820279990)
XLA Ops:
  0.6 1.5 collective-permute-start.2
  2.1 2.6 %collective-permute-start = (bf16[128,3328]{1,0:T(8,128)(2,1)}, bf16[128,3328]{1,0:T(8,128)(2,1)}, u32[]{:S(2)}, u32[]{:S(2)}) collective-permute-start(bf16[128,3328]{1,0:T(8,128)(2,1)} %param.3), channel_id=1, source_target_pairs={{0,2},{1,7},{2,4},{3,1},{4,6},{5,3},{6,0},{7,5},{8,10},{9,15},{10,... | collective-permute-start | bytes 2555912 | tf_op jit(solution)/shard_map/ppermute | solution.py:40
  4.7 1.3 collective-permute-start.1
  6.0 6.9 %collective-permute-done.1 = bf16[256,512]{1,0:T(8,128)(2,1)S(1)} collective-permute-done((bf16[256,512]{1,0:T(8,128)(2,1)}, bf16[256,512]{1,0:T(8,128)(2,1)S(1)}, u32[]{:S(2)}, u32[]{:S(2)}) %collective-permute-start.1) | collective-permute-done | bytes 262176 | tf_op jit(solution)/shard_map/ppermute | solution.py:40
  12.9 1.8 %pad_maximum_fusion.8 = bf16[512,512]{1,0:T(8,128)(2,1)} fusion(bf16[256,512]{1,0:T(8,128)(2,1)S(1)} %collective-permute-done.1, bf16[256,512]{1,0:T(8,128)(2,1)} %param.5), kind=kLoop, calls=%fused_computation.41 | loop fusion | flops 1048576 | bytes 1048576 | tf_op jit(solution)/shard_map/concatenate | solution.py:88
  14.7 3.8 %collective-permute-start.7 = (bf16[512,512]{1,0:T(8,128)(2,1)}, bf16[512,512]{1,0:T(8,128)(2,1)}, u32[]{:S(2)}, u32[]{:S(2)}) collective-permute-start(bf16[512,512]{1,0:T(8,128)(2,1)} %pad_maximum_fusion.8), channel_id=1, source_target_pairs={{0,32},{1,97},{2,34},{3,99},{4,36},{5,101},{6,38},{7,103},{8,40},{... | collective-permute-start | bytes 1572872 | tf_op jit(solution)/shard_map/ppermute | solution.py:40
  18.4 0.9 collective-permute-start.3
  19.4 2.2 %collective-permute-start.4 = (bf16[128,3328]{1,0:T(8,128)(2,1)}, bf16[128,3328]{1,0:T(8,128)(2,1)}, u32[]{:S(2)}, u32[]{:S(2)}) collective-permute-start(bf16[128,3328]{1,0:T(8,128)(2,1)} %collective-permute-done), channel_id=1, source_target_pairs={{0,2},{1,7},{2,4},{3,1},{4,6},{5,3},{6,0},{7,5},{8,10},{9,15},{10,... | collective-permute-start | bytes 2555912 | tf_op jit(solution)/shard_map/ppermute | solution.py:40
  21.6 1.1 slice.120
  22.8 3.0 %collective-permute-start.5 = (bf16[80,3328]{1,0:T(8,128)(2,1)S(1)}, bf16[80,3328]{1,0:T(8,128)(2,1)S(1)}, u32[]{:S(2)}, u32[]{:S(2)}) collective-permute-start(bf16[80,3328]{1,0:T(8,128)(2,1)S(1)} %slice.120), channel_id=1, source_target_pairs={{0,8},{1,9},{2,10},{3,11},{4,12},{5,13},{6,14},{7,15},{8,0},{9,1},... | collective-permute-start | bytes 1597448 | tf_op jit(solution)/shard_map/ppermute | solution.py:40
  25.8 2.6 %collective-permute-start.8 = (bf16[512,512]{1,0:T(8,128)(2,1)}, bf16[512,512]{1,0:T(8,128)(2,1)S(1)}, u32[]{:S(2)}, u32[]{:S(2)}) collective-permute-start(bf16[512,512]{1,0:T(8,128)(2,1)} %collective-permute-done.7), channel_id=1, source_target_pairs={{0,32},{1,97},{2,34},{3,99},{4,36},{5,101},{6,38},{7,103},{8,40},{... | collective-permute-start | bytes 1572872 | tf_op jit(solution)/shard_map/ppermute | solution.py:40
  28.4 5.7 %pad_maximum_fusion = bf16[3328,1024]{1,0:T(8,128)(2,1)} fusion(bf16[3328,512]{1,0:T(8,128)(2,1)} %collective-permute-done.2, bf16[3328,512]{1,0:T(8,128)(2,1)S(1)} %copy-done.3), kind=kLoop, calls=%fused_computation | loop fusion | flops 13631488 | bytes 13631488 | tf_op jit(solution)/shard_map/concatenate | solution.py:93
  34.1 2.9 %collective-permute-done.5 = bf16[80,3328]{1,0:T(8,128)(2,1)S(1)} collective-permute-done((bf16[80,3328]{1,0:T(8,128)(2,1)S(1)}, bf16[80,3328]{1,0:T(8,128)(2,1)S(1)}, u32[]{:S(2)}, u32[]{:S(2)}) %collective-permute-start.5) | collective-permute-done | bytes 532512 | tf_op jit(solution)/shard_map/ppermute | solution.py:40
  37.0 2.7 %collective-permute-done.3 = bf16[128,3328]{1,0:T(8,128)(2,1)} collective-permute-done((bf16[128,3328]{1,0:T(8,128)(2,1)}, bf16[128,3328]{1,0:T(8,128)(2,1)}, u32[]{:S(2)}, u32[]{:S(2)}) %collective-permute-start.3) | collective-permute-done | bytes 852000 | tf_op jit(solution)/shard_map/ppermute | solution.py:40
  39.7 0.5 collective-permute-done.4
  40.2 1.3 pad_maximum_fusion.2
  41.5 0.7 shard_map.58
  42.2 1.2 fusion.26
  43.4 1.6 %collective-permute-start.9 = (bf16[1024,512]{1,0:T(8,128)(2,1)}, bf16[1024,512]{1,0:T(8,128)(2,1)}, u32[]{:S(2)}, u32[]{:S(2)}) collective-permute-start(bf16[1024,512]{1,0:T(8,128)(2,1)} %bitcast.26), channel_id=1, source_target_pairs={{0,1},{1,0},{2,3},{3,2},{4,5},{5,4},{6,7},{7,6},{8,9},{9,8},{10,11... | collective-permute-start | bytes 3145736 | tf_op jit(solution)/shard_map/ppermute | solution.py:40
  45.1 1.0 slice.129
  46.1 0.7 collective-permute-start.10
  46.8 0.9 collective-permute-start.11
  47.7 1.0 slice.128
  48.6 1.0 slice.127
  49.7 3.0 %collective-permute-start.12 = (bf16[192,3328]{1,0:T(8,128)(2,1)S(1)}, bf16[192,3328]{1,0:T(8,128)(2,1)S(1)}, u32[]{:S(2)}, u32[]{:S(2)}) collective-permute-start(bf16[192,3328]{1,0:T(8,128)(2,1)S(1)} %pad_maximum_fusion.4), channel_id=1, source_target_pairs={{0,8},{1,9},{2,10},{3,11},{4,12},{5,13},{6,14},{7,15},{8,0},{9,1},... | collective-permute-start | bytes 3833864 | tf_op jit(solution)/shard_map/ppermute | solution.py:40
  52.7 1.6 %pad_maximum_fusion.1 = bf16[1024,1024]{1,0:T(8,128)(2,1)S(1)} fusion(bf16[1024,512]{1,0:T(8,128)(2,1)} %collective-permute-done.9, bf16[1024,512]{1,0:T(8,128)(2,1)S(1)} %bitcast.76), kind=kLoop, calls=%fused_computation.14 | loop fusion | flops 4194304 | bytes 4194304 | tf_op jit(solution)/shard_map/concatenate | solution.py:108
  54.4 7.6 %convolution_convert_fusion.2 = bf16[512,3328]{1,0:T(8,128)(2,1)S(1)} fusion(bf16[3328,1024]{1,0:T(8,128)(2,1)} %pad_maximum_fusion, bf16[1024,512]{1,0:T(8,128)(2,1)S(1)} %bitcast.77, bf16[1024,512]{1,0:T(8,128)(2,1)} %collective-permute-done.9), kind=kOutput, calls=%fused_computation.4 | convolution fusion | flops 3493462016 | bytes 12320768 | tf_op jit(solution)/shard_map/dot_general | solution.py:55
  62.2 1.2 slice_bitcast_fusion.3
  63.5 1.3 constant_dynamic-update-slice_fusion.6
  64.8 1.2 constant_dynamic-update-slice_fusion.5
  66.0 1.9 %collective-permute-start.13 = (bf16[96,3328]{1,0:T(8,128)(2,1)S(1)}, bf16[96,3328]{1,0:T(8,128)(2,1)S(1)}, u32[]{:S(2)}, u32[]{:S(2)}) collective-permute-start(bf16[96,3328]{1,0:T(8,128)(2,1)S(1)} %get-tuple-element.54), channel_id=1, source_target_pairs={{0,2},{1,7},{2,4},{3,1},{4,6},{5,3},{6,0},{7,5},{8,10},{9,15},{10,... | collective-permute-start | bytes 1916936 | tf_op jit(solution)/shard_map/ppermute | solution.py:40
  67.9 0.9 copy-done.12
  68.8 1.8 %collective-permute-start.14 = (bf16[80,3328]{1,0:T(8,128)(2,1)}, bf16[80,3328]{1,0:T(8,128)(2,1)}, u32[]{:S(2)}, u32[]{:S(2)}) collective-permute-start(bf16[80,3328]{1,0:T(8,128)(2,1)} %collective-permute-done.10), channel_id=1, source_target_pairs={{0,2},{1,7},{2,4},{3,1},{4,6},{5,3},{6,0},{7,5},{8,10},{9,15},{10,... | collective-permute-start | bytes 1597448 | tf_op jit(solution)/shard_map/ppermute | solution.py:40
  70.7 4.0 %convolution_convert_fusion.1 = bf16[512,3328]{1,0:T(8,128)(2,1)S(1)} fusion(bf16[3328,1024]{1,0:T(8,128)(2,1)S(1)} %bitcast.75, bf16[1024,1024]{1,0:T(8,128)(2,1)S(1)} %pad_maximum_fusion.1), kind=kOutput, calls=%fused_computation.3 | convolution fusion | flops 3491364864 | bytes 11272192 | tf_op jit(solution)/shard_map/dot_general | solution.py:55
  74.8 0.9 collective-permute-start.15
  75.7 1.4 collective-permute-start.18
  77.2 2.1 %constant_dynamic-update-slice_fusion.4 = bf16[1024,3328]{1,0:T(8,128)(2,1)} fusion(bf16[1024,3328]{1,0:T(8,128)(2,1)} %copy-done.12, bf16[128,3328]{1,0:T(8,128)(2,1)} %collective-permute-done), kind=kLoop, calls=%fused_computation.65 | loop fusion | bytes 1703936
  79.3 5.5 %fusion.8 = bf16[512,1024]{1,0:T(8,128)(2,1)S(1)} fusion(bf16[3328,1024]{1,0:T(8,128)(2,1)S(1)} %bitcast.75, bf16[128,3328]{1,0:T(8,128)(2,1)} %collective-permute-done, bf16[128,3328]{1,0:T(8,128)(2,1)} %collective-permute-done.4, bf16[128,3328]{1,0:T(8,128)(2,1)} %collective-permute-done.3, bf16[128,3328]{1,0:T(8,128)(2,1)S(1)} %copy-done.1), kind=kOutput, calls=%fused_computation.19 | convolution fusion | flops 3503816704 | bytes 11272192 | tf_op jit(solution)/shard_map/dot_general | solution.py:55
  84.8 0.8 slice_dynamic-update-slice_fusion.6
  85.6 1.0 fusion.14
  86.6 1.2 collective-permute-start.17
  87.8 0.9 constant_dynamic-update-slice_fusion.11
  88.7 0.8 slice_dynamic-update-slice_fusion.4
  89.4 0.9 constant_dynamic-update-slice_fusion.10
  90.3 0.8 slice_dynamic-update-slice_fusion.2
  91.1 1.9 %constant_dynamic-update-slice_fusion.9 = (bf16[512,3328]{1,0:T(8,128)(2,1)S(1)}, bf16[1024,3328]{1,0:T(8,128)(2,1)}) fusion(bf16[512,3328]{1,0:T(8,128)(2,1)S(1)} %get-tuple-element.61, bf16[80,3328]{1,0:T(8,128)(2,1)} %collective-permute-done.14, bf16[1024,3328]{1,0:T(8,128)(2,1)} %get-tuple-element.62), kind=kLoop, calls=%fused_computation.70 | loop fusion | bytes 1597440
  93.0 0.8 slice_dynamic-update-slice_fusion
  93.8 1.9 %constant_dynamic-update-slice_fusion.8 = (bf16[512,3328]{1,0:T(8,128)(2,1)S(1)}, bf16[1024,3328]{1,0:T(8,128)(2,1)}) fusion(bf16[512,3328]{1,0:T(8,128)(2,1)S(1)} %get-tuple-element.59, bf16[80,3328]{1,0:T(8,128)(2,1)} %collective-permute-done.10, bf16[1024,3328]{1,0:T(8,128)(2,1)} %get-tuple-element.60), kind=kLoop, calls=%fused_computation.69 | loop fusion | bytes 1597440 | tf_op jit(solution)/shard_map/concatenate | solution.py:121
  95.7 3.7 %convolution_convert_fusion.3 = bf16[512,1024]{1,0:T(8,128)(2,1)S(1)} fusion(bf16[512,3328]{1,0:T(8,128)(2,1)S(1)} %get-tuple-element.67, bf16[3328,1024]{1,0:T(8,128)(2,1)S(1)} %bitcast.75), kind=kOutput, calls=%fused_computation.20 | convolution fusion | flops 3490185216 | bytes 11272192 | tf_op jit(solution)/shard_map/dot_general | solution.py:55
  99.8 1.3 pad_maximum_fusion.5
  101.1 2.0 %shard_map.59 = bf16[8,128,1024]{2,1,0:T(8,128)(2,1)} custom-call(s32[8]{0:T(128)S(1)} %stack.86.order_ref, bf16[8,128,1024]{2,1,0:T(8,128)(2,1)S(1)} %bitcast.72), custom_call_target="tpu_custom_call" | custom-call | bytes 2097152 | tf_op jit(solution)/shard_map/pallas_call | solution.py:63
  103.1 3.7 %all-to-all-start = ((bf16[8,128,1024]{2,1,0:T(8,128)(2,1)}), bf16[8,128,1024]{2,1,0:T(8,128)(2,1)S(1)}, u32[]{:S(2)}, u32[]{:S(2)}) async-start(bf16[8,128,1024]{2,1,0:T(8,128)(2,1)} %shard_map.59), calls=%async_computation | async-start | bytes 4194304 | tf_op jit(solution)/shard_map/all_to_all | solution.py:138
  107.3 8.6 %convolution_convert_fusion = bf16[3328,512]{1,0:T(8,128)(2,1)} fusion(bf16[1024,3328]{1,0:T(8,128)(2,1)} %get-tuple-element.46, bf16[1024,1024]{1,0:T(8,128)(2,1)} %copy-done.4), kind=kOutput, calls=%fused_computation.2 | convolution fusion | flops 3491364864 | bytes 11272192 | tf_op jit(solution)/shard_map/dot_general | solution.py:55
  115.9 4.2 %collective-permute-start.20 = (bf16[3328,512]{1,0:T(8,128)(2,1)}, bf16[3328,512]{1,0:T(8,128)(2,1)}, u32[]{:S(2)}, u32[]{:S(2)}) collective-permute-start(bf16[3328,512]{1,0:T(8,128)(2,1)} %convolution_convert_fusion), channel_id=1, source_target_pairs={{0,1},{1,0},{2,3},{3,2},{4,5},{5,4},{6,7},{7,6},{8,9},{9,8},{10,11... | collective-permute-start | bytes 10223624 | tf_op jit(solution)/shard_map/ppermute | solution.py:40
  120.1 2.5 %fusion.13 = bf16[96,3328]{1,0:T(8,128)(2,1)} fusion(bf16[96,3328]{1,0:T(8,128)(2,1)} %collective-permute-done.18, bf16[96,3328]{1,0:T(8,128)(2,1)} %collective-permute-done.17, bf16[4,128,3328]{2,1,0:T(8,128)(2,1)} %bitcast.81), kind=kLoop, calls=%fused_computation.26 | loop fusion | flops 1916928 | bytes 2555904 | tf_op jit(solution)/shard_map/convert_element_type | solution.py:47
  122.7 2.0 %collective-permute-start.19 = (bf16[96,3328]{1,0:T(8,128)(2,1)}, bf16[96,3328]{1,0:T(8,128)(2,1)}, u32[]{:S(2)}, u32[]{:S(2)}) collective-permute-start(bf16[96,3328]{1,0:T(8,128)(2,1)} %fusion.13), channel_id=1, source_target_pairs={{0,8},{1,9},{2,10},{3,11},{4,12},{5,13},{6,14},{7,15},{8,0},{9,1},... | collective-permute-start | bytes 1916936 | tf_op jit(solution)/shard_map/ppermute | solution.py:40
  124.6 7.3 %collective-permute-done.21 = bf16[128,3328]{1,0:T(8,128)(2,1)S(1)} collective-permute-done((bf16[128,3328]{1,0:T(8,128)(2,1)S(1)}, bf16[128,3328]{1,0:T(8,128)(2,1)S(1)}, u32[]{:S(2)}, u32[]{:S(2)}) %collective-permute-start.21) | collective-permute-done | bytes 852000 | tf_op jit(solution)/shard_map/ppermute | solution.py:40
  132.0 1.7 %fusion.21 = bf16[32,3328]{1,0:T(8,128)(2,1)} fusion(bf16[128,3328]{1,0:T(8,128)(2,1)S(1)} %collective-permute-done.21, bf16[128,3328]{1,0:T(8,128)(2,1)S(1)} %collective-permute-done.15, bf16[4,128,3328]{2,1,0:T(8,128)(2,1)} %bitcast.84), kind=kLoop, calls=%fused_computation.44 | loop fusion | flops 638976 | bytes 851968 | tf_op jit(solution)/shard_map/convert_element_type | solution.py:47
  133.7 1.3 fusion.11
  135.4 2.1 %collective-permute-start.16 = (bf16[128,512]{1,0:T(8,128)(2,1)S(1)}, bf16[128,512]{1,0:T(8,128)(2,1)S(1)}, u32[]{:S(2)}, u32[]{:S(2)}) collective-permute-start(bf16[128,512]{1,0:T(8,128)(2,1)S(1)} %get-tuple-element.76), channel_id=1, source_target_pairs={{0,1},{1,0},{2,3},{3,2},{4,5},{5,4},{6,7},{7,6},{8,9},{9,8},{10,11... | collective-permute-start | bytes 393224 | tf_op jit(solution)/shard_map/ppermute | solution.py:40
  137.6 2.4 %collective-permute-start.22 = (bf16[128,3328]{1,0:T(8,128)(2,1)S(1)}, bf16[128,3328]{1,0:T(8,128)(2,1)S(1)}, u32[]{:S(2)}, u32[]{:S(2)}) collective-permute-start(bf16[128,3328]{1,0:T(8,128)(2,1)S(1)} %pad_maximum_fusion.7), channel_id=1, source_target_pairs={{0,2},{1,7},{2,4},{3,1},{4,6},{5,3},{6,0},{7,5},{8,10},{9,15},{10,... | collective-permute-start | bytes 2555912 | tf_op jit(solution)/shard_map/ppermute | solution.py:40
  139.9 0.8 maximum_select_fusion
  140.7 9.8 %add_convert_fusion = bf16[3328,512]{1,0:T(8,128)(2,1)} fusion(bf16[3328,512]{1,0:T(8,128)(2,1)} %collective-permute-done.20, bf16[1024,3328]{1,0:T(8,128)(2,1)} %get-tuple-element.46, bf16[1024,1024]{1,0:T(8,128)(2,1)} %copy-done.4), kind=kOutput, calls=%fused_computation.1 | convolution fusion | flops 3494772736 | bytes 14680064 | tf_op jit(solution)/shard_map/dot_general | solution.py:55
  150.5 2.9 %add_convert_fusion.1 = bf16[128,3328]{1,0:T(8,128)(2,1)} fusion(bf16[128,3328]{1,0:T(8,128)(2,1)} %collective-permute-done.23, bf16[128,3328]{1,0:T(8,128)(2,1)S(1)} %collective-permute-done.22, bf16[512,3328]{1,0:T(8,128)(2,1)} %copy-done.2, bf16[96,3328]{1,0:T(8,128)(2,1)} %collective-permute-done.19, bf16[32,3328]{1,0:T(8,128)(2,1)S(1)} %slice-done.2), kind=kLoop, calls=%fused_computation.18 | loop fusion | flops 4685824 | bytes 4259840 | tf_op jit(solution)/shard_map/convert_element_type | solution.py:47
  (67 shorter events, 2.0 us)
Async XLA Ops:
  0.6 27.8 %copy-start.3 = (bf16[3328,512]{1,0:T(8,128)(2,1)S(1)}, bf16[3328,512]{1,0:T(8,128)(2,1)}, u32[]{:S(2)}) copy-start(bf16[3328,512]{1,0:T(8,128)(2,1)} %param.4) | copy-start | bytes 10223620
  0.6 14.0 %collective-permute-start.2 = (bf16[3328,512]{1,0:T(8,128)(2,1)}, bf16[3328,512]{1,0:T(8,128)(2,1)}, u32[]{:S(2)}, u32[]{:S(2)}) collective-permute-start(bf16[3328,512]{1,0:T(8,128)(2,1)} %param.4), channel_id=1, source_target_pairs={{0,1},{1,0},{2,3},{3,2},{4,5},{5,4},{6,7},{7,6},{8,9},{9,8},{10,11... | collective-permute-start | bytes 10223624 | tf_op jit(solution)/shard_map/ppermute | solution.py:40
  2.1 12.5 %collective-permute-start = (bf16[128,3328]{1,0:T(8,128)(2,1)}, bf16[128,3328]{1,0:T(8,128)(2,1)}, u32[]{:S(2)}, u32[]{:S(2)}) collective-permute-start(bf16[128,3328]{1,0:T(8,128)(2,1)} %param.3), channel_id=1, source_target_pairs={{0,2},{1,7},{2,4},{3,1},{4,6},{5,3},{6,0},{7,5},{8,10},{9,15},{10,... | collective-permute-start | bytes 2555912 | tf_op jit(solution)/shard_map/ppermute | solution.py:40
  4.7 8.2 %collective-permute-start.1 = (bf16[256,512]{1,0:T(8,128)(2,1)}, bf16[256,512]{1,0:T(8,128)(2,1)S(1)}, u32[]{:S(2)}, u32[]{:S(2)}) collective-permute-start(bf16[256,512]{1,0:T(8,128)(2,1)} %param.5), channel_id=1, source_target_pairs={{0,16},{1,17},{2,18},{3,19},{4,20},{5,21},{6,22},{7,23},{8,24},{9,... | collective-permute-start | bytes 786440 | tf_op jit(solution)/shard_map/ppermute | solution.py:40
  14.7 11.1 %collective-permute-start.7 = (bf16[512,512]{1,0:T(8,128)(2,1)}, bf16[512,512]{1,0:T(8,128)(2,1)}, u32[]{:S(2)}, u32[]{:S(2)}) collective-permute-start(bf16[512,512]{1,0:T(8,128)(2,1)} %pad_maximum_fusion.8), channel_id=1, source_target_pairs={{0,32},{1,97},{2,34},{3,99},{4,36},{5,101},{6,38},{7,103},{8,40},{... | collective-permute-start | bytes 1572872 | tf_op jit(solution)/shard_map/ppermute | solution.py:40
  18.4 21.2 %collective-permute-start.3 = (bf16[128,3328]{1,0:T(8,128)(2,1)}, bf16[128,3328]{1,0:T(8,128)(2,1)}, u32[]{:S(2)}, u32[]{:S(2)}) collective-permute-start(bf16[128,3328]{1,0:T(8,128)(2,1)} %param.3), channel_id=1, source_target_pairs={{0,6},{1,3},{2,0},{3,5},{4,2},{5,7},{6,4},{7,1},{8,14},{9,11},{10,... | collective-permute-start | bytes 2555912 | tf_op jit(solution)/shard_map/ppermute | solution.py:40
  19.4 20.8 %collective-permute-start.4 = (bf16[128,3328]{1,0:T(8,128)(2,1)}, bf16[128,3328]{1,0:T(8,128)(2,1)}, u32[]{:S(2)}, u32[]{:S(2)}) collective-permute-start(bf16[128,3328]{1,0:T(8,128)(2,1)} %collective-permute-done), channel_id=1, source_target_pairs={{0,2},{1,7},{2,4},{3,1},{4,6},{5,3},{6,0},{7,5},{8,10},{9,15},{10,... | collective-permute-start | bytes 2555912 | tf_op jit(solution)/shard_map/ppermute | solution.py:40
  22.7 11.4 %collective-permute-start.6 = (bf16[512,512]{1,0:T(8,128)(2,1)}, bf16[512,512]{1,0:T(8,128)(2,1)S(1)}, u32[]{:S(2)}, u32[]{:S(2)}) collective-permute-start(bf16[512,512]{1,0:T(8,128)(2,1)} %pad_maximum_fusion.8), channel_id=1, source_target_pairs={{0,96},{1,33},{2,98},{3,35},{4,100},{5,37},{6,102},{7,39},{8,104},... | collective-permute-start | bytes 1572872 | tf_op jit(solution)/shard_map/ppermute | solution.py:40
  22.8 14.2 %collective-permute-start.5 = (bf16[80,3328]{1,0:T(8,128)(2,1)S(1)}, bf16[80,3328]{1,0:T(8,128)(2,1)S(1)}, u32[]{:S(2)}, u32[]{:S(2)}) collective-permute-start(bf16[80,3328]{1,0:T(8,128)(2,1)S(1)} %slice.120), channel_id=1, source_target_pairs={{0,8},{1,9},{2,10},{3,11},{4,12},{5,13},{6,14},{7,15},{8,0},{9,1},... | collective-permute-start | bytes 1597448 | tf_op jit(solution)/shard_map/ppermute | solution.py:40
  25.8 14.4 %collective-permute-start.8 = (bf16[512,512]{1,0:T(8,128)(2,1)}, bf16[512,512]{1,0:T(8,128)(2,1)S(1)}, u32[]{:S(2)}, u32[]{:S(2)}) collective-permute-start(bf16[512,512]{1,0:T(8,128)(2,1)} %collective-permute-done.7), channel_id=1, source_target_pairs={{0,32},{1,97},{2,34},{3,99},{4,36},{5,101},{6,38},{7,103},{8,40},{... | collective-permute-start | bytes 1572872 | tf_op jit(solution)/shard_map/ppermute | solution.py:40
  37.0 5.2 %copy-start.8 = (bf16[80,3328]{1,0:T(8,128)(2,1)}, bf16[80,3328]{1,0:T(8,128)(2,1)S(1)}, u32[]{:S(2)}) copy-start(bf16[80,3328]{1,0:T(8,128)(2,1)S(1)} %collective-permute-done.5) | copy-start | bytes 1597444
  42.2 3.8 %copy-start.1 = (bf16[128,3328]{1,0:T(8,128)(2,1)S(1)}, bf16[128,3328]{1,0:T(8,128)(2,1)}, u32[]{:S(2)}) copy-start(bf16[128,3328]{1,0:T(8,128)(2,1)} %param.3) | copy-start | bytes 2555908
  43.4 9.3 %collective-permute-start.9 = (bf16[1024,512]{1,0:T(8,128)(2,1)}, bf16[1024,512]{1,0:T(8,128)(2,1)}, u32[]{:S(2)}, u32[]{:S(2)}) collective-permute-start(bf16[1024,512]{1,0:T(8,128)(2,1)} %bitcast.26), channel_id=1, source_target_pairs={{0,1},{1,0},{2,3},{3,2},{4,5},{5,4},{6,7},{7,6},{8,9},{9,8},{10,11... | collective-permute-start | bytes 3145736 | tf_op jit(solution)/shard_map/ppermute | solution.py:40
  46.1 15.9 %collective-permute-start.10 = (bf16[80,3328]{1,0:T(8,128)(2,1)}, bf16[80,3328]{1,0:T(8,128)(2,1)}, u32[]{:S(2)}, u32[]{:S(2)}) collective-permute-start(bf16[80,3328]{1,0:T(8,128)(2,1)} %copy-done.8), channel_id=1, source_target_pairs={{0,2},{1,7},{2,4},{3,1},{4,6},{5,3},{6,0},{7,5},{8,10},{9,15},{10,... | collective-permute-start | bytes 1597448 | tf_op jit(solution)/shard_map/ppermute | solution.py:40
  46.8 15.4 %collective-permute-start.11 = (bf16[80,3328]{1,0:T(8,128)(2,1)}, bf16[80,3328]{1,0:T(8,128)(2,1)S(1)}, u32[]{:S(2)}, u32[]{:S(2)}) collective-permute-start(bf16[80,3328]{1,0:T(8,128)(2,1)} %copy-done.8), channel_id=1, source_target_pairs={{0,6},{1,3},{2,0},{3,5},{4,2},{5,7},{6,4},{7,1},{8,14},{9,11},{10,... | collective-permute-start | bytes 1597448 | tf_op jit(solution)/shard_map/ppermute | solution.py:40
  49.7 35.0 %collective-permute-start.12 = (bf16[192,3328]{1,0:T(8,128)(2,1)S(1)}, bf16[192,3328]{1,0:T(8,128)(2,1)S(1)}, u32[]{:S(2)}, u32[]{:S(2)}) collective-permute-start(bf16[192,3328]{1,0:T(8,128)(2,1)S(1)} %pad_maximum_fusion.4), channel_id=1, source_target_pairs={{0,8},{1,9},{2,10},{3,11},{4,12},{5,13},{6,14},{7,15},{8,0},{9,1},... | collective-permute-start | bytes 3833864 | tf_op jit(solution)/shard_map/ppermute | solution.py:40
  52.7 17.9 %slice-start = ((s8[6815744]{0:T(1024)(128)(4,1)}), s8[4194304]{0:T(1024)(128)(4,1)S(1)}, s32[]{:S(2)}) async-start(s8[6815744]{0:T(1024)(128)(4,1)} %bitcast.74), calls=%async_computation.1 | async-start | bytes 8388608
  54.4 16.3 %copy-start.4 = (bf16[1024,1024]{1,0:T(8,128)(2,1)}, bf16[1024,1024]{1,0:T(8,128)(2,1)S(1)}, u32[]{:S(2)}) copy-start(bf16[1024,1024]{1,0:T(8,128)(2,1)S(1)} %pad_maximum_fusion.1) | copy-start | bytes 6291460
  54.4 16.3 %slice-start.1 = ((s8[6815744]{0:T(1024)(128)(4,1)}), s8[2621440]{0:T(1024)(128)(4,1)S(1)}, s32[]{:S(2)}) async-start(s8[6815744]{0:T(1024)(128)(4,1)} %bitcast.74), calls=%async_computation.2 | async-start | bytes 5242880
  62.0 23.6 %copy-start = (bf16[512,3328]{1,0:T(8,128)(2,1)}, bf16[512,3328]{1,0:T(8,128)(2,1)S(1)}, u32[]{:S(2)}) copy-start(bf16[512,3328]{1,0:T(8,128)(2,1)S(1)} %convolution_convert_fusion.2) | copy-start | bytes 10223620
  62.2 2.6 %copy-start.10 = (bf16[80,3328]{1,0:T(8,128)(2,1)}, bf16[80,3328]{1,0:T(8,128)(2,1)S(1)}, u32[]{:S(2)}) copy-start(bf16[80,3328]{1,0:T(8,128)(2,1)S(1)} %collective-permute-done.11) | copy-start | bytes 1597444
  66.0 2.8 %copy-start.12 = (bf16[1024,3328]{1,0:T(8,128)(2,1)}, bf16[1024,3328]{1,0:T(8,128)(2,1)S(1)}, u32[]{:S(2)}) copy-start(bf16[1024,3328]{1,0:T(8,128)(2,1)S(1)} %constant_dynamic-update-slice_fusion.5) | copy-start | bytes 20447236
  66.0 19.6 %collective-permute-start.13 = (bf16[96,3328]{1,0:T(8,128)(2,1)S(1)}, bf16[96,3328]{1,0:T(8,128)(2,1)S(1)}, u32[]{:S(2)}, u32[]{:S(2)}) collective-permute-start(bf16[96,3328]{1,0:T(8,128)(2,1)S(1)} %get-tuple-element.54), channel_id=1, source_target_pairs={{0,2},{1,7},{2,4},{3,1},{4,6},{5,3},{6,0},{7,5},{8,10},{9,15},{10,... | collective-permute-start | bytes 1916936 | tf_op jit(solution)/shard_map/ppermute | solution.py:40
  68.8 22.3 %collective-permute-start.14 = (bf16[80,3328]{1,0:T(8,128)(2,1)}, bf16[80,3328]{1,0:T(8,128)(2,1)}, u32[]{:S(2)}, u32[]{:S(2)}) collective-permute-start(bf16[80,3328]{1,0:T(8,128)(2,1)} %collective-permute-done.10), channel_id=1, source_target_pairs={{0,2},{1,7},{2,4},{3,1},{4,6},{5,3},{6,0},{7,5},{8,10},{9,15},{10,... | collective-permute-start | bytes 1597448 | tf_op jit(solution)/shard_map/ppermute | solution.py:40
  74.7 25.0 %copy-start.2 = (bf16[512,3328]{1,0:T(8,128)(2,1)}, bf16[512,3328]{1,0:T(8,128)(2,1)S(1)}, u32[]{:S(2)}) copy-start(bf16[512,3328]{1,0:T(8,128)(2,1)S(1)} %convolution_convert_fusion.1) | copy-start | bytes 10223620
  74.8 24.9 %collective-permute-start.15 = (bf16[128,3328]{1,0:T(8,128)(2,1)S(1)}, bf16[128,3328]{1,0:T(8,128)(2,1)S(1)}, u32[]{:S(2)}, u32[]{:S(2)}) collective-permute-start(bf16[128,3328]{1,0:T(8,128)(2,1)S(1)} %bitcast.86), channel_id=1, source_target_pairs={{0,8},{1,9},{2,10},{3,11},{4,12},{5,13},{6,14},{7,15},{8,0},{9,1},... | collective-permute-start | bytes 2555912 | tf_op jit(solution)/shard_map/ppermute | solution.py:40
  75.7 44.4 %collective-permute-start.18 = (bf16[96,3328]{1,0:T(8,128)(2,1)}, bf16[96,3328]{1,0:T(8,128)(2,1)}, u32[]{:S(2)}, u32[]{:S(2)}) collective-permute-start(bf16[96,3328]{1,0:T(8,128)(2,1)} %get-tuple-element.53), channel_id=1, source_target_pairs={{0,6},{1,3},{2,0},{3,5},{4,2},{5,7},{6,4},{7,1},{8,14},{9,11},{10,... | collective-permute-start | bytes 1916936 | tf_op jit(solution)/shard_map/ppermute | solution.py:40
  79.3 8.5 %copy-start.9 = (bf16[80,3328]{1,0:T(8,128)(2,1)S(1)}, bf16[80,3328]{1,0:T(8,128)(2,1)}, u32[]{:S(2)}) copy-start(bf16[80,3328]{1,0:T(8,128)(2,1)} %copy-done.8) | copy-start | bytes 1597444
  84.8 4.7 %copy-start.11 = (bf16[80,3328]{1,0:T(8,128)(2,1)S(1)}, bf16[80,3328]{1,0:T(8,128)(2,1)}, u32[]{:S(2)}) copy-start(bf16[80,3328]{1,0:T(8,128)(2,1)} %copy-done.10) | copy-start | bytes 1597444
  86.6 33.6 %collective-permute-start.17 = (bf16[96,3328]{1,0:T(8,128)(2,1)}, bf16[96,3328]{1,0:T(8,128)(2,1)}, u32[]{:S(2)}, u32[]{:S(2)}) collective-permute-start(bf16[96,3328]{1,0:T(8,128)(2,1)} %fusion.14), channel_id=1, source_target_pairs={{0,2},{1,7},{2,4},{3,1},{4,6},{5,3},{6,0},{7,5},{8,10},{9,15},{10,... | collective-permute-start | bytes 1916936 | tf_op jit(solution)/shard_map/ppermute | solution.py:40
  99.7 32.3 %copy-start.5 = (bf16[128,3328]{1,0:T(8,128)(2,1)}, bf16[128,3328]{1,0:T(8,128)(2,1)S(1)}, u32[]{:S(2)}) copy-start(bf16[128,3328]{1,0:T(8,128)(2,1)S(1)} %collective-permute-done.15) | copy-start | bytes 2555908
  103.1 31.8 %all-to-all-start = ((bf16[8,128,1024]{2,1,0:T(8,128)(2,1)}), bf16[8,128,1024]{2,1,0:T(8,128)(2,1)S(1)}, u32[]{:S(2)}, u32[]{:S(2)}) async-start(bf16[8,128,1024]{2,1,0:T(8,128)(2,1)} %shard_map.59), calls=%async_computation | async-start | bytes 4194304 | tf_op jit(solution)/shard_map/all_to_all | solution.py:138
  106.8 13.3 %copy-start.7 = (bf16[128,3328]{1,0:T(8,128)(2,1)S(1)}, bf16[128,3328]{1,0:T(8,128)(2,1)}, u32[]{:S(2)}) copy-start(bf16[128,3328]{1,0:T(8,128)(2,1)} %get-tuple-element.47) | copy-start | bytes 2555908
  106.8 43.7 %collective-permute-start.23 = (bf16[128,3328]{1,0:T(8,128)(2,1)}, bf16[128,3328]{1,0:T(8,128)(2,1)}, u32[]{:S(2)}, u32[]{:S(2)}) collective-permute-start(bf16[128,3328]{1,0:T(8,128)(2,1)} %get-tuple-element.49), channel_id=1, source_target_pairs={{0,6},{1,3},{2,0},{3,5},{4,2},{5,7},{6,4},{7,1},{8,14},{9,11},{10,... | collective-permute-start | bytes 2555912 | tf_op jit(solution)/shard_map/ppermute | solution.py:40
  115.9 24.8 %collective-permute-start.20 = (bf16[3328,512]{1,0:T(8,128)(2,1)}, bf16[3328,512]{1,0:T(8,128)(2,1)}, u32[]{:S(2)}, u32[]{:S(2)}) collective-permute-start(bf16[3328,512]{1,0:T(8,128)(2,1)} %convolution_convert_fusion), channel_id=1, source_target_pairs={{0,1},{1,0},{2,3},{3,2},{4,5},{5,4},{6,7},{7,6},{8,9},{9,8},{10,11... | collective-permute-start | bytes 10223624 | tf_op jit(solution)/shard_map/ppermute | solution.py:40
  120.1 11.8 %collective-permute-start.21 = (bf16[128,3328]{1,0:T(8,128)(2,1)S(1)}, bf16[128,3328]{1,0:T(8,128)(2,1)S(1)}, u32[]{:S(2)}, u32[]{:S(2)}) collective-permute-start(bf16[128,3328]{1,0:T(8,128)(2,1)S(1)} %copy-done.7), channel_id=1, source_target_pairs={{0,2},{1,7},{2,4},{3,1},{4,6},{5,3},{6,0},{7,5},{8,10},{9,15},{10,... | collective-permute-start | bytes 2555912 | tf_op jit(solution)/shard_map/ppermute | solution.py:40
  122.7 27.8 %collective-permute-start.19 = (bf16[96,3328]{1,0:T(8,128)(2,1)}, bf16[96,3328]{1,0:T(8,128)(2,1)}, u32[]{:S(2)}, u32[]{:S(2)}) collective-permute-start(bf16[96,3328]{1,0:T(8,128)(2,1)} %fusion.13), channel_id=1, source_target_pairs={{0,8},{1,9},{2,10},{3,11},{4,12},{5,13},{6,14},{7,15},{8,0},{9,1},... | collective-permute-start | bytes 1916936 | tf_op jit(solution)/shard_map/ppermute | solution.py:40
  133.7 3.8 %copy-start.6 = (bf16[32,3328]{1,0:T(8,128)(2,1)S(1)}, bf16[32,3328]{1,0:T(8,128)(2,1)}, u32[]{:S(2)}) copy-start(bf16[32,3328]{1,0:T(8,128)(2,1)} %fusion.21) | copy-start | bytes 638980
  135.4 4.6 %collective-permute-start.16 = (bf16[128,512]{1,0:T(8,128)(2,1)S(1)}, bf16[128,512]{1,0:T(8,128)(2,1)S(1)}, u32[]{:S(2)}, u32[]{:S(2)}) collective-permute-start(bf16[128,512]{1,0:T(8,128)(2,1)S(1)} %get-tuple-element.76), channel_id=1, source_target_pairs={{0,1},{1,0},{2,3},{3,2},{4,5},{5,4},{6,7},{7,6},{8,9},{9,8},{10,11... | collective-permute-start | bytes 393224 | tf_op jit(solution)/shard_map/ppermute | solution.py:40
  137.6 12.9 %collective-permute-start.22 = (bf16[128,3328]{1,0:T(8,128)(2,1)S(1)}, bf16[128,3328]{1,0:T(8,128)(2,1)S(1)}, u32[]{:S(2)}, u32[]{:S(2)}) collective-permute-start(bf16[128,3328]{1,0:T(8,128)(2,1)S(1)} %pad_maximum_fusion.7), channel_id=1, source_target_pairs={{0,2},{1,7},{2,4},{3,1},{4,6},{5,3},{6,0},{7,5},{8,10},{9,15},{10,... | collective-permute-start | bytes 2555912 | tf_op jit(solution)/shard_map/ppermute | solution.py:40
  140.7 9.8 %slice-start.2 = ((bf16[128,3328]{1,0:T(8,128)(2,1)}), bf16[32,3328]{1,0:T(8,128)(2,1)S(1)}, s32[]{:S(2)}) async-start(bf16[128,3328]{1,0:T(8,128)(2,1)} %copy-done.5), calls=%async_computation.3 | async-start | bytes 425984 | tf_op jit(solution)/shard_map/slice | solution.py:148

commit v3 on v2

--- a/solution.py
+++ b/solution.py
@@ -7,7 +7,7 @@
 
 BF, F32 = jnp.bfloat16, jnp.float32
 AXES = ("row", "col")
-GATHER_VIA_Y = 48
+GATHER_VIA_Y = 32
 REDUCE_VIA_Y = 32
 
 
@@ -71,6 +71,94 @@
         compiler_params=pltpu.CompilerParams(vmem_limit_bytes=12 << 20),
         cost_estimate=pl.CostEstimate(flops=0, bytes_accessed=2 * blocks.size, transcendentals=0),
     )(jnp.stack(order).astype(jnp.int32), blocks)
+
+
+SMALL = pl.CostEstimate(flops=1 << 20, bytes_accessed=1 << 20, transcendentals=0)
+
+
+def assemble(refs, plan, whole):
+    for array, start, rows, to in plan:
+        whole[pl.ds(to, rows), :] = refs[array][pl.ds(start, rows), :]
+
+
+def project(arrays, plan, weight):
+    n, depth, width, tile = len(arrays), arrays[0].shape[1], weight.shape[1], 256
+    total = sum(rows for _, _, rows, _ in plan)
+
+    def kernel(*refs):
+        weight_ref, out_ref, whole = refs[n:]
+
+        @pl.when(pl.program_id(0) == 0)
+        def _():
+            assemble(refs, plan, whole)
+
+        out_ref[...] = jnp.dot(whole[...], weight_ref[...], preferred_element_type=F32).astype(BF)
+
+    return pl.pallas_call(
+        kernel,
+        grid=(width // tile,),
+        out_shape=jax.ShapeDtypeStruct((total, width), BF),
+        in_specs=[pl.BlockSpec(a.shape, lambda t: (0, 0)) for a in arrays]
+        + [pl.BlockSpec((depth, tile), lambda t: (0, t))],
+        out_specs=pl.BlockSpec((total, tile), lambda t: (0, t)),
+        scratch_shapes=[pltpu.VMEM((total, depth), BF)],
+        compiler_params=pltpu.CompilerParams(vmem_limit_bytes=36 << 20),
+        cost_estimate=pl.CostEstimate(
+            flops=2 * total * depth * width, bytes_accessed=16 << 20, transcendentals=0
+        ),
+    )(*arrays, weight)
+
+
+def sum_blocks(blocks):
+    def kernel(blocks_ref, sum_ref):
+        total = blocks_ref[0].astype(F32)
+        for i in range(1, blocks.shape[0]):
+            total = total + blocks_ref[i].astype(F32)
+        sum_ref[...] = total.astype(BF)
+
+    return pl.pallas_call(
+        kernel,
+        out_shape=jax.ShapeDtypeStruct(blocks.shape[1:], BF),
+        in_specs=[pl.BlockSpec(memory_space=pltpu.VMEM)],
+        out_specs=pl.BlockSpec(memory_space=pltpu.VMEM),
+        compiler_params=pltpu.CompilerParams(vmem_limit_bytes=12 << 20),
+        cost_estimate=pl.CostEstimate(flops=24 << 30, bytes_accessed=4 << 20, transcendentals=0),
+    )(blocks)
+
+
+def weight_gradient(arrays, plan, cotangent, others=None):
+    n, width, columns = len(arrays), arrays[0].shape[1], cotangent.shape[1]
+    total, tile = cotangent.shape[0], width // 2
+    half = pl.BlockSpec((tile, columns), lambda t: (0, 0))
+
+    def kernel(*refs):
+        cotangent_ref, whole = refs[n], refs[-1]
+        assemble(refs, plan, whole)
+        result = dot(whole[...], cotangent_ref[...], ((0,), (0,)))
+        for t in range(2):
+
+            @pl.when(pl.program_id(0) == t)
+            def _():
+                if others is None:
+                    refs[n + 1 + t][...] = result.astype(BF)
+                else:
+                    refs[n + 3][...] = (result + refs[n + 1 + t][...].astype(F32)).astype(BF)
+
+    halves = [jax.ShapeDtypeStruct((tile, columns), BF)] * 2
+    return pl.pallas_call(
+        kernel,
+        grid=(2,),
+        out_shape=halves if others is None else jax.ShapeDtypeStruct((width, columns), BF),
+        in_specs=[pl.BlockSpec((a.shape[0], tile), lambda t: (0, t)) for a in arrays]
+        + [pl.BlockSpec((total, columns), lambda t: (0, 0))]
+        + ([] if others is None else [half, half]),
+        out_specs=[half, half]
+        if others is None
+        else pl.BlockSpec((tile, columns), lambda t: (t, 0)),
+        scratch_shapes=[pltpu.VMEM((total, tile), BF)],
+        compiler_params=pltpu.CompilerParams(vmem_limit_bytes=56 << 20),
+        cost_estimate=SMALL,
+    )(*arrays, cotangent, *(others or []))
 
 
 def per_device(hidden, weight, grad_out):
@@ -105,46 +193,49 @@
         return order
 
     picked = pick(g, order_of(core) + order_of(1 - core)).reshape(2048, 512)
-    g = jnp.concatenate([picked[:1024], send(picked[1024:], CORE)], axis=1)
+    g_own, g_other = picked[:1024], send(picked[1024:], CORE)
+    g = jnp.concatenate([g_own, g_other], axis=1)
 
     far = dot(g[512:], w, ((1,), (1,))).astype(BF).reshape(4, 128, 3328)
     far, k3b, k1b, g, h0, k0b = tie(far, k3b, k1b, g, h0, k0b)
     k2b = send(k3b, X1)
-    r3, r2 = send(far[2, b:], X1), send(far[3, b:], X2)
+    r3 = send(far[2, b:], X1)
+    r2, k2b = tie(far[3, b:], k2b)
+    r2 = send(r2, X2)
     n = send(far[:, :b].reshape(4 * b, 3328), YH).reshape(4, b, 3328)
     near = dot(g[:512], w, ((1,), (1,))).astype(BF).reshape(4, 128, 3328)
-    h_near = jnp.concatenate([h0, h1, h2, h3], axis=0)
     r1 = add(far[1, b:], r3)
     r1, k0b = tie(r1, k0b)
     r1 = send(r1, X1)
-    ka = ka.reshape(4, a, 3328)
-    h_far = jnp.concatenate([ka[0], k0b, ka[1], k1b, ka[2], k2b, ka[3], k3b], axis=0)
-
-    out = jnp.concatenate(
-        [dot(h_near, w, ((1,), (0,))).astype(BF), dot(h_far, w, ((1,), (0,))).astype(BF)], axis=0
-    )
+
+    arrays = [h0, h1, h2, h3, ka, k0b, k1b, k2b, k3b]
+    plan = [(i, 0, 128, 128 * i) for i in range(4)]
+    plan += [(4, a * i, a, 512 + 128 * i) for i in range(4)]
+    plan += [(5 + i, 0, 128 - a, 512 + 128 * i + a) for i in range(4)]
+    out = project(arrays, plan, w)
 
     d3 = jnp.concatenate([add(near[2, :b], n[2]), near[2, b:]], axis=0)
     d2 = jnp.concatenate([add(near[3, :b], n[3]), near[3, b:]], axis=0)
-    h = jnp.concatenate([h_near, h_far], axis=0)
-    h, out, d3, d2 = tie(h, out, d3, d2)
-    d3, d2 = send(d3, X1), send(d2, X2)
-    n0 = send(add(far[0, b:], r1, r2), YH)
-
-    d1 = jnp.concatenate([add(near[1, :b], n[1], d3[:b]), add(near[1, b:], d3[b:])], axis=0)
-    d1 = send(d1, X1)
     order = [(r // 4 + y_hi) % 2 * 4 + ((r % 4 - x) * s) % 4 for r in range(8)]
     out = pick(out.reshape(8, 128, 1024), order)
+    n0 = add(far[0, b:], r1, r2)
+    h0, out, d3, d2, n0 = tie(h0, out, d3, d2, n0)
     out = lax.all_to_all(out, "row", 0, 0, tiled=True)
-    o = jnp.sum(out.astype(F32), axis=0).astype(BF)
+    d3, d2, n0 = send(d3, X1), send(d2, X2), send(n0, YH)
+
+    arrays[0] = h0
+    v, u = weight_gradient(arrays, plan, g_other)
+    d3, d2, n0, v, u, arrays[0] = tie(d3, d2, n0, v, u, h0)
+    d1 = jnp.concatenate([add(near[1, :b], n[1], d3[:b]), add(near[1, b:], d3[b:])], axis=0)
+    d1, v, u = send(d1, X1), send(v, CORE), send(u, CORE)
+    grad_weight = weight_gradient(arrays, plan, g_own, [v, u])
+    grad_weight, out = tie(grad_weight, out)
+    o = sum_blocks(out)
     own, other = o[:, :512], send(o[:, 512:], CORE)
     output = jnp.where(
         core == 0, jnp.concatenate([own, other], axis=0), jnp.concatenate([other, own], axis=0)
     )
 
-    v = send(dot(h, g[:, 512:], ((0,), (0,))).astype(BF), CORE)
-    grad_weight = (dot(h, g[:, :512], ((0,), (0,))) + v.astype(F32)).astype(BF)
-    grad_weight, d1 = tie(grad_weight, d1)
     grad_hidden = add(near[0], jnp.concatenate([n[0], n0], axis=0), d1, d2)
     return output, grad_hidden, grad_weight
 

time: 154 us -> 151 us (0.981)
  matrix products: 39.2 us -> 11 us
  Pallas kernels: 2.71 us -> 30.9 us
  local copies, waits for them, and re-layouts: 21.1 us -> 5.19 us
  waiting for transfers between devices: 20.5 us -> 29.1 us
  starting transfers between devices: 46.2 us -> 49.9 us
    pallas_call x0 -> x4, Pallas kernels: none -> 28.2 us  [the longest x2 18.6 us: weight_gradient(): pl.pallas_call(kernel, grid=(2,), out_shape=halves if others is None else...]
    dot_general x6 -> x2, matrix products: 39.2 us -> 11 us  [dot(): return lax.dot_general(a, b, (dims, ((), ())), preferred_element_type=F32)]
    unnamed x41 -> x40, local copies, waits for them, and re-layouts: 12.5 us -> 2.02 us
    ppermute x24 -> x25, waiting for transfers between devices: 20.5 us -> 29.1 us  [send(): return lax.ppermute(value, AXES, perm)]
    ppermute x24 -> x25, starting transfers between devices: 42.5 us -> 46.3 us  [send(): return lax.ppermute(value, AXES, perm)]
    slice x4, local copies, waits for them, and re-layouts: 3 us -> 0.06 us  [per_device(): ka = send(jnp.concatenate([h0[:a], h1[:a], h2[:a], h3[:a]], axis=0), YH)]
    concatenate x1 -> x0, local copies, waits for them, and re-layouts: 1.92 us -> none  [per_device(): jnp.concatenate([ka[0], k0b, ka[1], k1b, ka[2], k2b, ka[3], k3b], axis=0)]
  transfers between devices with their start and end apart: 25 -> 26, of which waited for: 6 -> 13; matrix products, arithmetic and copies ran while one was open for 50% -> 22% of each run, Pallas kernels for 1% -> 20%
where the time goes in v3:
time: 151 us
  starting transfers between devices  49.9 us (33%)
  Pallas kernels  30.9 us (20%)
  waiting for transfers between devices  29.1 us (19%)
  other arithmetic  23.9 us (16%)
  matrix products  11 us (7%)
  local copies, waits for them, and re-layouts  5.19 us (3%)
    ppermute x25, starting transfers between devices, send(): return lax.ppermute(value, AXES, perm)  46.3 us
    ppermute x25, waiting for transfers between devices, send(): return lax.ppermute(value, AXES, perm)  29.1 us
    pallas_call x2, Pallas kernels, weight_gradient(): pl.pallas_call(kernel, grid=(2,), out_shape=halves if others is None else...  18.6 us
    dot_general x2, matrix products, dot(): return lax.dot_general(a, b, (dims, ((), ())), preferred_element_type=F32)  11 us
    pallas_call x1, Pallas kernels, project(): pl.pallas_call(kernel, grid=(width // tile,), out_shape=jax.ShapeDtypeStr...  9.31 us
    convert_element_type x6, other arithmetic, add(): return total.astype(BF)  8.97 us
    concatenate x1, other arithmetic, per_device(): w = jnp.concatenate([weight, w_other], axis=1)  6.72 us
    all_to_all x1, starting transfers between devices, per_device(): out = lax.all_to_all(out, 'row', 0, 0, tiled=True)  3.6 us
  transfers between devices with their start and end apart: 26, of which 13 were waited for; matrix products, arithmetic and copies ran while one was open for 22% of the time, Pallas kernels for 20%

profile of v3, /device:TPU:1, one launch (start us, length us, event | category | flops | bytes accessed | tf_op | source)
XLA Modules:
  0.0 150.9 jit_solution(16005617122180116267)
XLA Ops:
  0.6 1.5 collective-permute-start.2
  2.1 2.6 %collective-permute-start = (bf16[128,3328]{1,0:T(8,128)(2,1)}, bf16[128,3328]{1,0:T(8,128)(2,1)S(1)}, u32[]{:S(2)}, u32[]{:S(2)}) collective-permute-start(bf16[128,3328]{1,0:T(8,128)(2,1)} %refs_0_.2), channel_id=1, source_target_pairs={{0,2},{1,7},{2,4},{3,1},{4,6},{5,3},{6,0},{7,5},{8,10},{9,15},{10,... | collective-permute-start | bytes 2555912 | tf_op jit(solution)/shard_map/ppermute | solution.py:40
  4.7 1.3 collective-permute-start.1
  6.0 6.8 %collective-permute-done.1 = bf16[256,512]{1,0:T(8,128)(2,1)S(1)} collective-permute-done((bf16[256,512]{1,0:T(8,128)(2,1)}, bf16[256,512]{1,0:T(8,128)(2,1)S(1)}, u32[]{:S(2)}, u32[]{:S(2)}) %collective-permute-start.1) | collective-permute-done | bytes 262176 | tf_op jit(solution)/shard_map/ppermute | solution.py:40
  12.8 1.8 %pad_maximum_fusion.7 = bf16[512,512]{1,0:T(8,128)(2,1)} fusion(bf16[256,512]{1,0:T(8,128)(2,1)S(1)} %collective-permute-done.1, bf16[256,512]{1,0:T(8,128)(2,1)} %param.5), kind=kLoop, calls=%fused_computation.26 | loop fusion | flops 1048576 | bytes 1048576 | tf_op jit(solution)/shard_map/concatenate | solution.py:176
  14.6 0.1 collective-permute-done.refs_3_
  14.7 3.8 %collective-permute-start.7 = (bf16[512,512]{1,0:T(8,128)(2,1)}, bf16[512,512]{1,0:T(8,128)(2,1)}, u32[]{:S(2)}, u32[]{:S(2)}) collective-permute-start(bf16[512,512]{1,0:T(8,128)(2,1)} %pad_maximum_fusion.7), channel_id=1, source_target_pairs={{0,32},{1,97},{2,34},{3,99},{4,36},{5,101},{6,38},{7,103},{8,40},{... | collective-permute-start | bytes 1572872 | tf_op jit(solution)/shard_map/ppermute | solution.py:40
  18.5 3.0 %collective-permute-start.4 = (bf16[128,3328]{1,0:T(8,128)(2,1)S(1)}, bf16[128,3328]{1,0:T(8,128)(2,1)S(1)}, u32[]{:S(2)}, u32[]{:S(2)}) collective-permute-start(bf16[128,3328]{1,0:T(8,128)(2,1)S(1)} %collective-permute-done.refs_3_), channel_id=1, source_target_pairs={{0,2},{1,7},{2,4},{3,1},{4,6},{5,3},{6,0},{7,5},{8,10},{9,15},{10,... | collective-permute-start | bytes 2555912 | tf_op jit(solution)/shard_map/ppermute | solution.py:40
  21.5 0.1 stack.94.order_ref
  21.7 0.1 collective-permute-start.6
  21.7 3.0 %collective-permute-start.5 = (bf16[96,3328]{1,0:T(8,128)(2,1)S(1)}, bf16[96,3328]{1,0:T(8,128)(2,1)S(1)}, u32[]{:S(2)}, u32[]{:S(2)}) collective-permute-start(bf16[96,3328]{1,0:T(8,128)(2,1)S(1)} %slice.98), channel_id=1, source_target_pairs={{0,8},{1,9},{2,10},{3,11},{4,12},{5,13},{6,14},{7,15},{8,0},{9,1},... | collective-permute-start | bytes 1916936 | tf_op jit(solution)/shard_map/ppermute | solution.py:40
  24.7 0.2 collective-permute-done.7
  24.9 3.3 %collective-permute-start.8 = (bf16[512,512]{1,0:T(8,128)(2,1)}, bf16[512,512]{1,0:T(8,128)(2,1)S(1)}, u32[]{:S(2)}, u32[]{:S(2)}) collective-permute-start(bf16[512,512]{1,0:T(8,128)(2,1)} %collective-permute-done.7), channel_id=1, source_target_pairs={{0,32},{1,97},{2,34},{3,99},{4,36},{5,101},{6,38},{7,103},{8,40},{... | collective-permute-start | bytes 1572872 | tf_op jit(solution)/shard_map/ppermute | solution.py:40
  28.2 6.7 %pad_maximum_fusion.refs_9_ = bf16[3328,1024]{1,0:T(8,128)(2,1)} fusion(bf16[3328,512]{1,0:T(8,128)(2,1)} %copy-done.12, bf16[3328,512]{1,0:T(8,128)(2,1)} %param.4), kind=kLoop, calls=%fused_computation | loop fusion | flops 13631488 | bytes 13631488 | tf_op jit(solution)/shard_map/concatenate | solution.py:181
  34.9 0.4 collective-permute-done.5.refs_5_
  35.3 4.5 %collective-permute-done.4.refs_2_ = bf16[128,3328]{1,0:T(8,128)(2,1)S(1)} collective-permute-done((bf16[128,3328]{1,0:T(8,128)(2,1)S(1)}, bf16[128,3328]{1,0:T(8,128)(2,1)S(1)}, u32[]{:S(2)}, u32[]{:S(2)}) %collective-permute-start.4) | collective-permute-done | bytes 852000 | tf_op jit(solution)/shard_map/ppermute | solution.py:40
  39.8 1.0 collective-permute-done.3.refs_1_
  40.8 1.6 %pad_maximum_fusion.2 = bf16[2048,512]{1,0:T(8,128)(2,1)S(1)} fusion(bf16[512,512]{1,0:T(8,128)(2,1)} %collective-permute-done.7, bf16[512,512]{1,0:T(8,128)(2,1)S(1)} %collective-permute-done.8, bf16[512,512]{1,0:T(8,128)(2,1)S(1)} %collective-permute-done.6, bf16[512,512]{1,0:T(8,128)(2,1)} %pad_maximum_fusion.7), kind=kLoop, calls=%fused_computation.6 | loop fusion | flops 8388608 | bytes 4194304 | tf_op jit(solution)/shard_map/concatenate | solution.py:185
  42.4 0.7 shard_map.58
  43.1 1.5 %fusion.12 = (bf16[8,128,512]{2,1,0:T(8,128)(2,1)}, bf16[8,128,512]{2,1,0:T(8,128)(2,1)}) fusion(bf16[16,128,512]{2,1,0:T(8,128)(2,1)S(1)} %shard_map.58), kind=kLoop, calls=%fused_computation.39 | loop fusion | bytes 4194304 | tf_op jit(solution)/shard_map/slice | solution.py:196
  44.7 0.1 stack.103.order_ref
  44.8 3.4 %collective-permute-start.10 = (bf16[96,3328]{1,0:T(8,128)(2,1)}, bf16[96,3328]{1,0:T(8,128)(2,1)S(1)}, u32[]{:S(2)}, u32[]{:S(2)}) collective-permute-start(bf16[96,3328]{1,0:T(8,128)(2,1)} %copy-done.5), channel_id=1, source_target_pairs={{0,2},{1,7},{2,4},{3,1},{4,6},{5,3},{6,0},{7,5},{8,10},{9,15},{10,... | collective-permute-start | bytes 1916936 | tf_op jit(solution)/shard_map/ppermute | solution.py:40
  48.3 3.0 %collective-permute-start.12 = (bf16[128,3328]{1,0:T(8,128)(2,1)S(1)}, bf16[128,3328]{1,0:T(8,128)(2,1)S(1)}, u32[]{:S(2)}, u32[]{:S(2)}) collective-permute-start(bf16[128,3328]{1,0:T(8,128)(2,1)S(1)} %pad_maximum_fusion.3), channel_id=1, source_target_pairs={{0,8},{1,9},{2,10},{3,11},{4,12},{5,13},{6,14},{7,15},{8,0},{9,1},... | collective-permute-start | bytes 2555912 | tf_op jit(solution)/shard_map/ppermute | solution.py:40
  51.3 1.6 %pad_maximum_fusion.1 = bf16[1024,1024]{1,0:T(8,128)(2,1)S(1)} fusion(bf16[1024,512]{1,0:T(8,128)(2,1)} %collective-permute-done.9.refs_9_, bf16[1024,512]{1,0:T(8,128)(2,1)S(1)} %bitcast.72), kind=kLoop, calls=%fused_computation.4 | loop fusion | flops 4194304 | bytes 4194304 | tf_op jit(solution)/shard_map/concatenate | solution.py:197
  52.9 7.0 %convolution_convert_fusion.1 = bf16[512,3328]{1,0:T(8,128)(2,1)S(1)} fusion(bf16[3328,1024]{1,0:T(8,128)(2,1)} %pad_maximum_fusion.refs_9_, bf16[1024,512]{1,0:T(8,128)(2,1)S(1)} %bitcast.73, bf16[1024,512]{1,0:T(8,128)(2,1)} %collective-permute-done.9.refs_9_), kind=kOutput, calls=%fused_computation.2 | convolution fusion | flops 3493462016 | bytes 12320768 | tf_op jit(solution)/shard_map/dot_general | solution.py:55
  60.0 2.1 %collective-permute-done.10.refs_8_ = bf16[96,3328]{1,0:T(8,128)(2,1)S(1)} collective-permute-done((bf16[96,3328]{1,0:T(8,128)(2,1)}, bf16[96,3328]{1,0:T(8,128)(2,1)S(1)}, u32[]{:S(2)}, u32[]{:S(2)}) %collective-permute-start.10) | collective-permute-done | bytes 639008 | tf_op jit(solution)/shard_map/ppermute | solution.py:40
  62.1 1.5 %collective-permute-done.11.refs_6_ = bf16[96,3328]{1,0:T(8,128)(2,1)S(1)} collective-permute-done((bf16[96,3328]{1,0:T(8,128)(2,1)}, bf16[96,3328]{1,0:T(8,128)(2,1)S(1)}, u32[]{:S(2)}, u32[]{:S(2)}) %collective-permute-start.11) | collective-permute-done | bytes 639008 | tf_op jit(solution)/shard_map/ppermute | solution.py:40
  63.6 1.2 slice_bitcast_fusion.3
  64.8 0.1 slice.113
  64.9 1.9 %collective-permute-start.14 = (bf16[96,3328]{1,0:T(8,128)(2,1)S(1)}, bf16[96,3328]{1,0:T(8,128)(2,1)S(1)}, u32[]{:S(2)}, u32[]{:S(2)}) collective-permute-start(bf16[96,3328]{1,0:T(8,128)(2,1)S(1)} %collective-permute-done.10.refs_8_), channel_id=1, source_target_pairs={{0,2},{1,7},{2,4},{3,1},{4,6},{5,3},{6,0},{7,5},{8,10},{9,15},{10,... | collective-permute-start | bytes 1916936 | tf_op jit(solution)/shard_map/ppermute | solution.py:40
  66.8 0.3 collective-permute-start.13
  67.0 4.0 %convolution_convert_fusion = bf16[512,3328]{1,0:T(8,128)(2,1)S(1)} fusion(bf16[3328,1024]{1,0:T(8,128)(2,1)S(1)} %bitcast.69, bf16[1024,1024]{1,0:T(8,128)(2,1)S(1)} %pad_maximum_fusion.1), kind=kOutput, calls=%fused_computation.1 | convolution fusion | flops 3491364864 | bytes 11272192 | tf_op jit(solution)/shard_map/dot_general | solution.py:55
  71.0 3.0 %collective-permute-start.15 = (bf16[128,3328]{1,0:T(8,128)(2,1)S(1)}, bf16[128,3328]{1,0:T(8,128)(2,1)S(1)}, u32[]{:S(2)}, u32[]{:S(2)}) collective-permute-start(bf16[128,3328]{1,0:T(8,128)(2,1)S(1)} %bitcast.82), channel_id=1, source_target_pairs={{0,8},{1,9},{2,10},{3,11},{4,12},{5,13},{6,14},{7,15},{8,0},{9,1},... | collective-permute-start | bytes 2555912 | tf_op jit(solution)/shard_map/ppermute | solution.py:40
  74.0 0.1 slice_bitcast_fusion.1
  74.1 0.4 collective-permute-done.14.refs_7_
  74.5 0.9 collective-permute-start.17
  75.4 7.8 %collective-permute-done.13 = bf16[96,3328]{1,0:T(8,128)(2,1)} collective-permute-done((bf16[96,3328]{1,0:T(8,128)(2,1)}, bf16[96,3328]{1,0:T(8,128)(2,1)}, u32[]{:S(2)}, u32[]{:S(2)}) %collective-permute-start.13) | collective-permute-done | bytes 639008 | tf_op jit(solution)/shard_map/ppermute | solution.py:40
  83.2 2.1 %fusion.3 = bf16[96,3328]{1,0:T(8,128)(2,1)} fusion(bf16[96,3328]{1,0:T(8,128)(2,1)} %collective-permute-done.13, bf16[4,128,3328]{2,1,0:T(8,128)(2,1)S(1)} %bitcast.76), kind=kLoop, calls=%fused_computation.14 | loop fusion | flops 1277952 | bytes 1916928 | tf_op jit(solution)/shard_map/convert_element_type | solution.py:47
  85.3 2.9 %collective-permute-start.16 = (bf16[96,3328]{1,0:T(8,128)(2,1)}, bf16[96,3328]{1,0:T(8,128)(2,1)S(1)}, u32[]{:S(2)}, u32[]{:S(2)}) collective-permute-start(bf16[96,3328]{1,0:T(8,128)(2,1)} %fusion.3), channel_id=1, source_target_pairs={{0,2},{1,7},{2,4},{3,1},{4,6},{5,3},{6,0},{7,5},{8,10},{9,15},{10,... | collective-permute-start | bytes 1916936 | tf_op jit(solution)/shard_map/ppermute | solution.py:40
  88.3 9.3 %shard_map.59 = bf16[1024,1024]{1,0:T(8,128)(2,1)S(1)} custom-call(bf16[128,3328]{1,0:T(8,128)(2,1)S(1)} %copy-done, bf16[128,3328]{1,0:T(8,128)(2,1)S(1)} %collective-permute-done.3.refs_1_, bf16[128,3328]{1,0:T(8,128)(2,1)S(1)} %collective-permute-done.4.refs_2_, bf16[128,3328]{1,0:T(8,128)(2,1)S(1)} %collective-permute-done.refs_3_, ...), custom_call_target="tpu_custom_call" | custom-call | flops 6979321856 | bytes 16777216 | tf_op jit(solution)/shard_map/pallas_call | solution.py:97
  97.6 2.0 %shard_map.60 = bf16[8,128,1024]{2,1,0:T(8,128)(2,1)} custom-call(s32[8]{0:T(128)S(1)} %stack.103.order_ref, bf16[8,128,1024]{2,1,0:T(8,128)(2,1)S(1)} %bitcast.70), custom_call_target="tpu_custom_call" | custom-call | bytes 2097152 | tf_op jit(solution)/shard_map/pallas_call | solution.py:63
  99.7 0.1 fusion.9
  99.8 1.4 pad_maximum_fusion.4
  101.2 1.1 fusion.2
  102.2 1.5 collective-permute-start.19
  103.7 2.9 %collective-permute-start.20 = (bf16[96,3328]{1,0:T(8,128)(2,1)}, bf16[96,3328]{1,0:T(8,128)(2,1)}, u32[]{:S(2)}, u32[]{:S(2)}) collective-permute-start(bf16[96,3328]{1,0:T(8,128)(2,1)} %fusion.2), channel_id=1, source_target_pairs={{0,8},{1,9},{2,10},{3,11},{4,12},{5,13},{6,14},{7,15},{8,0},{9,1},... | collective-permute-start | bytes 1916936 | tf_op jit(solution)/shard_map/ppermute | solution.py:40
  106.6 3.6 %all-to-all-start = ((bf16[8,128,1024]{2,1,0:T(8,128)(2,1)}), bf16[8,128,1024]{2,1,0:T(8,128)(2,1)S(1)}, u32[]{:S(2)}, u32[]{:S(2)}) async-start(bf16[8,128,1024]{2,1,0:T(8,128)(2,1)} %shard_map.60), calls=%async_computation | async-start | bytes 4194304 | tf_op jit(solution)/shard_map/all_to_all | solution.py:223
  110.2 9.0 %shard_map.61 = (bf16[1664,512]{1,0:T(8,128)(2,1)}, bf16[1664,512]{1,0:T(8,128)(2,1)}) custom-call(bf16[128,3328]{1,0:T(8,128)(2,1)} %refs_0_.2, bf16[128,3328]{1,0:T(8,128)(2,1)} %copy-done.3, bf16[128,3328]{1,0:T(8,128)(2,1)} %copy-done.2, bf16[128,3328]{1,0:T(8,128)(2,1)} %copy-done.1, bf16[128,3328]{1,0:T(8,128)(2,1)} %copy-done.4, ...), custom_call_target="tpu_custom_call" | custom-call | flops 1048576 | bytes 1048576 | tf_op jit(solution)/shard_map/pallas_call | solution.py:148
  119.3 0.9 collective-permute-done.18
  120.1 2.9 %collective-permute-done.19 = bf16[128,3328]{1,0:T(8,128)(2,1)} collective-permute-done((bf16[128,3328]{1,0:T(8,128)(2,1)}, bf16[128,3328]{1,0:T(8,128)(2,1)}, u32[]{:S(2)}, u32[]{:S(2)}) %collective-permute-start.19) | collective-permute-done | bytes 852000 | tf_op jit(solution)/shard_map/ppermute | solution.py:40
  123.0 2.7 %collective-permute-start.21 = (bf16[1664,512]{1,0:T(8,128)(2,1)}, bf16[1664,512]{1,0:T(8,128)(2,1)S(1)}, u32[]{:S(2)}, u32[]{:S(2)}) collective-permute-start(bf16[1664,512]{1,0:T(8,128)(2,1)} %get-tuple-element.65), channel_id=1, source_target_pairs={{0,1},{1,0},{2,3},{3,2},{4,5},{5,4},{6,7},{7,6},{8,9},{9,8},{10,11... | collective-permute-start | bytes 5111816 | tf_op jit(solution)/shard_map/ppermute | solution.py:40
  125.8 0.1 collective-permute-start.22
  125.9 1.1 fusion.8
  127.0 1.4 fusion
  128.4 1.0 pad_maximum_fusion.6
  129.4 1.7 %collective-permute-start.24 = (bf16[128,3328]{1,0:T(8,128)(2,1)}, bf16[128,3328]{1,0:T(8,128)(2,1)}, u32[]{:S(2)}, u32[]{:S(2)}) collective-permute-start(bf16[128,3328]{1,0:T(8,128)(2,1)} %pad_maximum_fusion.6), channel_id=1, source_target_pairs={{0,2},{1,7},{2,4},{3,1},{4,6},{5,3},{6,0},{7,5},{8,10},{9,15},{10,... | collective-permute-start | bytes 2555912 | tf_op jit(solution)/shard_map/ppermute | solution.py:40
  131.1 0.5 collective-permute-done.22.refs_11_
  131.7 0.6 copy-done.13
  132.3 1.3 copy-done.14
  133.6 9.6 %shard_map.62 = bf16[3328,512]{1,0:T(8,128)(2,1)} custom-call(bf16[128,3328]{1,0:T(8,128)(2,1)} %refs_0_.2, bf16[128,3328]{1,0:T(8,128)(2,1)} %copy-done.3, bf16[128,3328]{1,0:T(8,128)(2,1)} %copy-done.2, bf16[128,3328]{1,0:T(8,128)(2,1)} %copy-done.1, bf16[128,3328]{1,0:T(8,128)(2,1)} %copy-done.4, bf16[96,3328]{1,0:T(8,128)(2,1)} %copy-done.5, ...), custom_call_target="tpu_custom_call" | custom-call | flops 1048576 | bytes 1048576 | tf_op jit(solution)/shard_map/pallas_call | solution.py:148
  143.2 0.3 shard_map.63
  143.5 3.4 %collective-permute-start.23 = (bf16[128,512]{1,0:T(8,128)(2,1)S(1)}, bf16[128,512]{1,0:T(8,128)(2,1)S(1)}, u32[]{:S(2)}, u32[]{:S(2)}) collective-permute-start(bf16[128,512]{1,0:T(8,128)(2,1)S(1)} %get-tuple-element.82), channel_id=1, source_target_pairs={{0,1},{1,0},{2,3},{3,2},{4,5},{5,4},{6,7},{7,6},{8,9},{9,8},{10,11... | collective-permute-start | bytes 393224 | tf_op jit(solution)/shard_map/ppermute | solution.py:40
  146.9 3.2 %add_convert_fusion = bf16[128,3328]{1,0:T(8,128)(2,1)} fusion(bf16[128,3328]{1,0:T(8,128)(2,1)} %collective-permute-done.19, bf16[128,3328]{1,0:T(8,128)(2,1)} %collective-permute-done.24, bf16[512,3328]{1,0:T(8,128)(2,1)} %copy-done.11, bf16[96,3328]{1,0:T(8,128)(2,1)} %collective-permute-done.20, bf16[32,3328]{1,0:T(8,128)(2,1)S(1)} %slice-done.2), kind=kLoop, calls=%fused_computation.7 | loop fusion | flops 4685824 | bytes 4259840 | tf_op jit(solution)/shard_map/convert_element_type | solution.py:47
  150.1 0.8 maximum_select_fusion
  (65 shorter events, 0.3 us)
Async XLA Ops:
  0.6 21.0 %copy-start = (bf16[128,3328]{1,0:T(8,128)(2,1)S(1)}, bf16[128,3328]{1,0:T(8,128)(2,1)}, u32[]{:S(2)}) copy-start(bf16[128,3328]{1,0:T(8,128)(2,1)} %refs_0_.2) | copy-start | bytes 2555908
  0.6 14.0 %collective-permute-start.2 = (bf16[3328,512]{1,0:T(8,128)(2,1)}, bf16[3328,512]{1,0:T(8,128)(2,1)S(1)}, u32[]{:S(2)}, u32[]{:S(2)}) collective-permute-start(bf16[3328,512]{1,0:T(8,128)(2,1)} %param.4), channel_id=1, source_target_pairs={{0,1},{1,0},{2,3},{3,2},{4,5},{5,4},{6,7},{7,6},{8,9},{9,8},{10,11... | collective-permute-start | bytes 10223624 | tf_op jit(solution)/shard_map/ppermute | solution.py:40
  2.1 12.5 %collective-permute-start = (bf16[128,3328]{1,0:T(8,128)(2,1)}, bf16[128,3328]{1,0:T(8,128)(2,1)S(1)}, u32[]{:S(2)}, u32[]{:S(2)}) collective-permute-start(bf16[128,3328]{1,0:T(8,128)(2,1)} %refs_0_.2), channel_id=1, source_target_pairs={{0,2},{1,7},{2,4},{3,1},{4,6},{5,3},{6,0},{7,5},{8,10},{9,15},{10,... | collective-permute-start | bytes 2555912 | tf_op jit(solution)/shard_map/ppermute | solution.py:40
  4.7 8.1 %collective-permute-start.1 = (bf16[256,512]{1,0:T(8,128)(2,1)}, bf16[256,512]{1,0:T(8,128)(2,1)S(1)}, u32[]{:S(2)}, u32[]{:S(2)}) collective-permute-start(bf16[256,512]{1,0:T(8,128)(2,1)} %param.5), channel_id=1, source_target_pairs={{0,16},{1,17},{2,18},{3,19},{4,20},{5,21},{6,22},{7,23},{8,24},{9,... | collective-permute-start | bytes 786440 | tf_op jit(solution)/shard_map/ppermute | solution.py:40
  14.7 73.6 %copy-start.1 = (bf16[128,3328]{1,0:T(8,128)(2,1)}, bf16[128,3328]{1,0:T(8,128)(2,1)S(1)}, u32[]{:S(2)}) copy-start(bf16[128,3328]{1,0:T(8,128)(2,1)S(1)} %collective-permute-done.refs_3_) | copy-start | bytes 2555908
  14.7 3.8 %copy-start.12 = (bf16[3328,512]{1,0:T(8,128)(2,1)}, bf16[3328,512]{1,0:T(8,128)(2,1)S(1)}, u32[]{:S(2)}) copy-start(bf16[3328,512]{1,0:T(8,128)(2,1)S(1)} %collective-permute-done.2) | copy-start | bytes 10223620
  14.7 10.2 %collective-permute-start.7 = (bf16[512,512]{1,0:T(8,128)(2,1)}, bf16[512,512]{1,0:T(8,128)(2,1)}, u32[]{:S(2)}, u32[]{:S(2)}) collective-permute-start(bf16[512,512]{1,0:T(8,128)(2,1)} %pad_maximum_fusion.7), channel_id=1, source_target_pairs={{0,32},{1,97},{2,34},{3,99},{4,36},{5,101},{6,38},{7,103},{8,40},{... | collective-permute-start | bytes 1572872 | tf_op jit(solution)/shard_map/ppermute | solution.py:40
  18.5 21.3 %collective-permute-start.4 = (bf16[128,3328]{1,0:T(8,128)(2,1)S(1)}, bf16[128,3328]{1,0:T(8,128)(2,1)S(1)}, u32[]{:S(2)}, u32[]{:S(2)}) collective-permute-start(bf16[128,3328]{1,0:T(8,128)(2,1)S(1)} %collective-permute-done.refs_3_), channel_id=1, source_target_pairs={{0,2},{1,7},{2,4},{3,1},{4,6},{5,3},{6,0},{7,5},{8,10},{9,15},{10,... | collective-permute-start | bytes 2555912 | tf_op jit(solution)/shard_map/ppermute | solution.py:40
  21.5 19.3 %collective-permute-start.3 = (bf16[128,3328]{1,0:T(8,128)(2,1)}, bf16[128,3328]{1,0:T(8,128)(2,1)S(1)}, u32[]{:S(2)}, u32[]{:S(2)}) collective-permute-start(bf16[128,3328]{1,0:T(8,128)(2,1)} %refs_0_.2), channel_id=1, source_target_pairs={{0,6},{1,3},{2,0},{3,5},{4,2},{5,7},{6,4},{7,1},{8,14},{9,11},{10,... | collective-permute-start | bytes 2555912 | tf_op jit(solution)/shard_map/ppermute | solution.py:40
  21.7 13.3 %collective-permute-start.6 = (bf16[512,512]{1,0:T(8,128)(2,1)}, bf16[512,512]{1,0:T(8,128)(2,1)S(1)}, u32[]{:S(2)}, u32[]{:S(2)}) collective-permute-start(bf16[512,512]{1,0:T(8,128)(2,1)} %pad_maximum_fusion.7), channel_id=1, source_target_pairs={{0,96},{1,33},{2,98},{3,35},{4,100},{5,37},{6,102},{7,39},{8,104},... | collective-permute-start | bytes 1572872 | tf_op jit(solution)/shard_map/ppermute | solution.py:40
  21.7 13.6 %collective-permute-start.5 = (bf16[96,3328]{1,0:T(8,128)(2,1)S(1)}, bf16[96,3328]{1,0:T(8,128)(2,1)S(1)}, u32[]{:S(2)}, u32[]{:S(2)}) collective-permute-start(bf16[96,3328]{1,0:T(8,128)(2,1)S(1)} %slice.98), channel_id=1, source_target_pairs={{0,8},{1,9},{2,10},{3,11},{4,12},{5,13},{6,14},{7,15},{8,0},{9,1},... | collective-permute-start | bytes 1916936 | tf_op jit(solution)/shard_map/ppermute | solution.py:40
  24.9 15.9 %collective-permute-start.8 = (bf16[512,512]{1,0:T(8,128)(2,1)}, bf16[512,512]{1,0:T(8,128)(2,1)S(1)}, u32[]{:S(2)}, u32[]{:S(2)}) collective-permute-start(bf16[512,512]{1,0:T(8,128)(2,1)} %collective-permute-done.7), channel_id=1, source_target_pairs={{0,32},{1,97},{2,34},{3,99},{4,36},{5,101},{6,38},{7,103},{8,40},{... | collective-permute-start | bytes 1572872 | tf_op jit(solution)/shard_map/ppermute | solution.py:40
  35.3 7.1 %copy-start.5 = (bf16[96,3328]{1,0:T(8,128)(2,1)}, bf16[96,3328]{1,0:T(8,128)(2,1)S(1)}, u32[]{:S(2)}) copy-start(bf16[96,3328]{1,0:T(8,128)(2,1)S(1)} %collective-permute-done.5.refs_5_) | copy-start | bytes 1916932
  39.8 48.5 %copy-start.2 = (bf16[128,3328]{1,0:T(8,128)(2,1)}, bf16[128,3328]{1,0:T(8,128)(2,1)S(1)}, u32[]{:S(2)}) copy-start(bf16[128,3328]{1,0:T(8,128)(2,1)S(1)} %collective-permute-done.4.refs_2_) | copy-start | bytes 2555908
  40.8 47.5 %copy-start.3 = (bf16[128,3328]{1,0:T(8,128)(2,1)}, bf16[128,3328]{1,0:T(8,128)(2,1)S(1)}, u32[]{:S(2)}) copy-start(bf16[128,3328]{1,0:T(8,128)(2,1)S(1)} %collective-permute-done.3.refs_1_) | copy-start | bytes 2555908
  44.7 6.6 %collective-permute-start.9 = (bf16[1024,512]{1,0:T(8,128)(2,1)}, bf16[1024,512]{1,0:T(8,128)(2,1)}, u32[]{:S(2)}, u32[]{:S(2)}) collective-permute-start(bf16[1024,512]{1,0:T(8,128)(2,1)} %bitcast.18), channel_id=1, source_target_pairs={{0,1},{1,0},{2,3},{3,2},{4,5},{5,4},{6,7},{7,6},{8,9},{9,8},{10,11... | collective-permute-start | bytes 3145736 | tf_op jit(solution)/shard_map/ppermute | solution.py:40
  44.7 6.5 %copy-start.10 = (bf16[8,128,512]{2,1,0:T(8,128)(2,1)S(1)}, bf16[8,128,512]{2,1,0:T(8,128)(2,1)}, u32[]{:S(2)}) copy-start(bf16[8,128,512]{2,1,0:T(8,128)(2,1)} %get-tuple-element.80) | copy-start | bytes 3145732
  44.8 17.3 %collective-permute-start.10 = (bf16[96,3328]{1,0:T(8,128)(2,1)}, bf16[96,3328]{1,0:T(8,128)(2,1)S(1)}, u32[]{:S(2)}, u32[]{:S(2)}) collective-permute-start(bf16[96,3328]{1,0:T(8,128)(2,1)} %copy-done.5), channel_id=1, source_target_pairs={{0,2},{1,7},{2,4},{3,1},{4,6},{5,3},{6,0},{7,5},{8,10},{9,15},{10,... | collective-permute-start | bytes 1916936 | tf_op jit(solution)/shard_map/ppermute | solution.py:40
  48.2 15.5 %collective-permute-start.11 = (bf16[96,3328]{1,0:T(8,128)(2,1)}, bf16[96,3328]{1,0:T(8,128)(2,1)S(1)}, u32[]{:S(2)}, u32[]{:S(2)}) collective-permute-start(bf16[96,3328]{1,0:T(8,128)(2,1)} %copy-done.5), channel_id=1, source_target_pairs={{0,6},{1,3},{2,0},{3,5},{4,2},{5,7},{6,4},{7,1},{8,14},{9,11},{10,... | collective-permute-start | bytes 1916936 | tf_op jit(solution)/shard_map/ppermute | solution.py:40
  48.3 40.0 %collective-permute-start.12 = (bf16[128,3328]{1,0:T(8,128)(2,1)S(1)}, bf16[128,3328]{1,0:T(8,128)(2,1)S(1)}, u32[]{:S(2)}, u32[]{:S(2)}) collective-permute-start(bf16[128,3328]{1,0:T(8,128)(2,1)S(1)} %pad_maximum_fusion.3), channel_id=1, source_target_pairs={{0,8},{1,9},{2,10},{3,11},{4,12},{5,13},{6,14},{7,15},{8,0},{9,1},... | collective-permute-start | bytes 2555912 | tf_op jit(solution)/shard_map/ppermute | solution.py:40
  51.3 15.7 %slice-start = ((s8[6815744]{0:T(1024)(128)(4,1)}), s8[4194304]{0:T(1024)(128)(4,1)S(1)}, s32[]{:S(2)}) async-start(s8[6815744]{0:T(1024)(128)(4,1)} %bitcast.68), calls=%async_computation.1 | async-start | bytes 8388608
  52.9 14.1 %slice-start.1 = ((s8[6815744]{0:T(1024)(128)(4,1)}), s8[2621440]{0:T(1024)(128)(4,1)S(1)}, s32[]{:S(2)}) async-start(s8[6815744]{0:T(1024)(128)(4,1)} %bitcast.68), calls=%async_computation.2 | async-start | bytes 5242880
  62.1 26.2 %copy-start.7 = (bf16[96,3328]{1,0:T(8,128)(2,1)}, bf16[96,3328]{1,0:T(8,128)(2,1)S(1)}, u32[]{:S(2)}) copy-start(bf16[96,3328]{1,0:T(8,128)(2,1)S(1)} %collective-permute-done.10.refs_8_) | copy-start | bytes 1916932
  63.6 24.6 %copy-start.8 = (bf16[96,3328]{1,0:T(8,128)(2,1)}, bf16[96,3328]{1,0:T(8,128)(2,1)S(1)}, u32[]{:S(2)}) copy-start(bf16[96,3328]{1,0:T(8,128)(2,1)S(1)} %collective-permute-done.11.refs_6_) | copy-start | bytes 1916932
  64.9 9.6 %collective-permute-start.14 = (bf16[96,3328]{1,0:T(8,128)(2,1)S(1)}, bf16[96,3328]{1,0:T(8,128)(2,1)S(1)}, u32[]{:S(2)}, u32[]{:S(2)}) collective-permute-start(bf16[96,3328]{1,0:T(8,128)(2,1)S(1)} %collective-permute-done.10.refs_8_), channel_id=1, source_target_pairs={{0,2},{1,7},{2,4},{3,1},{4,6},{5,3},{6,0},{7,5},{8,10},{9,15},{10,... | collective-permute-start | bytes 1916936 | tf_op jit(solution)/shard_map/ppermute | solution.py:40
  66.8 16.5 %collective-permute-start.13 = (bf16[96,3328]{1,0:T(8,128)(2,1)}, bf16[96,3328]{1,0:T(8,128)(2,1)}, u32[]{:S(2)}, u32[]{:S(2)}) collective-permute-start(bf16[96,3328]{1,0:T(8,128)(2,1)} %get-tuple-element.78), channel_id=1, source_target_pairs={{0,2},{1,7},{2,4},{3,1},{4,6},{5,3},{6,0},{7,5},{8,10},{9,15},{10,... | collective-permute-start | bytes 1916936 | tf_op jit(solution)/shard_map/ppermute | solution.py:40
  71.0 28.6 %copy-start.11 = (bf16[512,3328]{1,0:T(8,128)(2,1)}, bf16[512,3328]{1,0:T(8,128)(2,1)S(1)}, u32[]{:S(2)}) copy-start(bf16[512,3328]{1,0:T(8,128)(2,1)S(1)} %convolution_convert_fusion) | copy-start | bytes 10223620
  71.0 3.5 %copy-start.17 = (bf16[96,3328]{1,0:T(8,128)(2,1)S(1)}, bf16[96,3328]{1,0:T(8,128)(2,1)}, u32[]{:S(2)}) copy-start(bf16[96,3328]{1,0:T(8,128)(2,1)} %get-tuple-element.57) | copy-start | bytes 1916932
  71.0 28.6 %collective-permute-start.15 = (bf16[128,3328]{1,0:T(8,128)(2,1)S(1)}, bf16[128,3328]{1,0:T(8,128)(2,1)S(1)}, u32[]{:S(2)}, u32[]{:S(2)}) collective-permute-start(bf16[128,3328]{1,0:T(8,128)(2,1)S(1)} %bitcast.82), channel_id=1, source_target_pairs={{0,8},{1,9},{2,10},{3,11},{4,12},{5,13},{6,14},{7,15},{8,0},{9,1},... | collective-permute-start | bytes 2555912 | tf_op jit(solution)/shard_map/ppermute | solution.py:40
  74.0 14.3 %copy-start.6 = (bf16[96,3328]{1,0:T(8,128)(2,1)S(1)}, bf16[96,3328]{1,0:T(8,128)(2,1)}, u32[]{:S(2)}) copy-start(bf16[96,3328]{1,0:T(8,128)(2,1)} %copy-done.5) | copy-start | bytes 1916932
  74.5 23.1 %copy-start.9 = (bf16[96,3328]{1,0:T(8,128)(2,1)}, bf16[96,3328]{1,0:T(8,128)(2,1)S(1)}, u32[]{:S(2)}) copy-start(bf16[96,3328]{1,0:T(8,128)(2,1)S(1)} %collective-permute-done.14.refs_7_) | copy-start | bytes 1916932
  74.5 26.6 %collective-permute-start.17 = (bf16[96,3328]{1,0:T(8,128)(2,1)S(1)}, bf16[96,3328]{1,0:T(8,128)(2,1)S(1)}, u32[]{:S(2)}, u32[]{:S(2)}) collective-permute-start(bf16[96,3328]{1,0:T(8,128)(2,1)S(1)} %copy-done.17), channel_id=1, source_target_pairs={{0,6},{1,3},{2,0},{3,5},{4,2},{5,7},{6,4},{7,1},{8,14},{9,11},{10,... | collective-permute-start | bytes 1916936 | tf_op jit(solution)/shard_map/ppermute | solution.py:40
  85.3 15.8 %collective-permute-start.16 = (bf16[96,3328]{1,0:T(8,128)(2,1)}, bf16[96,3328]{1,0:T(8,128)(2,1)S(1)}, u32[]{:S(2)}, u32[]{:S(2)}) collective-permute-start(bf16[96,3328]{1,0:T(8,128)(2,1)} %fusion.3), channel_id=1, source_target_pairs={{0,2},{1,7},{2,4},{3,1},{4,6},{5,3},{6,0},{7,5},{8,10},{9,15},{10,... | collective-permute-start | bytes 1916936 | tf_op jit(solution)/shard_map/ppermute | solution.py:40
  88.3 9.3 %copy-start.4 = (bf16[128,3328]{1,0:T(8,128)(2,1)}, bf16[128,3328]{1,0:T(8,128)(2,1)S(1)}, u32[]{:S(2)}) copy-start(bf16[128,3328]{1,0:T(8,128)(2,1)S(1)} %collective-permute-done.12.refs_4_) | copy-start | bytes 2555908
  99.6 1.5 copy-start.15
  102.2 17.9 %collective-permute-start.18 = (bf16[128,3328]{1,0:T(8,128)(2,1)}, bf16[128,3328]{1,0:T(8,128)(2,1)}, u32[]{:S(2)}, u32[]{:S(2)}) collective-permute-start(bf16[128,3328]{1,0:T(8,128)(2,1)} %get-tuple-element.58), channel_id=1, source_target_pairs={{0,2},{1,7},{2,4},{3,1},{4,6},{5,3},{6,0},{7,5},{8,10},{9,15},{10,... | collective-permute-start | bytes 2555912 | tf_op jit(solution)/shard_map/ppermute | solution.py:40
  102.2 20.8 %collective-permute-start.19 = (bf16[128,3328]{1,0:T(8,128)(2,1)}, bf16[128,3328]{1,0:T(8,128)(2,1)}, u32[]{:S(2)}, u32[]{:S(2)}) collective-permute-start(bf16[128,3328]{1,0:T(8,128)(2,1)} %get-tuple-element.59), channel_id=1, source_target_pairs={{0,6},{1,3},{2,0},{3,5},{4,2},{5,7},{6,4},{7,1},{8,14},{9,11},{10,... | collective-permute-start | bytes 2555912 | tf_op jit(solution)/shard_map/ppermute | solution.py:40
  103.7 15.6 %collective-permute-start.20 = (bf16[96,3328]{1,0:T(8,128)(2,1)}, bf16[96,3328]{1,0:T(8,128)(2,1)}, u32[]{:S(2)}, u32[]{:S(2)}) collective-permute-start(bf16[96,3328]{1,0:T(8,128)(2,1)} %fusion.2), channel_id=1, source_target_pairs={{0,8},{1,9},{2,10},{3,11},{4,12},{5,13},{6,14},{7,15},{8,0},{9,1},... | collective-permute-start | bytes 1916936 | tf_op jit(solution)/shard_map/ppermute | solution.py:40
  106.6 36.6 %all-to-all-start = ((bf16[8,128,1024]{2,1,0:T(8,128)(2,1)}), bf16[8,128,1024]{2,1,0:T(8,128)(2,1)S(1)}, u32[]{:S(2)}, u32[]{:S(2)}) async-start(bf16[8,128,1024]{2,1,0:T(8,128)(2,1)} %shard_map.60), calls=%async_computation | async-start | bytes 4194304 | tf_op jit(solution)/shard_map/all_to_all | solution.py:223
  110.2 15.7 %copy-start.16 = (bf16[128,3328]{1,0:T(8,128)(2,1)S(1)}, bf16[128,3328]{1,0:T(8,128)(2,1)}, u32[]{:S(2)}) copy-start(bf16[128,3328]{1,0:T(8,128)(2,1)} %copy-done.15) | copy-start | bytes 2555908
  123.0 8.1 %collective-permute-start.21 = (bf16[1664,512]{1,0:T(8,128)(2,1)}, bf16[1664,512]{1,0:T(8,128)(2,1)S(1)}, u32[]{:S(2)}, u32[]{:S(2)}) collective-permute-start(bf16[1664,512]{1,0:T(8,128)(2,1)} %get-tuple-element.65), channel_id=1, source_target_pairs={{0,1},{1,0},{2,3},{3,2},{4,5},{5,4},{6,7},{7,6},{8,9},{9,8},{10,11... | collective-permute-start | bytes 5111816 | tf_op jit(solution)/shard_map/ppermute | solution.py:40
  125.8 5.9 %collective-permute-start.22 = (bf16[1664,512]{1,0:T(8,128)(2,1)}, bf16[1664,512]{1,0:T(8,128)(2,1)S(1)}, u32[]{:S(2)}, u32[]{:S(2)}) collective-permute-start(bf16[1664,512]{1,0:T(8,128)(2,1)} %get-tuple-element.66), channel_id=1, source_target_pairs={{0,1},{1,0},{2,3},{3,2},{4,5},{5,4},{6,7},{7,6},{8,9},{9,8},{10,11... | collective-permute-start | bytes 5111816 | tf_op jit(solution)/shard_map/ppermute | solution.py:40
  129.4 17.6 %collective-permute-start.24 = (bf16[128,3328]{1,0:T(8,128)(2,1)}, bf16[128,3328]{1,0:T(8,128)(2,1)}, u32[]{:S(2)}, u32[]{:S(2)}) collective-permute-start(bf16[128,3328]{1,0:T(8,128)(2,1)} %pad_maximum_fusion.6), channel_id=1, source_target_pairs={{0,2},{1,7},{2,4},{3,1},{4,6},{5,3},{6,0},{7,5},{8,10},{9,15},{10,... | collective-permute-start | bytes 2555912 | tf_op jit(solution)/shard_map/ppermute | solution.py:40
  131.1 1.2 copy-start.13
  132.3 1.3 copy-start.14
  143.2 3.8 %slice-start.2 = ((bf16[128,3328]{1,0:T(8,128)(2,1)}), bf16[32,3328]{1,0:T(8,128)(2,1)S(1)}, s32[]{:S(2)}) async-start(bf16[128,3328]{1,0:T(8,128)(2,1)} %copy-done.15), calls=%async_computation.3 | async-start | bytes 425984 | tf_op jit(solution)/shard_map/slice | solution.py:239
  143.5 6.6 %collective-permute-start.23 = (bf16[128,512]{1,0:T(8,128)(2,1)S(1)}, bf16[128,512]{1,0:T(8,128)(2,1)S(1)}, u32[]{:S(2)}, u32[]{:S(2)}) collective-permute-start(bf16[128,512]{1,0:T(8,128)(2,1)S(1)} %get-tuple-element.82), channel_id=1, source_target_pairs={{0,1},{1,0},{2,3},{3,2},{4,5},{5,4},{6,7},{7,6},{8,9},{9,8},{10,11... | collective-permute-start | bytes 393224 | tf_op jit(solution)/shard_map/ppermute | solution.py:40

commit v4 on v3

--- a/solution.py
+++ b/solution.py
@@ -192,8 +192,8 @@
             order.append(((r // 2 - z) * s) % 4 * 4 + (r + y_lo) % 2 * 2 + which)
         return order
 
-    picked = pick(g, order_of(core) + order_of(1 - core)).reshape(2048, 512)
-    g_own, g_other = picked[:1024], send(picked[1024:], CORE)
+    g_other = send(pick(g, order_of(1 - core)).reshape(1024, 512), CORE)
+    g_own = pick(g, order_of(core)).reshape(1024, 512)
     g = jnp.concatenate([g_own, g_other], axis=1)
 
     far = dot(g[512:], w, ((1,), (1,))).astype(BF).reshape(4, 128, 3328)
@@ -205,23 +205,23 @@
     n = send(far[:, :b].reshape(4 * b, 3328), YH).reshape(4, b, 3328)
     near = dot(g[:512], w, ((1,), (1,))).astype(BF).reshape(4, 128, 3328)
     r1 = add(far[1, b:], r3)
-    r1, k0b = tie(r1, k0b)
-    r1 = send(r1, X1)
 
     arrays = [h0, h1, h2, h3, ka, k0b, k1b, k2b, k3b]
     plan = [(i, 0, 128, 128 * i) for i in range(4)]
     plan += [(4, a * i, a, 512 + 128 * i) for i in range(4)]
     plan += [(5 + i, 0, 128 - a, 512 + 128 * i + a) for i in range(4)]
     out = project(arrays, plan, w)
+    r1, out = tie(r1, out)
+    r1 = send(r1, X1)
 
     d3 = jnp.concatenate([add(near[2, :b], n[2]), near[2, b:]], axis=0)
     d2 = jnp.concatenate([add(near[3, :b], n[3]), near[3, b:]], axis=0)
     order = [(r // 4 + y_hi) % 2 * 4 + ((r % 4 - x) * s) % 4 for r in range(8)]
     out = pick(out.reshape(8, 128, 1024), order)
-    n0 = add(far[0, b:], r1, r2)
-    h0, out, d3, d2, n0 = tie(h0, out, d3, d2, n0)
+    h0, out, d3, d2 = tie(h0, out, d3, d2)
     out = lax.all_to_all(out, "row", 0, 0, tiled=True)
-    d3, d2, n0 = send(d3, X1), send(d2, X2), send(n0, YH)
+    d3, d2 = send(d3, X1), send(d2, X2)
+    n0 = send(add(far[0, b:], r1, r2), YH)
 
     arrays[0] = h0
     v, u = weight_gradient(arrays, plan, g_other)

time: 151 us -> 149 us (0.987)
  waiting for transfers between devices: 29.1 us -> 22.8 us
  local copies, waits for them, and re-layouts: 5.19 us -> 9.61 us
  Pallas kernels: 30.9 us -> 33.6 us
  matrix products: 11 us -> 9.26 us
    ppermute x25, waiting for transfers between devices: 29.1 us -> 22.8 us  [send(): return lax.ppermute(value, AXES, perm)]
    slice x4, local copies, waits for them, and re-layouts: 0.06 us -> 4.22 us  [per_device(): ka = send(jnp.concatenate([h0[:a], h1[:a], h2[:a], h3[:a]], axis=0), YH)]
    ppermute x25, starting transfers between devices: 46.3 us -> 44.2 us  [send(): return lax.ppermute(value, AXES, perm)]
    dot_general x2, matrix products: 11 us -> 9.26 us  [dot(): return lax.dot_general(a, b, (dims, ((), ())), preferred_element_type=F32)]
    slice x1 -> x0, local copies, waits for them, and re-layouts: 1.54 us -> none  [per_device(): g_own, g_other = (picked[:1024], send(picked[1024:], CORE))]
    pallas_call x2 -> x3, Pallas kernels: 2.68 us -> 4.19 us  [pick(): pl.pallas_call(kernel, out_shape=jax.ShapeDtypeStruct((len(order), *block...]
  transfers between devices with their start and end apart: 26 -> 26, of which waited for: 13 -> 11; matrix products, arithmetic and copies ran while one was open for 22% -> 25% of each run, Pallas kernels for 20% -> 22%
where the time goes in v4:
time: 149 us
  starting transfers between devices  48.8 us (33%)
  Pallas kernels  33.6 us (23%)
  other arithmetic  23.4 us (16%)
  waiting for transfers between devices  22.8 us (15%)
  local copies, waits for them, and re-layouts  9.61 us (6%)
  matrix products  9.26 us (6%)
    ppermute x25, starting transfers between devices, send(): return lax.ppermute(value, AXES, perm)  44.2 us
    ppermute x25, waiting for transfers between devices, send(): return lax.ppermute(value, AXES, perm)  22.8 us
    pallas_call x2, Pallas kernels, weight_gradient(): pl.pallas_call(kernel, grid=(2,), out_shape=halves if others is None else...  18.6 us
    pallas_call x1, Pallas kernels, project(): pl.pallas_call(kernel, grid=(width // tile,), out_shape=jax.ShapeDtypeStr...  10.6 us
    dot_general x2, matrix products, dot(): return lax.dot_general(a, b, (dims, ((), ())), preferred_element_type=F32)  9.26 us
    convert_element_type x6, other arithmetic, add(): return total.astype(BF)  8.18 us
    concatenate x1, other arithmetic, per_device(): w = jnp.concatenate([weight, w_other], axis=1)  6.75 us
    all_to_all x1, starting transfers between devices, per_device(): out = lax.all_to_all(out, 'row', 0, 0, tiled=True)  4.59 us
  transfers between devices with their start and end apart: 26, of which 11 were waited for; matrix products, arithmetic and copies ran while one was open for 25% of the time, Pallas kernels for 22%

profile of v4, /device:TPU:1, one launch (start us, length us, event | category | flops | bytes accessed | tf_op | source)
XLA Modules:
  0.0 148.5 jit_solution(6492363679887882423)
XLA Ops:
  0.6 1.5 %collective-permute-start.2 = (bf16[3328,512]{1,0:T(8,128)(2,1)}, bf16[3328,512]{1,0:T(8,128)(2,1)S(1)}, u32[]{:S(2)}, u32[]{:S(2)}) collective-permute-start(bf16[3328,512]{1,0:T(8,128)(2,1)} %param.4), channel_id=1, source_target_pairs={{0,1},{1,0},{2,3},{3,2},{4,5},{5,4},{6,7},{7,6},{8,9},{9,8},{10,11... | collective-permute-start | bytes 10223624 | tf_op jit(solution)/shard_map/ppermute | solution.py:40
  2.1 2.6 %collective-permute-start = (bf16[128,3328]{1,0:T(8,128)(2,1)}, bf16[128,3328]{1,0:T(8,128)(2,1)S(1)}, u32[]{:S(2)}, u32[]{:S(2)}) collective-permute-start(bf16[128,3328]{1,0:T(8,128)(2,1)} %refs_0_.2), channel_id=1, source_target_pairs={{0,2},{1,7},{2,4},{3,1},{4,6},{5,3},{6,0},{7,5},{8,10},{9,15},{10,... | collective-permute-start | bytes 2555912 | tf_op jit(solution)/shard_map/ppermute | solution.py:40
  4.7 1.3 collective-permute-start.1
  6.0 6.8 %collective-permute-done.1 = bf16[256,512]{1,0:T(8,128)(2,1)S(1)} collective-permute-done((bf16[256,512]{1,0:T(8,128)(2,1)}, bf16[256,512]{1,0:T(8,128)(2,1)S(1)}, u32[]{:S(2)}, u32[]{:S(2)}) %collective-permute-start.1) | collective-permute-done | bytes 262176 | tf_op jit(solution)/shard_map/ppermute | solution.py:40
  12.8 1.0 pad_maximum_fusion.7
  13.8 0.9 collective-permute-done.refs_3_
  14.7 3.8 %collective-permute-start.7 = (bf16[512,512]{1,0:T(8,128)(2,1)S(1)}, bf16[512,512]{1,0:T(8,128)(2,1)S(1)}, u32[]{:S(2)}, u32[]{:S(2)}) collective-permute-start(bf16[512,512]{1,0:T(8,128)(2,1)S(1)} %pad_maximum_fusion.7), channel_id=1, source_target_pairs={{0,32},{1,97},{2,34},{3,99},{4,36},{5,101},{6,38},{7,103},{8,40},{... | collective-permute-start | bytes 1572872 | tf_op jit(solution)/shard_map/ppermute | solution.py:40
  18.4 0.9 collective-permute-start.3
  19.3 2.2 %collective-permute-start.4 = (bf16[128,3328]{1,0:T(8,128)(2,1)S(1)}, bf16[128,3328]{1,0:T(8,128)(2,1)}, u32[]{:S(2)}, u32[]{:S(2)}) collective-permute-start(bf16[128,3328]{1,0:T(8,128)(2,1)S(1)} %collective-permute-done.refs_3_), channel_id=1, source_target_pairs={{0,2},{1,7},{2,4},{3,1},{4,6},{5,3},{6,0},{7,5},{8,10},{9,15},{10,... | collective-permute-start | bytes 2555912 | tf_op jit(solution)/shard_map/ppermute | solution.py:40
  21.7 3.0 %collective-permute-start.5 = (bf16[96,3328]{1,0:T(8,128)(2,1)S(1)}, bf16[96,3328]{1,0:T(8,128)(2,1)S(1)}, u32[]{:S(2)}, u32[]{:S(2)}) collective-permute-start(bf16[96,3328]{1,0:T(8,128)(2,1)S(1)} %slice.86), channel_id=1, source_target_pairs={{0,8},{1,9},{2,10},{3,11},{4,12},{5,13},{6,14},{7,15},{8,0},{9,1},... | collective-permute-start | bytes 1916936 | tf_op jit(solution)/shard_map/ppermute | solution.py:40
  24.7 3.4 %collective-permute-start.8 = (bf16[512,512]{1,0:T(8,128)(2,1)S(1)}, bf16[512,512]{1,0:T(8,128)(2,1)S(1)}, u32[]{:S(2)}, u32[]{:S(2)}) collective-permute-start(bf16[512,512]{1,0:T(8,128)(2,1)S(1)} %collective-permute-done.7), channel_id=1, source_target_pairs={{0,32},{1,97},{2,34},{3,99},{4,36},{5,101},{6,38},{7,103},{8,40},{... | collective-permute-start | bytes 1572872 | tf_op jit(solution)/shard_map/ppermute | solution.py:40
  28.1 6.8 %pad_maximum_fusion.refs_9_ = bf16[3328,1024]{1,0:T(8,128)(2,1)} fusion(bf16[3328,512]{1,0:T(8,128)(2,1)} %copy-done.13, bf16[3328,512]{1,0:T(8,128)(2,1)} %param.4), kind=kLoop, calls=%fused_computation | loop fusion | flops 13631488 | bytes 13631488 | tf_op jit(solution)/shard_map/concatenate | solution.py:181
  34.8 1.6 %collective-permute-done.5.refs_5_ = bf16[96,3328]{1,0:T(8,128)(2,1)S(1)} collective-permute-done((bf16[96,3328]{1,0:T(8,128)(2,1)S(1)}, bf16[96,3328]{1,0:T(8,128)(2,1)S(1)}, u32[]{:S(2)}, u32[]{:S(2)}) %collective-permute-start.5) | collective-permute-done | bytes 639008 | tf_op jit(solution)/shard_map/ppermute | solution.py:40
  36.4 3.5 %collective-permute-done.3.refs_1_ = bf16[128,3328]{1,0:T(8,128)(2,1)} collective-permute-done((bf16[128,3328]{1,0:T(8,128)(2,1)}, bf16[128,3328]{1,0:T(8,128)(2,1)}, u32[]{:S(2)}, u32[]{:S(2)}) %collective-permute-start.3) | collective-permute-done | bytes 852000 | tf_op jit(solution)/shard_map/ppermute | solution.py:40
  39.9 0.3 collective-permute-done.4.refs_2_
  40.2 1.2 pad_maximum_fusion.2
  41.3 1.6 %shard_map.59 = bf16[8,128,512]{2,1,0:T(8,128)(2,1)} custom-call(s32[8]{0:T(128)S(1)} %stack.98.order_ref, bf16[16,128,512]{2,1,0:T(8,128)(2,1)S(1)} %bitcast.67), custom_call_target="tpu_custom_call" | custom-call | bytes 2097152 | tf_op jit(solution)/shard_map/pallas_call | solution.py:63
  42.9 1.6 %collective-permute-start.9 = (bf16[1024,512]{1,0:T(8,128)(2,1)}, bf16[1024,512]{1,0:T(8,128)(2,1)}, u32[]{:S(2)}, u32[]{:S(2)}) collective-permute-start(bf16[1024,512]{1,0:T(8,128)(2,1)} %bitcast.18), channel_id=1, source_target_pairs={{0,1},{1,0},{2,3},{3,2},{4,5},{5,4},{6,7},{7,6},{8,9},{9,8},{10,11... | collective-permute-start | bytes 3145736 | tf_op jit(solution)/shard_map/ppermute | solution.py:40
  44.7 0.9 slice.93
  45.7 2.7 %collective-permute-start.10 = (bf16[96,3328]{1,0:T(8,128)(2,1)}, bf16[96,3328]{1,0:T(8,128)(2,1)S(1)}, u32[]{:S(2)}, u32[]{:S(2)}) collective-permute-start(bf16[96,3328]{1,0:T(8,128)(2,1)} %copy-done.7), channel_id=1, source_target_pairs={{0,2},{1,7},{2,4},{3,1},{4,6},{5,3},{6,0},{7,5},{8,10},{9,15},{10,... | collective-permute-start | bytes 1916936 | tf_op jit(solution)/shard_map/ppermute | solution.py:40
  48.4 1.6 %slice.91 = bf16[32,3328]{1,0:T(8,128)(2,1)} slice(bf16[128,3328]{1,0:T(8,128)(2,1)} %collective-permute-done.3.refs_1_), slice={[0:32], [0:3328]} | slice | bytes 425984 | tf_op jit(solution)/shard_map/slice | solution.py:184
  50.0 1.6 %slice.92 = bf16[32,3328]{1,0:T(8,128)(2,1)} slice(bf16[128,3328]{1,0:T(8,128)(2,1)} %collective-permute-done.4.refs_2_), slice={[0:32], [0:3328]} | slice | bytes 425984 | tf_op jit(solution)/shard_map/slice | solution.py:184
  51.6 1.1 pad_maximum_fusion.3
  52.7 3.0 %collective-permute-start.13 = (bf16[128,3328]{1,0:T(8,128)(2,1)S(1)}, bf16[128,3328]{1,0:T(8,128)(2,1)S(1)}, u32[]{:S(2)}, u32[]{:S(2)}) collective-permute-start(bf16[128,3328]{1,0:T(8,128)(2,1)S(1)} %pad_maximum_fusion.3), channel_id=1, source_target_pairs={{0,8},{1,9},{2,10},{3,11},{4,12},{5,13},{6,14},{7,15},{8,0},{9,1},... | collective-permute-start | bytes 2555912 | tf_op jit(solution)/shard_map/ppermute | solution.py:40
  55.7 0.6 shard_map.58
  56.4 2.1 %pad_maximum_fusion.1 = bf16[1024,1024]{1,0:T(8,128)(2,1)S(1)} fusion(bf16[1024,512]{1,0:T(8,128)(2,1)} %collective-permute-done.9.refs_9_, bf16[1024,512]{1,0:T(8,128)(2,1)S(1)} %bitcast.69), kind=kLoop, calls=%fused_computation.4 | loop fusion | flops 4194304 | bytes 4194304 | tf_op jit(solution)/shard_map/concatenate | solution.py:197
  58.5 0.8 copy-done.3
  59.4 5.3 %convolution_convert_fusion.1 = bf16[512,3328]{1,0:T(8,128)(2,1)S(1)} fusion(bf16[3328,1024]{1,0:T(8,128)(2,1)S(1)} %copy-done.3, bf16[1024,512]{1,0:T(8,128)(2,1)S(1)} %bitcast.70, bf16[1024,512]{1,0:T(8,128)(2,1)} %collective-permute-done.9.refs_9_), kind=kOutput, calls=%fused_computation.2 | convolution fusion | flops 3493462016 | bytes 12320768 | tf_op jit(solution)/shard_map/dot_general | solution.py:55
  64.7 1.0 slice.97
  65.7 1.2 slice_bitcast_fusion.3
  66.9 0.5 collective-permute-start.14
  67.3 2.8 %collective-permute-start.15 = (bf16[128,3328]{1,0:T(8,128)(2,1)}, bf16[128,3328]{1,0:T(8,128)(2,1)S(1)}, u32[]{:S(2)}, u32[]{:S(2)}) collective-permute-start(bf16[128,3328]{1,0:T(8,128)(2,1)} %bitcast.34), channel_id=1, source_target_pairs={{0,8},{1,9},{2,10},{3,11},{4,12},{5,13},{6,14},{7,15},{8,0},{9,1},... | collective-permute-start | bytes 2555912 | tf_op jit(solution)/shard_map/ppermute | solution.py:40
  70.1 4.0 %convolution_convert_fusion = bf16[512,3328]{1,0:T(8,128)(2,1)S(1)} fusion(bf16[3328,1024]{1,0:T(8,128)(2,1)S(1)} %copy-done.3, bf16[1024,1024]{1,0:T(8,128)(2,1)S(1)} %pad_maximum_fusion.1), kind=kOutput, calls=%fused_computation.1 | convolution fusion | flops 3491364864 | bytes 11272192 | tf_op jit(solution)/shard_map/dot_general | solution.py:55
  74.2 2.2 %collective-permute-done.14.refs_7_ = bf16[96,3328]{1,0:T(8,128)(2,1)S(1)} collective-permute-done((bf16[96,3328]{1,0:T(8,128)(2,1)S(1)}, bf16[96,3328]{1,0:T(8,128)(2,1)S(1)}, u32[]{:S(2)}, u32[]{:S(2)}) %collective-permute-start.14) | collective-permute-done | bytes 639008 | tf_op jit(solution)/shard_map/ppermute | solution.py:40
  76.5 0.3 copy-done.5
  76.7 0.2 copy-done.8
  76.9 10.6 %shard_map.60 = bf16[1024,1024]{1,0:T(8,128)(2,1)S(1)} custom-call(bf16[128,3328]{1,0:T(8,128)(2,1)S(1)} %copy-done.2, bf16[128,3328]{1,0:T(8,128)(2,1)} %collective-permute-done.3.refs_1_, bf16[128,3328]{1,0:T(8,128)(2,1)} %collective-permute-done.4.refs_2_, bf16[128,3328]{1,0:T(8,128)(2,1)S(1)} %copy-done.5, ...), custom_call_target="tpu_custom_call" | custom-call | flops 6979321856 | bytes 16777216 | tf_op jit(solution)/shard_map/pallas_call | solution.py:97
  87.5 1.3 fusion.3
  88.8 2.3 %collective-permute-start.18 = (bf16[96,3328]{1,0:T(8,128)(2,1)S(1)}, bf16[96,3328]{1,0:T(8,128)(2,1)S(1)}, u32[]{:S(2)}, u32[]{:S(2)}) collective-permute-start(bf16[96,3328]{1,0:T(8,128)(2,1)S(1)} %fusion.3), channel_id=1, source_target_pairs={{0,2},{1,7},{2,4},{3,1},{4,6},{5,3},{6,0},{7,5},{8,10},{9,15},{10,... | collective-permute-start | bytes 1916936 | tf_op jit(solution)/shard_map/ppermute | solution.py:40
  91.1 2.0 %shard_map.61 = bf16[8,128,1024]{2,1,0:T(8,128)(2,1)} custom-call(s32[8]{0:T(128)S(1)} %stack.107.order_ref, bf16[8,128,1024]{2,1,0:T(8,128)(2,1)S(1)} %bitcast.72), custom_call_target="tpu_custom_call" | custom-call | bytes 2097152 | tf_op jit(solution)/shard_map/pallas_call | solution.py:63
  93.1 0.1 collective-permute-done.15
  93.2 0.1 fusion.9
  93.3 1.4 pad_maximum_fusion.4
  94.6 0.4 collective-permute-start.16
  95.0 1.1 collective-permute-start.17
  96.1 2.5 %collective-permute-done.18 = bf16[96,3328]{1,0:T(8,128)(2,1)S(1)} collective-permute-done((bf16[96,3328]{1,0:T(8,128)(2,1)S(1)}, bf16[96,3328]{1,0:T(8,128)(2,1)S(1)}, u32[]{:S(2)}, u32[]{:S(2)}) %collective-permute-start.18) | collective-permute-done | bytes 639008 | tf_op jit(solution)/shard_map/ppermute | solution.py:40
  98.6 1.1 fusion.2
  99.8 1.6 %collective-permute-start.20 = (bf16[96,3328]{1,0:T(8,128)(2,1)}, bf16[96,3328]{1,0:T(8,128)(2,1)}, u32[]{:S(2)}, u32[]{:S(2)}) collective-permute-start(bf16[96,3328]{1,0:T(8,128)(2,1)} %fusion.2), channel_id=1, source_target_pairs={{0,8},{1,9},{2,10},{3,11},{4,12},{5,13},{6,14},{7,15},{8,0},{9,1},... | collective-permute-start | bytes 1916936 | tf_op jit(solution)/shard_map/ppermute | solution.py:40
  101.3 4.6 %all-to-all-start = ((bf16[8,128,1024]{2,1,0:T(8,128)(2,1)}), bf16[8,128,1024]{2,1,0:T(8,128)(2,1)S(1)}, u32[]{:S(2)}, u32[]{:S(2)}) async-start(bf16[8,128,1024]{2,1,0:T(8,128)(2,1)} %shard_map.61), calls=%async_computation | async-start | bytes 4194304 | tf_op jit(solution)/shard_map/all_to_all | solution.py:222
  105.9 9.0 %shard_map.62 = (bf16[1664,512]{1,0:T(8,128)(2,1)}, bf16[1664,512]{1,0:T(8,128)(2,1)}) custom-call(bf16[128,3328]{1,0:T(8,128)(2,1)} %refs_0_.2, bf16[128,3328]{1,0:T(8,128)(2,1)} %collective-permute-done.3.refs_1_, bf16[128,3328]{1,0:T(8,128)(2,1)} %collective-permute-done.4.refs_2_, bf16[128,3328]{1,0:T(8,128)(2,1)} %copy-done.4, ...), custom_call_target="tpu_custom_call" | custom-call | flops 1048576 | bytes 1048576 | tf_op jit(solution)/shard_map/pallas_call | solution.py:148
  115.0 0.8 collective-permute-done.16
  115.7 1.9 %collective-permute-done.17 = bf16[128,3328]{1,0:T(8,128)(2,1)} collective-permute-done((bf16[128,3328]{1,0:T(8,128)(2,1)}, bf16[128,3328]{1,0:T(8,128)(2,1)}, u32[]{:S(2)}, u32[]{:S(2)}) %collective-permute-start.17) | collective-permute-done | bytes 852000 | tf_op jit(solution)/shard_map/ppermute | solution.py:40
  117.6 9.3 %collective-permute-start.21 = (bf16[1664,512]{1,0:T(8,128)(2,1)}, bf16[1664,512]{1,0:T(8,128)(2,1)S(1)}, u32[]{:S(2)}, u32[]{:S(2)}) collective-permute-start(bf16[1664,512]{1,0:T(8,128)(2,1)} %get-tuple-element.63), channel_id=1, source_target_pairs={{0,1},{1,0},{2,3},{3,2},{4,5},{5,4},{6,7},{7,6},{8,9},{9,8},{10,11... | collective-permute-start | bytes 5111816 | tf_op jit(solution)/shard_map/ppermute | solution.py:40
  126.9 1.1 fusion.8
  128.0 1.4 fusion
  129.5 1.0 pad_maximum_fusion.6
  130.4 2.3 %collective-permute-done.22.refs_11_ = bf16[1664,512]{1,0:T(8,128)(2,1)S(1)} collective-permute-done((bf16[1664,512]{1,0:T(8,128)(2,1)}, bf16[1664,512]{1,0:T(8,128)(2,1)S(1)}, u32[]{:S(2)}, u32[]{:S(2)}) %collective-permute-start.22) | collective-permute-done | bytes 1703968 | tf_op jit(solution)/shard_map/ppermute | solution.py:40
  132.8 1.3 copy-done.15
  134.1 9.6 %shard_map.63 = bf16[3328,512]{1,0:T(8,128)(2,1)} custom-call(bf16[128,3328]{1,0:T(8,128)(2,1)} %refs_0_.2, bf16[128,3328]{1,0:T(8,128)(2,1)} %collective-permute-done.3.refs_1_, bf16[128,3328]{1,0:T(8,128)(2,1)} %collective-permute-done.4.refs_2_, bf16[128,3328]{1,0:T(8,128)(2,1)} %copy-done.4, bf16[128,3328]{1,0:T(8,128)(2,1)} %copy-done.6, ...), custom_call_target="tpu_custom_call" | custom-call | flops 1048576 | bytes 1048576 | tf_op jit(solution)/shard_map/pallas_call | solution.py:148
  143.7 0.3 shard_map.64
  144.0 0.5 collective-permute-start.23
  144.4 0.2 slice-done
  144.6 3.2 %add_convert_fusion = bf16[128,3328]{1,0:T(8,128)(2,1)} fusion(bf16[128,3328]{1,0:T(8,128)(2,1)} %collective-permute-done.17, bf16[128,3328]{1,0:T(8,128)(2,1)} %collective-permute-done.24, bf16[512,3328]{1,0:T(8,128)(2,1)} %copy-done.12, bf16[96,3328]{1,0:T(8,128)(2,1)} %collective-permute-done.20, bf16[32,3328]{1,0:T(8,128)(2,1)S(1)} %slice-done), kind=kLoop, calls=%fused_computation.7 | loop fusion | flops 4685824 | bytes 4259840 | tf_op jit(solution)/shard_map/convert_element_type | solution.py:47
  147.8 0.8 maximum_select_fusion
  (63 shorter events, 0.6 us)
Async XLA Ops:
  0.6 21.0 %copy-start.1 = (bf16[128,3328]{1,0:T(8,128)(2,1)S(1)}, bf16[128,3328]{1,0:T(8,128)(2,1)}, u32[]{:S(2)}) copy-start(bf16[128,3328]{1,0:T(8,128)(2,1)} %refs_0_.2) | copy-start | bytes 2555908
  0.6 14.0 %collective-permute-start.2 = (bf16[3328,512]{1,0:T(8,128)(2,1)}, bf16[3328,512]{1,0:T(8,128)(2,1)S(1)}, u32[]{:S(2)}, u32[]{:S(2)}) collective-permute-start(bf16[3328,512]{1,0:T(8,128)(2,1)} %param.4), channel_id=1, source_target_pairs={{0,1},{1,0},{2,3},{3,2},{4,5},{5,4},{6,7},{7,6},{8,9},{9,8},{10,11... | collective-permute-start | bytes 10223624 | tf_op jit(solution)/shard_map/ppermute | solution.py:40
  2.1 12.5 %collective-permute-start = (bf16[128,3328]{1,0:T(8,128)(2,1)}, bf16[128,3328]{1,0:T(8,128)(2,1)S(1)}, u32[]{:S(2)}, u32[]{:S(2)}) collective-permute-start(bf16[128,3328]{1,0:T(8,128)(2,1)} %refs_0_.2), channel_id=1, source_target_pairs={{0,2},{1,7},{2,4},{3,1},{4,6},{5,3},{6,0},{7,5},{8,10},{9,15},{10,... | collective-permute-start | bytes 2555912 | tf_op jit(solution)/shard_map/ppermute | solution.py:40
  4.7 8.1 %collective-permute-start.1 = (bf16[256,512]{1,0:T(8,128)(2,1)}, bf16[256,512]{1,0:T(8,128)(2,1)S(1)}, u32[]{:S(2)}, u32[]{:S(2)}) collective-permute-start(bf16[256,512]{1,0:T(8,128)(2,1)} %param.5), channel_id=1, source_target_pairs={{0,16},{1,17},{2,18},{3,19},{4,20},{5,21},{6,22},{7,23},{8,24},{9,... | collective-permute-start | bytes 786440 | tf_op jit(solution)/shard_map/ppermute | solution.py:40
  14.7 20.2 %copy-start.4 = (bf16[128,3328]{1,0:T(8,128)(2,1)}, bf16[128,3328]{1,0:T(8,128)(2,1)S(1)}, u32[]{:S(2)}) copy-start(bf16[128,3328]{1,0:T(8,128)(2,1)S(1)} %collective-permute-done.refs_3_) | copy-start | bytes 2555908
  14.7 3.8 %copy-start.13 = (bf16[3328,512]{1,0:T(8,128)(2,1)}, bf16[3328,512]{1,0:T(8,128)(2,1)S(1)}, u32[]{:S(2)}) copy-start(bf16[3328,512]{1,0:T(8,128)(2,1)S(1)} %collective-permute-done.2) | copy-start | bytes 10223620
  14.7 10.0 %collective-permute-start.7 = (bf16[512,512]{1,0:T(8,128)(2,1)S(1)}, bf16[512,512]{1,0:T(8,128)(2,1)S(1)}, u32[]{:S(2)}, u32[]{:S(2)}) collective-permute-start(bf16[512,512]{1,0:T(8,128)(2,1)S(1)} %pad_maximum_fusion.7), channel_id=1, source_target_pairs={{0,32},{1,97},{2,34},{3,99},{4,36},{5,101},{6,38},{7,103},{8,40},{... | collective-permute-start | bytes 1572872 | tf_op jit(solution)/shard_map/ppermute | solution.py:40
  18.4 21.5 %collective-permute-start.3 = (bf16[128,3328]{1,0:T(8,128)(2,1)}, bf16[128,3328]{1,0:T(8,128)(2,1)}, u32[]{:S(2)}, u32[]{:S(2)}) collective-permute-start(bf16[128,3328]{1,0:T(8,128)(2,1)} %refs_0_.2), channel_id=1, source_target_pairs={{0,6},{1,3},{2,0},{3,5},{4,2},{5,7},{6,4},{7,1},{8,14},{9,11},{10,... | collective-permute-start | bytes 2555912 | tf_op jit(solution)/shard_map/ppermute | solution.py:40
  19.3 20.8 %collective-permute-start.4 = (bf16[128,3328]{1,0:T(8,128)(2,1)S(1)}, bf16[128,3328]{1,0:T(8,128)(2,1)}, u32[]{:S(2)}, u32[]{:S(2)}) collective-permute-start(bf16[128,3328]{1,0:T(8,128)(2,1)S(1)} %collective-permute-done.refs_3_), channel_id=1, source_target_pairs={{0,2},{1,7},{2,4},{3,1},{4,6},{5,3},{6,0},{7,5},{8,10},{9,15},{10,... | collective-permute-start | bytes 2555912 | tf_op jit(solution)/shard_map/ppermute | solution.py:40
  21.6 13.2 %collective-permute-start.6 = (bf16[512,512]{1,0:T(8,128)(2,1)S(1)}, bf16[512,512]{1,0:T(8,128)(2,1)S(1)}, u32[]{:S(2)}, u32[]{:S(2)}) collective-permute-start(bf16[512,512]{1,0:T(8,128)(2,1)S(1)} %pad_maximum_fusion.7), channel_id=1, source_target_pairs={{0,96},{1,33},{2,98},{3,35},{4,100},{5,37},{6,102},{7,39},{8,104},... | collective-permute-start | bytes 1572872 | tf_op jit(solution)/shard_map/ppermute | solution.py:40
  21.7 14.7 %collective-permute-start.5 = (bf16[96,3328]{1,0:T(8,128)(2,1)S(1)}, bf16[96,3328]{1,0:T(8,128)(2,1)S(1)}, u32[]{:S(2)}, u32[]{:S(2)}) collective-permute-start(bf16[96,3328]{1,0:T(8,128)(2,1)S(1)} %slice.86), channel_id=1, source_target_pairs={{0,8},{1,9},{2,10},{3,11},{4,12},{5,13},{6,14},{7,15},{8,0},{9,1},... | collective-permute-start | bytes 1916936 | tf_op jit(solution)/shard_map/ppermute | solution.py:40
  24.7 10.2 %copy-start.18 = (bf16[512,512]{1,0:T(8,128)(2,1)}, bf16[512,512]{1,0:T(8,128)(2,1)S(1)}, u32[]{:S(2)}) copy-start(bf16[512,512]{1,0:T(8,128)(2,1)S(1)} %collective-permute-done.7) | copy-start | bytes 1572868
  24.7 15.5 %collective-permute-start.8 = (bf16[512,512]{1,0:T(8,128)(2,1)S(1)}, bf16[512,512]{1,0:T(8,128)(2,1)S(1)}, u32[]{:S(2)}, u32[]{:S(2)}) collective-permute-start(bf16[512,512]{1,0:T(8,128)(2,1)S(1)} %collective-permute-done.7), channel_id=1, source_target_pairs={{0,32},{1,97},{2,34},{3,99},{4,36},{5,101},{6,38},{7,103},{8,40},{... | collective-permute-start | bytes 1572872 | tf_op jit(solution)/shard_map/ppermute | solution.py:40
  36.4 3.8 %copy-start.7 = (bf16[96,3328]{1,0:T(8,128)(2,1)}, bf16[96,3328]{1,0:T(8,128)(2,1)S(1)}, u32[]{:S(2)}) copy-start(bf16[96,3328]{1,0:T(8,128)(2,1)S(1)} %collective-permute-done.5.refs_5_) | copy-start | bytes 1916932
  42.9 13.4 %collective-permute-start.9 = (bf16[1024,512]{1,0:T(8,128)(2,1)}, bf16[1024,512]{1,0:T(8,128)(2,1)}, u32[]{:S(2)}, u32[]{:S(2)}) collective-permute-start(bf16[1024,512]{1,0:T(8,128)(2,1)} %bitcast.18), channel_id=1, source_target_pairs={{0,1},{1,0},{2,3},{3,2},{4,5},{5,4},{6,7},{7,6},{8,9},{9,8},{10,11... | collective-permute-start | bytes 3145736 | tf_op jit(solution)/shard_map/ppermute | solution.py:40
  45.6 19.0 %collective-permute-start.11 = (bf16[96,3328]{1,0:T(8,128)(2,1)}, bf16[96,3328]{1,0:T(8,128)(2,1)S(1)}, u32[]{:S(2)}, u32[]{:S(2)}) collective-permute-start(bf16[96,3328]{1,0:T(8,128)(2,1)} %copy-done.7), channel_id=1, source_target_pairs={{0,6},{1,3},{2,0},{3,5},{4,2},{5,7},{6,4},{7,1},{8,14},{9,11},{10,... | collective-permute-start | bytes 1916936 | tf_op jit(solution)/shard_map/ppermute | solution.py:40
  45.7 18.9 %collective-permute-start.10 = (bf16[96,3328]{1,0:T(8,128)(2,1)}, bf16[96,3328]{1,0:T(8,128)(2,1)S(1)}, u32[]{:S(2)}, u32[]{:S(2)}) collective-permute-start(bf16[96,3328]{1,0:T(8,128)(2,1)} %copy-done.7), channel_id=1, source_target_pairs={{0,2},{1,7},{2,4},{3,1},{4,6},{5,3},{6,0},{7,5},{8,10},{9,15},{10,... | collective-permute-start | bytes 1916936 | tf_op jit(solution)/shard_map/ppermute | solution.py:40
  52.7 23.7 %collective-permute-start.13 = (bf16[128,3328]{1,0:T(8,128)(2,1)S(1)}, bf16[128,3328]{1,0:T(8,128)(2,1)S(1)}, u32[]{:S(2)}, u32[]{:S(2)}) collective-permute-start(bf16[128,3328]{1,0:T(8,128)(2,1)S(1)} %pad_maximum_fusion.3), channel_id=1, source_target_pairs={{0,8},{1,9},{2,10},{3,11},{4,12},{5,13},{6,14},{7,15},{8,0},{9,1},... | collective-permute-start | bytes 2555912 | tf_op jit(solution)/shard_map/ppermute | solution.py:40
  55.7 3.6 %copy-start.3 = (bf16[3328,1024]{1,0:T(8,128)(2,1)S(1)}, bf16[3328,1024]{1,0:T(8,128)(2,1)}, u32[]{:S(2)}) copy-start(bf16[3328,1024]{1,0:T(8,128)(2,1)} %pad_maximum_fusion.refs_9_) | copy-start | bytes 20447236
  56.3 2.2 %copy-start = (bf16[8,128,512]{2,1,0:T(8,128)(2,1)}, bf16[8,128,512]{2,1,0:T(8,128)(2,1)S(1)}, u32[]{:S(2)}) copy-start(bf16[8,128,512]{2,1,0:T(8,128)(2,1)S(1)} %shard_map.58) | copy-start | bytes 3145732
  64.7 11.8 %copy-start.9 = (bf16[96,3328]{1,0:T(8,128)(2,1)}, bf16[96,3328]{1,0:T(8,128)(2,1)S(1)}, u32[]{:S(2)}) copy-start(bf16[96,3328]{1,0:T(8,128)(2,1)S(1)} %collective-permute-done.11.refs_6_) | copy-start | bytes 1916932
  64.7 11.8 %copy-start.10 = (bf16[96,3328]{1,0:T(8,128)(2,1)}, bf16[96,3328]{1,0:T(8,128)(2,1)S(1)}, u32[]{:S(2)}) copy-start(bf16[96,3328]{1,0:T(8,128)(2,1)S(1)} %collective-permute-done.10.refs_8_) | copy-start | bytes 1916932
  66.9 9.6 %collective-permute-start.14 = (bf16[96,3328]{1,0:T(8,128)(2,1)S(1)}, bf16[96,3328]{1,0:T(8,128)(2,1)S(1)}, u32[]{:S(2)}, u32[]{:S(2)}) collective-permute-start(bf16[96,3328]{1,0:T(8,128)(2,1)S(1)} %collective-permute-done.10.refs_8_), channel_id=1, source_target_pairs={{0,2},{1,7},{2,4},{3,1},{4,6},{5,3},{6,0},{7,5},{8,10},{9,15},{10,... | collective-permute-start | bytes 1916936 | tf_op jit(solution)/shard_map/ppermute | solution.py:40
  67.3 25.8 %collective-permute-start.15 = (bf16[128,3328]{1,0:T(8,128)(2,1)}, bf16[128,3328]{1,0:T(8,128)(2,1)S(1)}, u32[]{:S(2)}, u32[]{:S(2)}) collective-permute-start(bf16[128,3328]{1,0:T(8,128)(2,1)} %bitcast.34), channel_id=1, source_target_pairs={{0,8},{1,9},{2,10},{3,11},{4,12},{5,13},{6,14},{7,15},{8,0},{9,1},... | collective-permute-start | bytes 2555912 | tf_op jit(solution)/shard_map/ppermute | solution.py:40
  70.1 17.4 %collective-permute-start.12 = (bf16[96,3328]{1,0:T(8,128)(2,1)}, bf16[96,3328]{1,0:T(8,128)(2,1)}, u32[]{:S(2)}, u32[]{:S(2)}) collective-permute-start(bf16[96,3328]{1,0:T(8,128)(2,1)} %get-tuple-element.76), channel_id=1, source_target_pairs={{0,2},{1,7},{2,4},{3,1},{4,6},{5,3},{6,0},{7,5},{8,10},{9,15},{10,... | collective-permute-start | bytes 1916936 | tf_op jit(solution)/shard_map/ppermute | solution.py:40
  74.1 19.1 %copy-start.12 = (bf16[512,3328]{1,0:T(8,128)(2,1)}, bf16[512,3328]{1,0:T(8,128)(2,1)S(1)}, u32[]{:S(2)}) copy-start(bf16[512,3328]{1,0:T(8,128)(2,1)S(1)} %convolution_convert_fusion) | copy-start | bytes 10223620
  74.1 2.4 %copy-start.2 = (bf16[128,3328]{1,0:T(8,128)(2,1)S(1)}, bf16[128,3328]{1,0:T(8,128)(2,1)}, u32[]{:S(2)}) copy-start(bf16[128,3328]{1,0:T(8,128)(2,1)} %refs_0_.2) | copy-start | bytes 2555908
  74.1 2.6 %copy-start.5 = (bf16[128,3328]{1,0:T(8,128)(2,1)S(1)}, bf16[128,3328]{1,0:T(8,128)(2,1)}, u32[]{:S(2)}) copy-start(bf16[128,3328]{1,0:T(8,128)(2,1)} %copy-done.4) | copy-start | bytes 2555908
  74.1 2.8 %copy-start.8 = (bf16[96,3328]{1,0:T(8,128)(2,1)S(1)}, bf16[96,3328]{1,0:T(8,128)(2,1)}, u32[]{:S(2)}) copy-start(bf16[96,3328]{1,0:T(8,128)(2,1)} %copy-done.7) | copy-start | bytes 1916932
  76.4 11.1 %copy-start.11 = (bf16[96,3328]{1,0:T(8,128)(2,1)}, bf16[96,3328]{1,0:T(8,128)(2,1)S(1)}, u32[]{:S(2)}) copy-start(bf16[96,3328]{1,0:T(8,128)(2,1)S(1)} %collective-permute-done.14.refs_7_) | copy-start | bytes 1916932
  76.4 19.7 %collective-permute-start.19 = (bf16[96,3328]{1,0:T(8,128)(2,1)}, bf16[96,3328]{1,0:T(8,128)(2,1)S(1)}, u32[]{:S(2)}, u32[]{:S(2)}) collective-permute-start(bf16[96,3328]{1,0:T(8,128)(2,1)} %get-tuple-element.58), channel_id=1, source_target_pairs={{0,6},{1,3},{2,0},{3,5},{4,2},{5,7},{6,4},{7,1},{8,14},{9,11},{10,... | collective-permute-start | bytes 1916936 | tf_op jit(solution)/shard_map/ppermute | solution.py:40
  76.9 10.6 %copy-start.6 = (bf16[128,3328]{1,0:T(8,128)(2,1)}, bf16[128,3328]{1,0:T(8,128)(2,1)S(1)}, u32[]{:S(2)}) copy-start(bf16[128,3328]{1,0:T(8,128)(2,1)S(1)} %collective-permute-done.13.refs_4_) | copy-start | bytes 2555908
  88.8 9.9 %collective-permute-start.18 = (bf16[96,3328]{1,0:T(8,128)(2,1)S(1)}, bf16[96,3328]{1,0:T(8,128)(2,1)S(1)}, u32[]{:S(2)}, u32[]{:S(2)}) collective-permute-start(bf16[96,3328]{1,0:T(8,128)(2,1)S(1)} %fusion.3), channel_id=1, source_target_pairs={{0,2},{1,7},{2,4},{3,1},{4,6},{5,3},{6,0},{7,5},{8,10},{9,15},{10,... | collective-permute-start | bytes 1916936 | tf_op jit(solution)/shard_map/ppermute | solution.py:40
  93.2 1.5 copy-start.16
  94.6 21.1 %collective-permute-start.16 = (bf16[128,3328]{1,0:T(8,128)(2,1)}, bf16[128,3328]{1,0:T(8,128)(2,1)}, u32[]{:S(2)}, u32[]{:S(2)}) collective-permute-start(bf16[128,3328]{1,0:T(8,128)(2,1)} %get-tuple-element.55), channel_id=1, source_target_pairs={{0,2},{1,7},{2,4},{3,1},{4,6},{5,3},{6,0},{7,5},{8,10},{9,15},{10,... | collective-permute-start | bytes 2555912 | tf_op jit(solution)/shard_map/ppermute | solution.py:40
  95.0 22.6 %collective-permute-start.17 = (bf16[128,3328]{1,0:T(8,128)(2,1)}, bf16[128,3328]{1,0:T(8,128)(2,1)}, u32[]{:S(2)}, u32[]{:S(2)}) collective-permute-start(bf16[128,3328]{1,0:T(8,128)(2,1)} %get-tuple-element.56), channel_id=1, source_target_pairs={{0,6},{1,3},{2,0},{3,5},{4,2},{5,7},{6,4},{7,1},{8,14},{9,11},{10,... | collective-permute-start | bytes 2555912 | tf_op jit(solution)/shard_map/ppermute | solution.py:40
  99.8 17.8 %collective-permute-start.20 = (bf16[96,3328]{1,0:T(8,128)(2,1)}, bf16[96,3328]{1,0:T(8,128)(2,1)}, u32[]{:S(2)}, u32[]{:S(2)}) collective-permute-start(bf16[96,3328]{1,0:T(8,128)(2,1)} %fusion.2), channel_id=1, source_target_pairs={{0,8},{1,9},{2,10},{3,11},{4,12},{5,13},{6,14},{7,15},{8,0},{9,1},... | collective-permute-start | bytes 1916936 | tf_op jit(solution)/shard_map/ppermute | solution.py:40
  101.3 42.3 %all-to-all-start = ((bf16[8,128,1024]{2,1,0:T(8,128)(2,1)}), bf16[8,128,1024]{2,1,0:T(8,128)(2,1)S(1)}, u32[]{:S(2)}, u32[]{:S(2)}) async-start(bf16[8,128,1024]{2,1,0:T(8,128)(2,1)} %shard_map.61), calls=%async_computation | async-start | bytes 4194304 | tf_op jit(solution)/shard_map/all_to_all | solution.py:222
  105.9 21.0 %copy-start.17 = (bf16[128,3328]{1,0:T(8,128)(2,1)S(1)}, bf16[128,3328]{1,0:T(8,128)(2,1)}, u32[]{:S(2)}) copy-start(bf16[128,3328]{1,0:T(8,128)(2,1)} %copy-done.16) | copy-start | bytes 2555908
  117.6 12.9 %collective-permute-start.21 = (bf16[1664,512]{1,0:T(8,128)(2,1)}, bf16[1664,512]{1,0:T(8,128)(2,1)S(1)}, u32[]{:S(2)}, u32[]{:S(2)}) collective-permute-start(bf16[1664,512]{1,0:T(8,128)(2,1)} %get-tuple-element.63), channel_id=1, source_target_pairs={{0,1},{1,0},{2,3},{3,2},{4,5},{5,4},{6,7},{7,6},{8,9},{9,8},{10,11... | collective-permute-start | bytes 5111816 | tf_op jit(solution)/shard_map/ppermute | solution.py:40
  126.9 5.9 %collective-permute-start.22 = (bf16[1664,512]{1,0:T(8,128)(2,1)}, bf16[1664,512]{1,0:T(8,128)(2,1)S(1)}, u32[]{:S(2)}, u32[]{:S(2)}) collective-permute-start(bf16[1664,512]{1,0:T(8,128)(2,1)} %get-tuple-element.64), channel_id=1, source_target_pairs={{0,1},{1,0},{2,3},{3,2},{4,5},{5,4},{6,7},{7,6},{8,9},{9,8},{10,11... | collective-permute-start | bytes 5111816 | tf_op jit(solution)/shard_map/ppermute | solution.py:40
  130.4 14.0 %collective-permute-start.24 = (bf16[128,3328]{1,0:T(8,128)(2,1)}, bf16[128,3328]{1,0:T(8,128)(2,1)}, u32[]{:S(2)}, u32[]{:S(2)}) collective-permute-start(bf16[128,3328]{1,0:T(8,128)(2,1)} %pad_maximum_fusion.6), channel_id=1, source_target_pairs={{0,2},{1,7},{2,4},{3,1},{4,6},{5,3},{6,0},{7,5},{8,10},{9,15},{10,... | collective-permute-start | bytes 2555912 | tf_op jit(solution)/shard_map/ppermute | solution.py:40
  130.4 2.3 %copy-start.14 = (bf16[1664,512]{1,0:T(8,128)(2,1)}, bf16[1664,512]{1,0:T(8,128)(2,1)S(1)}, u32[]{:S(2)}) copy-start(bf16[1664,512]{1,0:T(8,128)(2,1)S(1)} %collective-permute-done.21.refs_10_) | copy-start | bytes 5111812
  132.8 1.3 copy-start.15
  143.7 0.9 slice-start
  144.0 3.8 %collective-permute-start.23 = (bf16[128,512]{1,0:T(8,128)(2,1)S(1)}, bf16[128,512]{1,0:T(8,128)(2,1)S(1)}, u32[]{:S(2)}, u32[]{:S(2)}) collective-permute-start(bf16[128,512]{1,0:T(8,128)(2,1)S(1)} %get-tuple-element.78), channel_id=1, source_target_pairs={{0,1},{1,0},{2,3},{3,2},{4,5},{5,4},{6,7},{7,6},{8,9},{9,8},{10,11... | collective-permute-start | bytes 393224 | tf_op jit(solution)/shard_map/ppermute | solution.py:40

commit v5 on v4

--- a/solution.py
+++ b/solution.py
@@ -174,9 +174,10 @@
     h3 = send(h0, X1)
     w_other = send(weight, CORE)
     g = jnp.concatenate([grad_out, side], axis=0)
-    h0, h3, g, w_other = tie(h0, h3, g, w_other)
+    h0, g, w_other = tie(h0, g, w_other)
     g3, g1 = send(g, Z1), send(g, Z2)
-    h1, h2, k0b = send(h0, X2), send(h3, X1), send(h0[a:], YH)
+    h1, h2, k0b = send(hidden, X2), send(h3, X1), send(h0[a:], YH)
+    g3, g1 = tie(g3, g1)
     g2 = send(g3, Z1)
     w = jnp.concatenate([weight, w_other], axis=1)
     h1, h2, k0b, g1, g2, w = tie(h1, h2, k0b, g1, g2, w)
@@ -221,15 +222,15 @@
     h0, out, d3, d2 = tie(h0, out, d3, d2)
     out = lax.all_to_all(out, "row", 0, 0, tiled=True)
     d3, d2 = send(d3, X1), send(d2, X2)
-    n0 = send(add(far[0, b:], r1, r2), YH)
+    n0 = add(far[0, b:], r1, r2)
 
     arrays[0] = h0
     v, u = weight_gradient(arrays, plan, g_other)
     d3, d2, n0, v, u, arrays[0] = tie(d3, d2, n0, v, u, h0)
     d1 = jnp.concatenate([add(near[1, :b], n[1], d3[:b]), add(near[1, b:], d3[b:])], axis=0)
-    d1, v, u = send(d1, X1), send(v, CORE), send(u, CORE)
+    n0, d1, v, u = send(n0, YH), send(d1, X1), send(v, CORE), send(u, CORE)
     grad_weight = weight_gradient(arrays, plan, g_own, [v, u])
-    grad_weight, out = tie(grad_weight, out)
+    grad_weight, out, n0 = tie(grad_weight, out, n0)
     o = sum_blocks(out)
     own, other = o[:, :512], send(o[:, 512:], CORE)
     output = jnp.where(

time: 149 us -> 150 us (level)
  starting transfers between devices: 48.8 us -> 41.1 us
  waiting for transfers between devices: 22.8 us -> 26.2 us
  local copies, waits for them, and re-layouts: 9.61 us -> 12.2 us
  other arithmetic: 23.4 us -> 25.9 us
    ppermute x25, starting transfers between devices: 44.2 us -> 37.5 us  [send(): return lax.ppermute(value, AXES, perm)]
    ppermute x25, waiting for transfers between devices: 22.8 us -> 26.2 us  [send(): return lax.ppermute(value, AXES, perm)]
    convert_element_type x6, other arithmetic: 8.18 us -> 10.6 us  [add(): return total.astype(BF)]
    unnamed x38 -> x46, local copies, waits for them, and re-layouts: 2.64 us -> 4.85 us
  transfers between devices with their start and end apart: 26 -> 26, of which waited for: 11 -> 7; matrix products, arithmetic and copies ran while one was open for 25% -> 27% of each run, Pallas kernels for 22% -> 21%
where the time goes in v5:
time: 150 us; the launch traced here: 149 us
  starting transfers between devices  41.1 us (27%)
  Pallas kernels  33.5 us (22%)
  waiting for transfers between devices  26.2 us (17%)
  other arithmetic  25.9 us (17%)
  local copies, waits for them, and re-layouts  12.2 us (8%)
  matrix products  9.27 us (6%)
    ppermute x25, starting transfers between devices, send(): return lax.ppermute(value, AXES, perm)  37.5 us
    ppermute x25, waiting for transfers between devices, send(): return lax.ppermute(value, AXES, perm)  26.2 us
    pallas_call x2, Pallas kernels, weight_gradient(): pl.pallas_call(kernel, grid=(2,), out_shape=halves if others is None else...  18.5 us
    convert_element_type x6, other arithmetic, add(): return total.astype(BF)  10.6 us
    pallas_call x1, Pallas kernels, project(): pl.pallas_call(kernel, grid=(width // tile,), out_shape=jax.ShapeDtypeStr...  10.6 us
    dot_general x2, matrix products, dot(): return lax.dot_general(a, b, (dims, ((), ())), preferred_element_type=F32)  9.27 us
    concatenate x1, other arithmetic, per_device(): w = jnp.concatenate([weight, w_other], axis=1)  6.72 us
    unnamed x46, local copies, waits for them, and re-layouts  4.85 us
  transfers between devices with their start and end apart: 26, of which 7 were waited for; matrix products, arithmetic and copies ran while one was open for 27% of the time, Pallas kernels for 21%

profile of v5, /device:TPU:1, one launch (start us, length us, event | category | flops | bytes accessed | tf_op | source)
XLA Modules:
  0.0 149.2 jit_solution(11519428271380716469)
XLA Ops:
  0.6 1.5 %collective-permute-start.1 = (bf16[3328,512]{1,0:T(8,128)(2,1)}, bf16[3328,512]{1,0:T(8,128)(2,1)S(1)}, u32[]{:S(2)}, u32[]{:S(2)}) collective-permute-start(bf16[3328,512]{1,0:T(8,128)(2,1)} %param.4), channel_id=1, source_target_pairs={{0,1},{1,0},{2,3},{3,2},{4,5},{5,4},{6,7},{7,6},{8,9},{9,8},{10,11... | collective-permute-start | bytes 10223624 | tf_op jit(solution)/shard_map/ppermute | solution.py:40
  2.1 2.6 %collective-permute-start.3 = (bf16[128,3328]{1,0:T(8,128)(2,1)}, bf16[128,3328]{1,0:T(8,128)(2,1)S(1)}, u32[]{:S(2)}, u32[]{:S(2)}) collective-permute-start(bf16[128,3328]{1,0:T(8,128)(2,1)} %refs_0_.2), channel_id=1, source_target_pairs={{0,2},{1,7},{2,4},{3,1},{4,6},{5,3},{6,0},{7,5},{8,10},{9,15},{10,... | collective-permute-start | bytes 2555912 | tf_op jit(solution)/shard_map/ppermute | solution.py:40
  4.7 1.3 collective-permute-start
  6.0 6.8 %collective-permute-done = bf16[256,512]{1,0:T(8,128)(2,1)S(1)} collective-permute-done((bf16[256,512]{1,0:T(8,128)(2,1)}, bf16[256,512]{1,0:T(8,128)(2,1)S(1)}, u32[]{:S(2)}, u32[]{:S(2)}) %collective-permute-start) | collective-permute-done | bytes 262176 | tf_op jit(solution)/shard_map/ppermute | solution.py:40
  12.8 1.0 pad_maximum_fusion.7
  13.8 1.7 %collective-permute-start.7 = (bf16[512,512]{1,0:T(8,128)(2,1)S(1)}, bf16[512,512]{1,0:T(8,128)(2,1)S(1)}, u32[]{:S(2)}, u32[]{:S(2)}) collective-permute-start(bf16[512,512]{1,0:T(8,128)(2,1)S(1)} %pad_maximum_fusion.7), channel_id=1, source_target_pairs={{0,96},{1,33},{2,98},{3,35},{4,100},{5,37},{6,102},{7,39},{8,104},... | collective-permute-start | bytes 1572872 | tf_op jit(solution)/shard_map/ppermute | solution.py:40
  15.5 2.2 %collective-permute-start.6 = (bf16[512,512]{1,0:T(8,128)(2,1)S(1)}, bf16[512,512]{1,0:T(8,128)(2,1)}, u32[]{:S(2)}, u32[]{:S(2)}) collective-permute-start(bf16[512,512]{1,0:T(8,128)(2,1)S(1)} %pad_maximum_fusion.7), channel_id=1, source_target_pairs={{0,32},{1,97},{2,34},{3,99},{4,36},{5,101},{6,38},{7,103},{8,40},{... | collective-permute-start | bytes 1572872 | tf_op jit(solution)/shard_map/ppermute | solution.py:40
  17.7 2.7 %collective-permute-start.4 = (bf16[128,3328]{1,0:T(8,128)(2,1)S(1)}, bf16[128,3328]{1,0:T(8,128)(2,1)}, u32[]{:S(2)}, u32[]{:S(2)}) collective-permute-start(bf16[128,3328]{1,0:T(8,128)(2,1)S(1)} %collective-permute-done.3.refs_3_), channel_id=1, source_target_pairs={{0,2},{1,7},{2,4},{3,1},{4,6},{5,3},{6,0},{7,5},{8,10},{9,15},{10,... | collective-permute-start | bytes 2555912 | tf_op jit(solution)/shard_map/ppermute | solution.py:40
  20.5 0.1 stack.98.order_ref
  20.6 3.0 %collective-permute-start.5 = (bf16[96,3328]{1,0:T(8,128)(2,1)S(1)}, bf16[96,3328]{1,0:T(8,128)(2,1)S(1)}, u32[]{:S(2)}, u32[]{:S(2)}) collective-permute-start(bf16[96,3328]{1,0:T(8,128)(2,1)S(1)} %slice.86), channel_id=1, source_target_pairs={{0,8},{1,9},{2,10},{3,11},{4,12},{5,13},{6,14},{7,15},{8,0},{9,1},... | collective-permute-start | bytes 1916936 | tf_op jit(solution)/shard_map/ppermute | solution.py:40
  23.6 3.1 %collective-permute-done.7 = bf16[512,512]{1,0:T(8,128)(2,1)S(1)} collective-permute-done((bf16[512,512]{1,0:T(8,128)(2,1)S(1)}, bf16[512,512]{1,0:T(8,128)(2,1)S(1)}, u32[]{:S(2)}, u32[]{:S(2)}) %collective-permute-start.7) | collective-permute-done | bytes 524320 | tf_op jit(solution)/shard_map/ppermute | solution.py:40
  26.7 2.4 %collective-permute-done.6 = bf16[512,512]{1,0:T(8,128)(2,1)} collective-permute-done((bf16[512,512]{1,0:T(8,128)(2,1)S(1)}, bf16[512,512]{1,0:T(8,128)(2,1)}, u32[]{:S(2)}, u32[]{:S(2)}) %collective-permute-start.6) | collective-permute-done | bytes 524320 | tf_op jit(solution)/shard_map/ppermute | solution.py:40
  29.1 3.5 %collective-permute-start.8 = (bf16[512,512]{1,0:T(8,128)(2,1)}, bf16[512,512]{1,0:T(8,128)(2,1)S(1)}, u32[]{:S(2)}, u32[]{:S(2)}) collective-permute-start(bf16[512,512]{1,0:T(8,128)(2,1)} %collective-permute-done.6), channel_id=1, source_target_pairs={{0,32},{1,97},{2,34},{3,99},{4,36},{5,101},{6,38},{7,103},{8,40},{... | collective-permute-start | bytes 1572872 | tf_op jit(solution)/shard_map/ppermute | solution.py:40
  32.6 6.7 %pad_maximum_fusion.refs_9_ = bf16[3328,1024]{1,0:T(8,128)(2,1)} fusion(bf16[3328,512]{1,0:T(8,128)(2,1)} %copy-done.14, bf16[3328,512]{1,0:T(8,128)(2,1)} %param.4), kind=kLoop, calls=%fused_computation | loop fusion | flops 13631488 | bytes 13631488 | tf_op jit(solution)/shard_map/concatenate | solution.py:182
  39.4 0.8 copy-done.7
  40.3 1.3 pad_maximum_fusion.2
  41.6 1.6 %shard_map.59 = bf16[8,128,512]{2,1,0:T(8,128)(2,1)} custom-call(s32[8]{0:T(128)S(1)} %stack.98.order_ref, bf16[16,128,512]{2,1,0:T(8,128)(2,1)S(1)} %bitcast.67), custom_call_target="tpu_custom_call" | custom-call | bytes 2097152 | tf_op jit(solution)/shard_map/pallas_call | solution.py:63
  43.2 1.2 collective-permute-start.9
  44.5 1.0 slice.115
  45.6 2.7 %collective-permute-start.10 = (bf16[96,3328]{1,0:T(8,128)(2,1)}, bf16[96,3328]{1,0:T(8,128)(2,1)S(1)}, u32[]{:S(2)}, u32[]{:S(2)}) collective-permute-start(bf16[96,3328]{1,0:T(8,128)(2,1)} %copy-done.7), channel_id=1, source_target_pairs={{0,2},{1,7},{2,4},{3,1},{4,6},{5,3},{6,0},{7,5},{8,10},{9,15},{10,... | collective-permute-start | bytes 1916936 | tf_op jit(solution)/shard_map/ppermute | solution.py:40
  48.3 1.6 %slice.91 = bf16[32,3328]{1,0:T(8,128)(2,1)} slice(bf16[128,3328]{1,0:T(8,128)(2,1)} %collective-permute-done.2.refs_1_), slice={[0:32], [0:3328]} | slice | bytes 425984 | tf_op jit(solution)/shard_map/slice | solution.py:185
  49.9 1.6 %slice.92 = bf16[32,3328]{1,0:T(8,128)(2,1)} slice(bf16[128,3328]{1,0:T(8,128)(2,1)} %collective-permute-done.4.refs_2_), slice={[0:32], [0:3328]} | slice | bytes 425984 | tf_op jit(solution)/shard_map/slice | solution.py:185
  51.5 1.1 pad_maximum_fusion.3
  52.6 3.0 %collective-permute-start.13 = (bf16[128,3328]{1,0:T(8,128)(2,1)S(1)}, bf16[128,3328]{1,0:T(8,128)(2,1)S(1)}, u32[]{:S(2)}, u32[]{:S(2)}) collective-permute-start(bf16[128,3328]{1,0:T(8,128)(2,1)S(1)} %pad_maximum_fusion.3), channel_id=1, source_target_pairs={{0,8},{1,9},{2,10},{3,11},{4,12},{5,13},{6,14},{7,15},{8,0},{9,1},... | collective-permute-start | bytes 2555912 | tf_op jit(solution)/shard_map/ppermute | solution.py:40
  55.6 0.6 shard_map.58
  56.3 2.1 %pad_maximum_fusion.1 = bf16[1024,1024]{1,0:T(8,128)(2,1)S(1)} fusion(bf16[1024,512]{1,0:T(8,128)(2,1)} %collective-permute-done.9.refs_9_, bf16[1024,512]{1,0:T(8,128)(2,1)S(1)} %bitcast.69), kind=kLoop, calls=%fused_computation.4 | loop fusion | flops 4194304 | bytes 4194304 | tf_op jit(solution)/shard_map/concatenate | solution.py:198
  58.4 0.8 copy-done.3
  59.2 5.3 %convolution_convert_fusion.1 = bf16[512,3328]{1,0:T(8,128)(2,1)S(1)} fusion(bf16[3328,1024]{1,0:T(8,128)(2,1)S(1)} %copy-done.3, bf16[1024,512]{1,0:T(8,128)(2,1)S(1)} %bitcast.70, bf16[1024,512]{1,0:T(8,128)(2,1)} %collective-permute-done.9.refs_9_), kind=kOutput, calls=%fused_computation.2 | convolution fusion | flops 3493462016 | bytes 12320768 | tf_op jit(solution)/shard_map/dot_general | solution.py:55
  64.6 1.1 slice.97
  65.7 1.7 %slice_bitcast_fusion.3 = (bf16[96,3328]{1,0:T(8,128)(2,1)}, bf16[96,3328]{1,0:T(8,128)(2,1)}) fusion(bf16[4,128,3328]{2,1,0:T(8,128)(2,1)S(1)} %bitcast.74), kind=kLoop, calls=%fused_computation.24 | loop fusion | bytes 2555904 | tf_op jit(solution)/shard_map/squeeze | solution.py:204
  67.4 1.0 collective-permute-start.14
  68.4 2.4 %collective-permute-start.15 = (bf16[128,3328]{1,0:T(8,128)(2,1)}, bf16[128,3328]{1,0:T(8,128)(2,1)S(1)}, u32[]{:S(2)}, u32[]{:S(2)}) collective-permute-start(bf16[128,3328]{1,0:T(8,128)(2,1)} %bitcast.34), channel_id=1, source_target_pairs={{0,8},{1,9},{2,10},{3,11},{4,12},{5,13},{6,14},{7,15},{8,0},{9,1},... | collective-permute-start | bytes 2555912 | tf_op jit(solution)/shard_map/ppermute | solution.py:40
  70.8 4.0 %convolution_convert_fusion = bf16[512,3328]{1,0:T(8,128)(2,1)S(1)} fusion(bf16[3328,1024]{1,0:T(8,128)(2,1)S(1)} %copy-done.3, bf16[1024,1024]{1,0:T(8,128)(2,1)S(1)} %pad_maximum_fusion.1), kind=kOutput, calls=%fused_computation.1 | convolution fusion | flops 3491364864 | bytes 11272192 | tf_op jit(solution)/shard_map/dot_general | solution.py:55
  74.8 0.1 slice_bitcast_fusion.1
  74.9 2.0 %collective-permute-done.14.refs_7_ = bf16[96,3328]{1,0:T(8,128)(2,1)S(1)} collective-permute-done((bf16[96,3328]{1,0:T(8,128)(2,1)S(1)}, bf16[96,3328]{1,0:T(8,128)(2,1)S(1)}, u32[]{:S(2)}, u32[]{:S(2)}) %collective-permute-start.14) | collective-permute-done | bytes 639008 | tf_op jit(solution)/shard_map/ppermute | solution.py:40
  77.0 0.4 copy-done.5
  77.4 0.2 copy-done.8
  77.6 10.6 %shard_map.60 = bf16[1024,1024]{1,0:T(8,128)(2,1)S(1)} custom-call(bf16[128,3328]{1,0:T(8,128)(2,1)S(1)} %copy-done.2, bf16[128,3328]{1,0:T(8,128)(2,1)} %collective-permute-done.2.refs_1_, bf16[128,3328]{1,0:T(8,128)(2,1)} %collective-permute-done.4.refs_2_, bf16[128,3328]{1,0:T(8,128)(2,1)S(1)} %copy-done.5, ...), custom_call_target="tpu_custom_call" | custom-call | flops 6979321856 | bytes 16777216 | tf_op jit(solution)/shard_map/pallas_call | solution.py:97
  88.2 2.1 %fusion.3 = bf16[96,3328]{1,0:T(8,128)(2,1)} fusion(bf16[96,3328]{1,0:T(8,128)(2,1)} %collective-permute-done.12, bf16[4,128,3328]{2,1,0:T(8,128)(2,1)S(1)} %bitcast.75), kind=kLoop, calls=%fused_computation.14 | loop fusion | flops 1277952 | bytes 1916928 | tf_op jit(solution)/shard_map/convert_element_type | solution.py:47
  90.3 2.1 %collective-permute-start.18 = (bf16[96,3328]{1,0:T(8,128)(2,1)}, bf16[96,3328]{1,0:T(8,128)(2,1)}, u32[]{:S(2)}, u32[]{:S(2)}) collective-permute-start(bf16[96,3328]{1,0:T(8,128)(2,1)} %fusion.3), channel_id=1, source_target_pairs={{0,2},{1,7},{2,4},{3,1},{4,6},{5,3},{6,0},{7,5},{8,10},{9,15},{10,... | collective-permute-start | bytes 1916936 | tf_op jit(solution)/shard_map/ppermute | solution.py:40
  92.4 2.0 %shard_map.61 = bf16[8,128,1024]{2,1,0:T(8,128)(2,1)} custom-call(s32[8]{0:T(128)S(1)} %stack.107.order_ref, bf16[8,128,1024]{2,1,0:T(8,128)(2,1)S(1)} %bitcast.72), custom_call_target="tpu_custom_call" | custom-call | bytes 2097152 | tf_op jit(solution)/shard_map/pallas_call | solution.py:63
  94.4 0.1 fusion.9
  94.5 1.3 pad_maximum_fusion.4
  95.8 3.6 %all-to-all-start = ((bf16[8,128,1024]{2,1,0:T(8,128)(2,1)}), bf16[8,128,1024]{2,1,0:T(8,128)(2,1)S(1)}, u32[]{:S(2)}, u32[]{:S(2)}) async-start(bf16[8,128,1024]{2,1,0:T(8,128)(2,1)} %shard_map.61), calls=%async_computation | async-start | bytes 4194304 | tf_op jit(solution)/shard_map/all_to_all | solution.py:223
  99.4 1.1 collective-permute-start.16
  100.5 0.5 collective-permute-start.17
  100.9 8.9 %shard_map.62 = (bf16[1664,512]{1,0:T(8,128)(2,1)}, bf16[1664,512]{1,0:T(8,128)(2,1)}) custom-call(bf16[128,3328]{1,0:T(8,128)(2,1)} %refs_0_.2, bf16[128,3328]{1,0:T(8,128)(2,1)} %collective-permute-done.2.refs_1_, bf16[128,3328]{1,0:T(8,128)(2,1)} %collective-permute-done.4.refs_2_, bf16[128,3328]{1,0:T(8,128)(2,1)} %copy-done.4, ...), custom_call_target="tpu_custom_call" | custom-call | flops 1048576 | bytes 1048576 | tf_op jit(solution)/shard_map/pallas_call | solution.py:148
  109.9 2.7 %fusion.2 = bf16[96,3328]{1,0:T(8,128)(2,1)} fusion(bf16[96,3328]{1,0:T(8,128)(2,1)} %collective-permute-done.19, bf16[96,3328]{1,0:T(8,128)(2,1)} %collective-permute-done.18, bf16[4,128,3328]{2,1,0:T(8,128)(2,1)} %bitcast.76), kind=kLoop, calls=%fused_computation.12 | loop fusion | flops 1916928 | bytes 2555904 | tf_op jit(solution)/shard_map/convert_element_type | solution.py:47
  112.6 5.6 %collective-permute-done.16 = bf16[128,3328]{1,0:T(8,128)(2,1)S(1)} collective-permute-done((bf16[128,3328]{1,0:T(8,128)(2,1)}, bf16[128,3328]{1,0:T(8,128)(2,1)S(1)}, u32[]{:S(2)}, u32[]{:S(2)}) %collective-permute-start.16) | collective-permute-done | bytes 852000 | tf_op jit(solution)/shard_map/ppermute | solution.py:40
  118.2 4.7 %collective-permute-done.17 = bf16[128,3328]{1,0:T(8,128)(2,1)S(1)} collective-permute-done((bf16[128,3328]{1,0:T(8,128)(2,1)}, bf16[128,3328]{1,0:T(8,128)(2,1)S(1)}, u32[]{:S(2)}, u32[]{:S(2)}) %collective-permute-start.17) | collective-permute-done | bytes 852000 | tf_op jit(solution)/shard_map/ppermute | solution.py:40
  122.9 1.6 %collective-permute-start.20 = (bf16[1664,512]{1,0:T(8,128)(2,1)}, bf16[1664,512]{1,0:T(8,128)(2,1)S(1)}, u32[]{:S(2)}, u32[]{:S(2)}) collective-permute-start(bf16[1664,512]{1,0:T(8,128)(2,1)} %get-tuple-element.66), channel_id=1, source_target_pairs={{0,1},{1,0},{2,3},{3,2},{4,5},{5,4},{6,7},{7,6},{8,9},{9,8},{10,11... | collective-permute-start | bytes 5111816 | tf_op jit(solution)/shard_map/ppermute | solution.py:40
  124.5 0.3 collective-permute-start.21
  124.8 1.4 fusion
  126.2 2.0 %collective-permute-start.22 = (bf16[96,3328]{1,0:T(8,128)(2,1)}, bf16[96,3328]{1,0:T(8,128)(2,1)}, u32[]{:S(2)}, u32[]{:S(2)}) collective-permute-start(bf16[96,3328]{1,0:T(8,128)(2,1)} %fusion.2), channel_id=1, source_target_pairs={{0,8},{1,9},{2,10},{3,11},{4,12},{5,13},{6,14},{7,15},{8,0},{9,1},... | collective-permute-start | bytes 1916936 | tf_op jit(solution)/shard_map/ppermute | solution.py:40
  128.2 1.1 fusion.8
  129.4 1.0 pad_maximum_fusion.6
  130.4 1.2 copy-done.15
  131.5 1.3 copy-done.16
  132.8 9.6 %shard_map.63 = bf16[3328,512]{1,0:T(8,128)(2,1)} custom-call(bf16[128,3328]{1,0:T(8,128)(2,1)} %refs_0_.2, bf16[128,3328]{1,0:T(8,128)(2,1)} %collective-permute-done.2.refs_1_, bf16[128,3328]{1,0:T(8,128)(2,1)} %collective-permute-done.4.refs_2_, bf16[128,3328]{1,0:T(8,128)(2,1)} %copy-done.4, bf16[128,3328]{1,0:T(8,128)(2,1)} %copy-done.6, ...), custom_call_target="tpu_custom_call" | custom-call | flops 1048576 | bytes 1048576 | tf_op jit(solution)/shard_map/pallas_call | solution.py:148
  142.4 1.4 collective-permute-done.22
  143.9 0.3 shard_map.64
  144.2 1.1 collective-permute-start.23
  145.3 3.2 %add_convert_fusion = bf16[128,3328]{1,0:T(8,128)(2,1)} fusion(bf16[128,3328]{1,0:T(8,128)(2,1)} %copy-done.19, bf16[128,3328]{1,0:T(8,128)(2,1)} %collective-permute-done.24, bf16[512,3328]{1,0:T(8,128)(2,1)} %copy-done.13, bf16[96,3328]{1,0:T(8,128)(2,1)} %collective-permute-done.22, bf16[32,3328]{1,0:T(8,128)(2,1)S(1)} %slice-done), kind=kLoop, calls=%fused_computation.7 | loop fusion | flops 4685824 | bytes 4259840 | tf_op jit(solution)/shard_map/convert_element_type | solution.py:47
  148.5 0.8 maximum_select_fusion
  (71 shorter events, 0.5 us)
Async XLA Ops:
  0.6 19.9 %copy-start.1 = (bf16[128,3328]{1,0:T(8,128)(2,1)S(1)}, bf16[128,3328]{1,0:T(8,128)(2,1)}, u32[]{:S(2)}) copy-start(bf16[128,3328]{1,0:T(8,128)(2,1)} %refs_0_.2) | copy-start | bytes 2555908
  0.6 13.1 %collective-permute-start.1 = (bf16[3328,512]{1,0:T(8,128)(2,1)}, bf16[3328,512]{1,0:T(8,128)(2,1)S(1)}, u32[]{:S(2)}, u32[]{:S(2)}) collective-permute-start(bf16[3328,512]{1,0:T(8,128)(2,1)} %param.4), channel_id=1, source_target_pairs={{0,1},{1,0},{2,3},{3,2},{4,5},{5,4},{6,7},{7,6},{8,9},{9,8},{10,11... | collective-permute-start | bytes 10223624 | tf_op jit(solution)/shard_map/ppermute | solution.py:40
  2.1 15.6 %collective-permute-start.3 = (bf16[128,3328]{1,0:T(8,128)(2,1)}, bf16[128,3328]{1,0:T(8,128)(2,1)S(1)}, u32[]{:S(2)}, u32[]{:S(2)}) collective-permute-start(bf16[128,3328]{1,0:T(8,128)(2,1)} %refs_0_.2), channel_id=1, source_target_pairs={{0,2},{1,7},{2,4},{3,1},{4,6},{5,3},{6,0},{7,5},{8,10},{9,15},{10,... | collective-permute-start | bytes 2555912 | tf_op jit(solution)/shard_map/ppermute | solution.py:40
  4.7 8.1 %collective-permute-start = (bf16[256,512]{1,0:T(8,128)(2,1)}, bf16[256,512]{1,0:T(8,128)(2,1)S(1)}, u32[]{:S(2)}, u32[]{:S(2)}) collective-permute-start(bf16[256,512]{1,0:T(8,128)(2,1)} %param.5), channel_id=1, source_target_pairs={{0,16},{1,17},{2,18},{3,19},{4,20},{5,21},{6,22},{7,23},{8,24},{9,... | collective-permute-start | bytes 786440 | tf_op jit(solution)/shard_map/ppermute | solution.py:40
  13.8 3.9 %copy-start.14 = (bf16[3328,512]{1,0:T(8,128)(2,1)}, bf16[3328,512]{1,0:T(8,128)(2,1)S(1)}, u32[]{:S(2)}) copy-start(bf16[3328,512]{1,0:T(8,128)(2,1)S(1)} %collective-permute-done.1) | copy-start | bytes 10223620
  13.8 12.9 %collective-permute-start.7 = (bf16[512,512]{1,0:T(8,128)(2,1)S(1)}, bf16[512,512]{1,0:T(8,128)(2,1)S(1)}, u32[]{:S(2)}, u32[]{:S(2)}) collective-permute-start(bf16[512,512]{1,0:T(8,128)(2,1)S(1)} %pad_maximum_fusion.7), channel_id=1, source_target_pairs={{0,96},{1,33},{2,98},{3,35},{4,100},{5,37},{6,102},{7,39},{8,104},... | collective-permute-start | bytes 1572872 | tf_op jit(solution)/shard_map/ppermute | solution.py:40
  15.5 13.6 %collective-permute-start.6 = (bf16[512,512]{1,0:T(8,128)(2,1)S(1)}, bf16[512,512]{1,0:T(8,128)(2,1)}, u32[]{:S(2)}, u32[]{:S(2)}) collective-permute-start(bf16[512,512]{1,0:T(8,128)(2,1)S(1)} %pad_maximum_fusion.7), channel_id=1, source_target_pairs={{0,32},{1,97},{2,34},{3,99},{4,36},{5,101},{6,38},{7,103},{8,40},{... | collective-permute-start | bytes 1572872 | tf_op jit(solution)/shard_map/ppermute | solution.py:40
  17.7 21.7 %collective-permute-start.2 = (bf16[128,3328]{1,0:T(8,128)(2,1)}, bf16[128,3328]{1,0:T(8,128)(2,1)}, u32[]{:S(2)}, u32[]{:S(2)}) collective-permute-start(bf16[128,3328]{1,0:T(8,128)(2,1)} %refs_0_.2), channel_id=1, source_target_pairs={{0,6},{1,3},{2,0},{3,5},{4,2},{5,7},{6,4},{7,1},{8,14},{9,11},{10,... | collective-permute-start | bytes 2555912 | tf_op jit(solution)/shard_map/ppermute | solution.py:40
  17.7 21.6 %copy-start.4 = (bf16[128,3328]{1,0:T(8,128)(2,1)}, bf16[128,3328]{1,0:T(8,128)(2,1)S(1)}, u32[]{:S(2)}) copy-start(bf16[128,3328]{1,0:T(8,128)(2,1)S(1)} %collective-permute-done.3.refs_3_) | copy-start | bytes 2555908
  17.7 21.6 %collective-permute-start.4 = (bf16[128,3328]{1,0:T(8,128)(2,1)S(1)}, bf16[128,3328]{1,0:T(8,128)(2,1)}, u32[]{:S(2)}, u32[]{:S(2)}) collective-permute-start(bf16[128,3328]{1,0:T(8,128)(2,1)S(1)} %collective-permute-done.3.refs_3_), channel_id=1, source_target_pairs={{0,2},{1,7},{2,4},{3,1},{4,6},{5,3},{6,0},{7,5},{8,10},{9,15},{10,... | collective-permute-start | bytes 2555912 | tf_op jit(solution)/shard_map/ppermute | solution.py:40
  20.6 18.8 %collective-permute-start.5 = (bf16[96,3328]{1,0:T(8,128)(2,1)S(1)}, bf16[96,3328]{1,0:T(8,128)(2,1)S(1)}, u32[]{:S(2)}, u32[]{:S(2)}) collective-permute-start(bf16[96,3328]{1,0:T(8,128)(2,1)S(1)} %slice.86), channel_id=1, source_target_pairs={{0,8},{1,9},{2,10},{3,11},{4,12},{5,13},{6,14},{7,15},{8,0},{9,1},... | collective-permute-start | bytes 1916936 | tf_op jit(solution)/shard_map/ppermute | solution.py:40
  26.7 12.7 %copy-start.21 = (bf16[512,512]{1,0:T(8,128)(2,1)}, bf16[512,512]{1,0:T(8,128)(2,1)S(1)}, u32[]{:S(2)}) copy-start(bf16[512,512]{1,0:T(8,128)(2,1)S(1)} %collective-permute-done.7) | copy-start | bytes 1572868
  29.1 11.1 %collective-permute-start.8 = (bf16[512,512]{1,0:T(8,128)(2,1)}, bf16[512,512]{1,0:T(8,128)(2,1)S(1)}, u32[]{:S(2)}, u32[]{:S(2)}) collective-permute-start(bf16[512,512]{1,0:T(8,128)(2,1)} %collective-permute-done.6), channel_id=1, source_target_pairs={{0,32},{1,97},{2,34},{3,99},{4,36},{5,101},{6,38},{7,103},{8,40},{... | collective-permute-start | bytes 1572872 | tf_op jit(solution)/shard_map/ppermute | solution.py:40
  39.4 0.8 copy-start.7
  43.2 13.1 %collective-permute-start.9 = (bf16[1024,512]{1,0:T(8,128)(2,1)}, bf16[1024,512]{1,0:T(8,128)(2,1)}, u32[]{:S(2)}, u32[]{:S(2)}) collective-permute-start(bf16[1024,512]{1,0:T(8,128)(2,1)} %bitcast.18), channel_id=1, source_target_pairs={{0,1},{1,0},{2,3},{3,2},{4,5},{5,4},{6,7},{7,6},{8,9},{9,8},{10,11... | collective-permute-start | bytes 3145736 | tf_op jit(solution)/shard_map/ppermute | solution.py:40
  45.5 19.0 %collective-permute-start.11 = (bf16[96,3328]{1,0:T(8,128)(2,1)}, bf16[96,3328]{1,0:T(8,128)(2,1)S(1)}, u32[]{:S(2)}, u32[]{:S(2)}) collective-permute-start(bf16[96,3328]{1,0:T(8,128)(2,1)} %copy-done.7), channel_id=1, source_target_pairs={{0,6},{1,3},{2,0},{3,5},{4,2},{5,7},{6,4},{7,1},{8,14},{9,11},{10,... | collective-permute-start | bytes 1916936 | tf_op jit(solution)/shard_map/ppermute | solution.py:40
  45.6 19.0 %collective-permute-start.10 = (bf16[96,3328]{1,0:T(8,128)(2,1)}, bf16[96,3328]{1,0:T(8,128)(2,1)S(1)}, u32[]{:S(2)}, u32[]{:S(2)}) collective-permute-start(bf16[96,3328]{1,0:T(8,128)(2,1)} %copy-done.7), channel_id=1, source_target_pairs={{0,2},{1,7},{2,4},{3,1},{4,6},{5,3},{6,0},{7,5},{8,10},{9,15},{10,... | collective-permute-start | bytes 1916936 | tf_op jit(solution)/shard_map/ppermute | solution.py:40
  52.6 24.3 %collective-permute-start.13 = (bf16[128,3328]{1,0:T(8,128)(2,1)S(1)}, bf16[128,3328]{1,0:T(8,128)(2,1)S(1)}, u32[]{:S(2)}, u32[]{:S(2)}) collective-permute-start(bf16[128,3328]{1,0:T(8,128)(2,1)S(1)} %pad_maximum_fusion.3), channel_id=1, source_target_pairs={{0,8},{1,9},{2,10},{3,11},{4,12},{5,13},{6,14},{7,15},{8,0},{9,1},... | collective-permute-start | bytes 2555912 | tf_op jit(solution)/shard_map/ppermute | solution.py:40
  55.6 3.6 %copy-start.3 = (bf16[3328,1024]{1,0:T(8,128)(2,1)S(1)}, bf16[3328,1024]{1,0:T(8,128)(2,1)}, u32[]{:S(2)}) copy-start(bf16[3328,1024]{1,0:T(8,128)(2,1)} %pad_maximum_fusion.refs_9_) | copy-start | bytes 20447236
  56.2 2.2 %copy-start = (bf16[8,128,512]{2,1,0:T(8,128)(2,1)}, bf16[8,128,512]{2,1,0:T(8,128)(2,1)S(1)}, u32[]{:S(2)}) copy-start(bf16[8,128,512]{2,1,0:T(8,128)(2,1)S(1)} %shard_map.58) | copy-start | bytes 3145732
  64.5 23.7 %copy-start.12 = (bf16[512,3328]{1,0:T(8,128)(2,1)}, bf16[512,3328]{1,0:T(8,128)(2,1)S(1)}, u32[]{:S(2)}) copy-start(bf16[512,3328]{1,0:T(8,128)(2,1)S(1)} %convolution_convert_fusion.1) | copy-start | bytes 10223620
  64.6 12.4 %copy-start.9 = (bf16[96,3328]{1,0:T(8,128)(2,1)}, bf16[96,3328]{1,0:T(8,128)(2,1)S(1)}, u32[]{:S(2)}) copy-start(bf16[96,3328]{1,0:T(8,128)(2,1)S(1)} %collective-permute-done.11.refs_6_) | copy-start | bytes 1916932
  64.6 12.4 %copy-start.10 = (bf16[96,3328]{1,0:T(8,128)(2,1)}, bf16[96,3328]{1,0:T(8,128)(2,1)S(1)}, u32[]{:S(2)}) copy-start(bf16[96,3328]{1,0:T(8,128)(2,1)S(1)} %collective-permute-done.10.refs_8_) | copy-start | bytes 1916932
  67.4 9.6 %collective-permute-start.14 = (bf16[96,3328]{1,0:T(8,128)(2,1)S(1)}, bf16[96,3328]{1,0:T(8,128)(2,1)S(1)}, u32[]{:S(2)}, u32[]{:S(2)}) collective-permute-start(bf16[96,3328]{1,0:T(8,128)(2,1)S(1)} %collective-permute-done.10.refs_8_), channel_id=1, source_target_pairs={{0,2},{1,7},{2,4},{3,1},{4,6},{5,3},{6,0},{7,5},{8,10},{9,15},{10,... | collective-permute-start | bytes 1916936 | tf_op jit(solution)/shard_map/ppermute | solution.py:40
  68.4 26.0 %collective-permute-start.15 = (bf16[128,3328]{1,0:T(8,128)(2,1)}, bf16[128,3328]{1,0:T(8,128)(2,1)S(1)}, u32[]{:S(2)}, u32[]{:S(2)}) collective-permute-start(bf16[128,3328]{1,0:T(8,128)(2,1)} %bitcast.34), channel_id=1, source_target_pairs={{0,8},{1,9},{2,10},{3,11},{4,12},{5,13},{6,14},{7,15},{8,0},{9,1},... | collective-permute-start | bytes 2555912 | tf_op jit(solution)/shard_map/ppermute | solution.py:40
  70.7 17.4 %collective-permute-start.12 = (bf16[96,3328]{1,0:T(8,128)(2,1)}, bf16[96,3328]{1,0:T(8,128)(2,1)}, u32[]{:S(2)}, u32[]{:S(2)}) collective-permute-start(bf16[96,3328]{1,0:T(8,128)(2,1)} %get-tuple-element.80), channel_id=1, source_target_pairs={{0,2},{1,7},{2,4},{3,1},{4,6},{5,3},{6,0},{7,5},{8,10},{9,15},{10,... | collective-permute-start | bytes 1916936 | tf_op jit(solution)/shard_map/ppermute | solution.py:40
  74.7 19.6 %copy-start.13 = (bf16[512,3328]{1,0:T(8,128)(2,1)}, bf16[512,3328]{1,0:T(8,128)(2,1)S(1)}, u32[]{:S(2)}) copy-start(bf16[512,3328]{1,0:T(8,128)(2,1)S(1)} %convolution_convert_fusion) | copy-start | bytes 10223620
  74.7 2.2 %copy-start.2 = (bf16[128,3328]{1,0:T(8,128)(2,1)S(1)}, bf16[128,3328]{1,0:T(8,128)(2,1)}, u32[]{:S(2)}) copy-start(bf16[128,3328]{1,0:T(8,128)(2,1)} %refs_0_.2) | copy-start | bytes 2555908
  74.8 2.6 %copy-start.5 = (bf16[128,3328]{1,0:T(8,128)(2,1)S(1)}, bf16[128,3328]{1,0:T(8,128)(2,1)}, u32[]{:S(2)}) copy-start(bf16[128,3328]{1,0:T(8,128)(2,1)} %copy-done.4) | copy-start | bytes 2555908
  74.8 2.8 %copy-start.8 = (bf16[96,3328]{1,0:T(8,128)(2,1)S(1)}, bf16[96,3328]{1,0:T(8,128)(2,1)}, u32[]{:S(2)}) copy-start(bf16[96,3328]{1,0:T(8,128)(2,1)} %copy-done.7) | copy-start | bytes 1916932
  76.9 11.2 %copy-start.11 = (bf16[96,3328]{1,0:T(8,128)(2,1)}, bf16[96,3328]{1,0:T(8,128)(2,1)S(1)}, u32[]{:S(2)}) copy-start(bf16[96,3328]{1,0:T(8,128)(2,1)S(1)} %collective-permute-done.14.refs_7_) | copy-start | bytes 1916932
  76.9 33.0 %collective-permute-start.19 = (bf16[96,3328]{1,0:T(8,128)(2,1)}, bf16[96,3328]{1,0:T(8,128)(2,1)}, u32[]{:S(2)}, u32[]{:S(2)}) collective-permute-start(bf16[96,3328]{1,0:T(8,128)(2,1)} %get-tuple-element.61), channel_id=1, source_target_pairs={{0,6},{1,3},{2,0},{3,5},{4,2},{5,7},{6,4},{7,1},{8,14},{9,11},{10,... | collective-permute-start | bytes 1916936 | tf_op jit(solution)/shard_map/ppermute | solution.py:40
  77.6 10.6 %copy-start.6 = (bf16[128,3328]{1,0:T(8,128)(2,1)}, bf16[128,3328]{1,0:T(8,128)(2,1)S(1)}, u32[]{:S(2)}) copy-start(bf16[128,3328]{1,0:T(8,128)(2,1)S(1)} %collective-permute-done.13.refs_4_) | copy-start | bytes 2555908
  90.3 19.6 %collective-permute-start.18 = (bf16[96,3328]{1,0:T(8,128)(2,1)}, bf16[96,3328]{1,0:T(8,128)(2,1)}, u32[]{:S(2)}, u32[]{:S(2)}) collective-permute-start(bf16[96,3328]{1,0:T(8,128)(2,1)} %fusion.3), channel_id=1, source_target_pairs={{0,2},{1,7},{2,4},{3,1},{4,6},{5,3},{6,0},{7,5},{8,10},{9,15},{10,... | collective-permute-start | bytes 1916936 | tf_op jit(solution)/shard_map/ppermute | solution.py:40
  94.4 1.4 copy-start.17
  95.8 48.1 %all-to-all-start = ((bf16[8,128,1024]{2,1,0:T(8,128)(2,1)}), bf16[8,128,1024]{2,1,0:T(8,128)(2,1)S(1)}, u32[]{:S(2)}, u32[]{:S(2)}) async-start(bf16[8,128,1024]{2,1,0:T(8,128)(2,1)} %shard_map.61), calls=%async_computation | async-start | bytes 4194304 | tf_op jit(solution)/shard_map/all_to_all | solution.py:223
  99.4 18.8 %collective-permute-start.16 = (bf16[128,3328]{1,0:T(8,128)(2,1)}, bf16[128,3328]{1,0:T(8,128)(2,1)S(1)}, u32[]{:S(2)}, u32[]{:S(2)}) collective-permute-start(bf16[128,3328]{1,0:T(8,128)(2,1)} %get-tuple-element.58), channel_id=1, source_target_pairs={{0,2},{1,7},{2,4},{3,1},{4,6},{5,3},{6,0},{7,5},{8,10},{9,15},{10,... | collective-permute-start | bytes 2555912 | tf_op jit(solution)/shard_map/ppermute | solution.py:40
  100.5 22.4 %collective-permute-start.17 = (bf16[128,3328]{1,0:T(8,128)(2,1)}, bf16[128,3328]{1,0:T(8,128)(2,1)S(1)}, u32[]{:S(2)}, u32[]{:S(2)}) collective-permute-start(bf16[128,3328]{1,0:T(8,128)(2,1)} %get-tuple-element.59), channel_id=1, source_target_pairs={{0,6},{1,3},{2,0},{3,5},{4,2},{5,7},{6,4},{7,1},{8,14},{9,11},{10,... | collective-permute-start | bytes 2555912 | tf_op jit(solution)/shard_map/ppermute | solution.py:40
  109.9 14.7 %copy-start.22 = (bf16[1664,512]{1,0:T(8,128)(2,1)S(1)}, bf16[1664,512]{1,0:T(8,128)(2,1)}, u32[]{:S(2)}) copy-start(bf16[1664,512]{1,0:T(8,128)(2,1)} %get-tuple-element.67) | copy-start | bytes 5111812
  109.9 18.4 %copy-start.18 = (bf16[128,3328]{1,0:T(8,128)(2,1)S(1)}, bf16[128,3328]{1,0:T(8,128)(2,1)}, u32[]{:S(2)}) copy-start(bf16[128,3328]{1,0:T(8,128)(2,1)} %copy-done.17) | copy-start | bytes 2555908
  118.2 4.7 %copy-start.20 = (bf16[128,3328]{1,0:T(8,128)(2,1)}, bf16[128,3328]{1,0:T(8,128)(2,1)S(1)}, u32[]{:S(2)}) copy-start(bf16[128,3328]{1,0:T(8,128)(2,1)S(1)} %collective-permute-done.16) | copy-start | bytes 2555908
  122.9 1.6 %copy-start.19 = (bf16[128,3328]{1,0:T(8,128)(2,1)}, bf16[128,3328]{1,0:T(8,128)(2,1)S(1)}, u32[]{:S(2)}) copy-start(bf16[128,3328]{1,0:T(8,128)(2,1)S(1)} %collective-permute-done.17) | copy-start | bytes 2555908
  122.9 7.4 %collective-permute-start.20 = (bf16[1664,512]{1,0:T(8,128)(2,1)}, bf16[1664,512]{1,0:T(8,128)(2,1)S(1)}, u32[]{:S(2)}, u32[]{:S(2)}) collective-permute-start(bf16[1664,512]{1,0:T(8,128)(2,1)} %get-tuple-element.66), channel_id=1, source_target_pairs={{0,1},{1,0},{2,3},{3,2},{4,5},{5,4},{6,7},{7,6},{8,9},{9,8},{10,11... | collective-permute-start | bytes 5111816 | tf_op jit(solution)/shard_map/ppermute | solution.py:40
  124.5 5.8 %collective-permute-start.21 = (bf16[1664,512]{1,0:T(8,128)(2,1)S(1)}, bf16[1664,512]{1,0:T(8,128)(2,1)S(1)}, u32[]{:S(2)}, u32[]{:S(2)}) collective-permute-start(bf16[1664,512]{1,0:T(8,128)(2,1)S(1)} %copy-done.22), channel_id=1, source_target_pairs={{0,1},{1,0},{2,3},{3,2},{4,5},{5,4},{6,7},{7,6},{8,9},{9,8},{10,11... | collective-permute-start | bytes 5111816 | tf_op jit(solution)/shard_map/ppermute | solution.py:40
  126.2 17.6 %collective-permute-start.22 = (bf16[96,3328]{1,0:T(8,128)(2,1)}, bf16[96,3328]{1,0:T(8,128)(2,1)}, u32[]{:S(2)}, u32[]{:S(2)}) collective-permute-start(bf16[96,3328]{1,0:T(8,128)(2,1)} %fusion.2), channel_id=1, source_target_pairs={{0,8},{1,9},{2,10},{3,11},{4,12},{5,13},{6,14},{7,15},{8,0},{9,1},... | collective-permute-start | bytes 1916936 | tf_op jit(solution)/shard_map/ppermute | solution.py:40
  130.3 15.0 %collective-permute-start.24 = (bf16[128,3328]{1,0:T(8,128)(2,1)}, bf16[128,3328]{1,0:T(8,128)(2,1)}, u32[]{:S(2)}, u32[]{:S(2)}) collective-permute-start(bf16[128,3328]{1,0:T(8,128)(2,1)} %pad_maximum_fusion.6), channel_id=1, source_target_pairs={{0,2},{1,7},{2,4},{3,1},{4,6},{5,3},{6,0},{7,5},{8,10},{9,15},{10,... | collective-permute-start | bytes 2555912 | tf_op jit(solution)/shard_map/ppermute | solution.py:40
  130.4 1.2 copy-start.15
  131.5 1.3 copy-start.16
  142.4 2.9 %slice-start = ((bf16[128,3328]{1,0:T(8,128)(2,1)}), bf16[32,3328]{1,0:T(8,128)(2,1)S(1)}, s32[]{:S(2)}) async-start(bf16[128,3328]{1,0:T(8,128)(2,1)} %copy-done.17), calls=%async_computation.1 | async-start | bytes 425984 | tf_op jit(solution)/shard_map/slice | solution.py:240
  144.2 4.3 %collective-permute-start.23 = (bf16[128,512]{1,0:T(8,128)(2,1)S(1)}, bf16[128,512]{1,0:T(8,128)(2,1)S(1)}, u32[]{:S(2)}, u32[]{:S(2)}) collective-permute-start(bf16[128,512]{1,0:T(8,128)(2,1)S(1)} %get-tuple-element.82), channel_id=1, source_target_pairs={{0,1},{1,0},{2,3},{3,2},{4,5},{5,4},{6,7},{7,6},{8,9},{9,8},{10,11... | collective-permute-start | bytes 393224 | tf_op jit(solution)/shard_map/ppermute | solution.py:40
